TPU v7x, 32 devices: a whole 2x2x4 slice. The times are simulated.
32 devices in a mesh: section: 2 (over core), dp: 16 (over z, y, x).
Axes of the slice: x: 2, y: 2, z: 4, core: 2. Of those that a mesh axis runs over, the one named last changes fastest.
Arguments:
- tokens: bfloat16 [18432, 768], P('dp', 'section'), may hold values from -6 to 6
- image_ids: int32 [32, 576], P('dp'), may hold values from -1 to 4, as said below
- routes: int32 [18432, 2], P('dp'), may hold values from 0 to 3, all different within a row; in each aligned block of 576 rows (0 to 575, 576 to 1151, ...) at most 304 rows name the same one
- norm1_gain: bfloat16 [768], P('section'), may hold values from 0.5 to 1.5
- norm1_bias: bfloat16 [768], P('section'), may hold values from -3 to 3
- qkv_weight: bfloat16 [768, 2304], P('section'), may hold values from -0.21875 to 0.21875
- attn_out_weight: bfloat16 [768, 768], P('section'), may hold values from -0.625 to 0.625
- norm2_gain: bfloat16 [768], P('section'), may hold values from 0.5 to 1.5
- norm2_bias: bfloat16 [768], P('section'), may hold values from -3 to 3
- fc1_weight: bfloat16 [768, 3072], P('section'), may hold values from -0.21875 to 0.21875
- fc2_weight: bfloat16 [3072, 768], P('section'), may hold values from -0.109375 to 0.109375
- norm3_gain: bfloat16 [768], P('section'), may hold values from 0.5 to 1.5
- norm3_bias: bfloat16 [768], P('section'), may hold values from -3 to 3
- router_weight: bfloat16 [768, 4], P('section'), may hold values from -0.15625 to 0.15625
- expert_up: bfloat16 [768, 12288], P('section', 'dp'), may hold values from -0.21875 to 0.21875
- expert_down: bfloat16 [768, 12288], P('section', 'dp'), may hold values from -0.109375 to 0.109375
- cotangent: bfloat16 [18432, 768], P('dp', 'section'), may hold values from -6 to 6
Outputs:
- block_out: bfloat16 [18432, 768], P('dp', 'section')
- input_grad: float32 [18432, 768], P('dp', 'section')
- grad_norm1_gain: float32 [768], P('section')
- grad_norm1_bias: float32 [768], P('section')
- grad_qkv: float32 [768, 2304], P('section')
- grad_attn_out: float32 [768, 768], P('section')
- grad_norm2_gain: float32 [768], P('section')
- grad_norm2_bias: float32 [768], P('section')
- grad_fc1: float32 [768, 3072], P('section')
- grad_fc2: float32 [3072, 768], P('section')
- grad_norm3_gain: float32 [768], P('section')
- grad_norm3_bias: float32 [768], P('section')
- grad_router: float32 [768, 4], P('section')
- grad_expert_up: float32 [768, 12288], P('section', 'dp')
- grad_expert_down: float32 [768, 12288], P('section', 'dp')
Inputs may be any that keep to these rules, and one draw needn't show every extreme that they name: `image_ids`: in each row, padding (-1) stands only at the end and covers at most 144 slots; live slots carry image numbers that never fall along the row and that take every value 0 to 4; some row has no padding and some row has 144 padded slots. The routes of padding slots are not used.
All inputs are finite; a program needn't handle non-finite values.
Results may differ from a plain program's by a relative error of at most 0.014.
Values may be sent and summed in bfloat16 or wider, within the bound.
No kernel may reach another device: no remote copies, remote signals or barrier semaphores. Data moves between devices by JAX's collectives and lax.ppermute only.
A program may use at most 384 MiB of HBM per device.

v0:
```python
import functools

import jax
import jax.numpy as jnp
from jax import lax
from jax.experimental import pallas as pl
from jax.experimental.pallas import tpu as pltpu
from jax.sharding import PartitionSpec as P

HEAD = 64
TOP = 2
GROUP = 4
SLOTS = 576
WIDE = 128

EPSILON = 1e-06
MASKED = -1e30
BF = jnp.bfloat16
F32 = jnp.float32
LIMIT = 24 * 1024 * 1024
LIMITS = dict(
    attention_forward=28,
    dense_forward=36,
    expert=28,
    dense_backward=40,
    attention_backward=28,
    input_backward=24,
    merge=20,
    hold=12,
    finish=24,
    spread=16,
)


def dot(a, b):
    return jnp.dot(a, b, preferred_element_type=F32)


def dot_nt(a, b):
    return lax.dot_general(a, b, (((1,), (1,)), ((), ())), preferred_element_type=F32)


def dot_tn(a, b):
    return lax.dot_general(a, b, (((0,), (0,)), ((), ())), preferred_element_type=F32)


def normalize(v):
    center = v - jnp.mean(v, axis=-1, keepdims=True)
    scale = lax.rsqrt(jnp.mean(center * center, axis=-1, keepdims=True) + EPSILON)
    return center * scale, scale


def gelu_pair(x):
    bell = jnp.exp(x * x * -0.5)
    t = 1.0 / (1.0 + jnp.abs(x) * (0.3275911 * 0.5**0.5))
    tail = (
        t
        * (
            0.127414796
            + t * (-0.142248368 + t * (0.7107068705 + t * (-0.7265760135 + t * 0.5307027145)))
        )
        * bell
    )
    cdf = jnp.where(x >= 0.0, 1.0 - tail, tail)
    return x * cdf, cdf + x * (bell * 0.3989422804014327)


def iota(shape, axis):
    return lax.broadcasted_iota(jnp.int32, shape, axis)


def halves_into(s, own, other, dest, sems, first):
    rows = own.shape[0]
    return [
        pltpu.make_async_copy(own, dest.at[pl.ds(pl.multiple_of(s * rows, rows), rows)], sems.at[first]),
        pltpu.make_async_copy(
            other, dest.at[pl.ds(pl.multiple_of((1 - s) * rows, rows), rows)], sems.at[first + 1]
        ),
    ]


def split3(v):
    hi = v.astype(BF)
    rest = v - hi.astype(F32)
    mid = rest.astype(BF)
    low = (rest - mid.astype(F32)).astype(BF)
    return hi, mid, low


VM = pl.BlockSpec(memory_space=pltpu.VMEM)
SM = pl.BlockSpec(memory_space=pltpu.SMEM)
HB = pl.BlockSpec(memory_space=pl.ANY)


def call(kernel, in_specs, out_shape, scratch, flops, moved, name, after=(), weight=16, flushed=()):
    limit = LIMITS[name] * 1024 * 1024
    count, extra = len(in_specs), len(after)
    single = not isinstance(out_shape, list)
    shapes = [out_shape] if single else out_shape
    total, held = len(shapes), len(flushed)

    def body(*refs):
        inputs, outs = refs[:count], list(refs[count + extra : count + extra + total])
        rest = refs[count + extra + total :]
        if not held:
            kernel(*inputs, *outs, *rest)
            return
        own, (buffers, sems) = rest[: len(rest) - held - 1], (rest[len(rest) - held - 1 : -1], rest[-1])
        copies = {}
        for k, index in enumerate(flushed):
            copies[index] = pltpu.make_async_copy(buffers[k], outs[index], sems.at[k])
            outs[index] = buffers[k]
        kernel(*inputs, *outs, *own, flush=lambda index: copies[index].start())
        for index in flushed:
            copies[index].wait()

    made = pl.pallas_call(
        body,
        in_specs=in_specs + [HB] * extra,
        out_specs=VM
        if single
        else [pl.BlockSpec(memory_space=pltpu.HBM) if i in flushed else VM for i in range(total)],
        out_shape=out_shape
        if not held
        else [pltpu.HBM(v.shape, v.dtype) if i in flushed else v for i, v in enumerate(shapes)],
        scratch_shapes=scratch
        + [pltpu.VMEM(shapes[i].shape, shapes[i].dtype) for i in flushed]
        + ([pltpu.SemaphoreType.DMA((held,))] if held else []),
        compiler_params=pltpu.CompilerParams(vmem_limit_bytes=limit),
        cost_estimate=pl.CostEstimate(
            flops=int(weight * flops), bytes_accessed=int(weight * moved), transcendentals=0
        ),
        name=name,
    )
    return lambda *operands: made(*operands, *after)


def shape(dims, kind):
    return jax.ShapeDtypeStruct(dims, kind)


def front_kernel(
    s_ref, x_ref, id_row, id_col, gb_ref, qkv_a, qkv_b, wo_a, wo_b,
    normed, packed, context, lse, hidden,
    wq, wo, bias, lse_col, sems, flush,
):
    s = s_ref[0]
    rows, width = x_ref.shape
    copies = halves_into(s, qkv_a, qkv_b, wq, sems, 0) + halves_into(s, wo_a, wo_b, wo, sems, 2)
    for c in copies:
        c.start()
    tile = rows // 6

    @pl.loop(0, 6)
    def _(i):
        at = pl.ds(pl.multiple_of(i * tile, 16), tile)
        n, _ = normalize(x_ref[at, :].astype(F32))
        normed[at, :] = (n * gb_ref[0:1, :] + gb_ref[1:2, :]).astype(BF)
        bias[at, :] = jnp.where(id_col[at, :] == id_row[...], 0.0, MASKED)

    copies[0].wait()
    copies[1].wait()

    @pl.loop(0, wq.shape[1] // 256)
    def _(j):
        at = pl.ds(pl.multiple_of(j * 256, 256), 256)
        packed[:, at] = dot(normed[...], wq[:, at]).astype(BF)

    flush(0)
    flush(1)
    lane = iota((1, WIDE), 1)
    lse_col[...] = jnp.zeros_like(lse_col)
    third = rows // 3

    @pl.loop(0, width // WIDE)
    def _(pair):
        col = pl.multiple_of(pair * WIDE, WIDE)
        keys = packed[:, pl.ds(width + col, WIDE)]
        values = packed[:, pl.ds(2 * width + col, WIDE)]
        for r in range(3):
            at = slice(r * third, (r + 1) * third)
            q = packed[at, pl.ds(col, WIDE)] * jnp.asarray(HEAD**-0.5, BF)
            outs = []
            sums = lse_col[at, :]
            for h in range(2):
                mine = (lane >= h * HEAD) & (lane < (h + 1) * HEAD)
                scores = dot_nt(jnp.where(mine, q, jnp.zeros_like(q)), keys) + bias[at, :]
                top = jnp.max(scores, axis=1, keepdims=True)
                p = jnp.exp(scores - top)
                total = jnp.sum(p, axis=1, keepdims=True)
                outs.append(dot(p.astype(BF), values) * (1.0 / total))
                sums = jnp.where(lane == 2 * pair + h, top + jnp.log(total), sums)
            lse_col[at, :] = sums
            context[at, pl.ds(col, WIDE)] = jnp.where(lane < HEAD, outs[0], outs[1]).astype(BF)

    flush(2)
    lse[...] = jnp.transpose(lse_col[...])[0 : lse.shape[0], :]
    copies[2].wait()
    copies[3].wait()

    @pl.loop(0, width // 256)
    def _(j):
        at = pl.ds(pl.multiple_of(j * 256, 256), 256)
        hidden[:, at] = x_ref[:, at].astype(F32) + dot(context[...], wo[:, at])


def front(s, x, ids, gb, qkv, wo, after):
    rows, width = x.shape
    n3 = qkv[0].shape[1]
    return call(
        front_kernel,
        [SM, VM, VM, VM, VM, HB, HB, HB, HB],
        [
            shape((rows, width), BF),
            shape((rows, n3), BF),
            shape((rows, width), BF),
            shape((16, rows), F32),
            shape((rows, width), F32),
        ],
        [
            pltpu.VMEM((width, n3), BF),
            pltpu.VMEM((width, width), BF),
            pltpu.VMEM((rows, rows), F32),
            pltpu.VMEM((rows, WIDE), F32),
            pltpu.SemaphoreType.DMA((4,)),
        ],
        2 * rows * width * (n3 + width) + 4 * rows * rows * width,
        2 * (width * (n3 + width) + rows * (3 * width + n3)) + 4 * rows * width,
        "attention_forward",
        after,
        flushed=(0, 1, 2),
    )(s, x, ids[None, :], ids[:, None], gb, *qkv, *wo)


def mlp_kernel(experts, cap, hid, gb_ref, router, place, route, live, fc1, fc2, *refs, flush):
    normed2, act, slope, dense, normed3, soft = refs[:6]
    chunks = refs[6 : 6 + experts]
    w1, w2, sems = refs[6 + experts :]
    rows, width = hid.shape
    copies = [
        pltpu.make_async_copy(fc1, w1, sems.at[0]),
        pltpu.make_async_copy(fc2, w2, sems.at[1]),
    ]
    for c in copies:
        c.start()
    tile = rows // 6

    @pl.loop(0, 6)
    def _(i):
        at = pl.ds(pl.multiple_of(i * tile, 16), tile)
        n, _ = normalize(hid[at, :])
        normed2[at, :] = (n * gb_ref[2:3, :] + gb_ref[3:4, :]).astype(BF)
        dense[at, :] = hid[at, :]

    flush(0)
    for c in copies:
        c.wait()

    @pl.loop(0, w1.shape[1] // 512)
    def _(j):
        at = pl.ds(pl.multiple_of(j * 512, 512), 512)
        a, sl = gelu_pair(dot(normed2[...], w1[:, at]))
        act[:, at] = a.astype(BF)
        slope[:, at] = sl.astype(BF)
        dense[...] += dot(act[:, at], w2[at, :])

    flush(1)
    flush(2)
    flush(3)

    @pl.loop(0, 6)
    def _(i):
        at = pl.ds(pl.multiple_of(i * tile, 16), tile)
        n, _ = normalize(dense[at, :])
        normed3[at, :] = (n * gb_ref[4:5, :] + gb_ref[5:6, :]).astype(BF)

    flush(4)
    logits = dot_nt(router[...], normed3[...])
    expert = iota(logits.shape, 0)
    chosen = [
        jnp.sum(jnp.where(expert == route[k : k + 1, :], logits, 0.0), axis=0, keepdims=True)
        for k in range(TOP)
    ]
    top = jnp.maximum(chosen[0], chosen[1])
    raised = [jnp.exp(c - top) for c in chosen]
    total = raised[0] + raised[1]
    pieces = []
    for k in range(TOP):
        share = raised[k] / total
        soft[k : k + 1, :] = share
        three = split3(share * live[...])
        row = iota((16, rows), 0)
        pieces.append(
            jnp.where(row == 0, three[0].astype(F32), 0.0)
            + jnp.where(row == 1, three[1].astype(F32), 0.0)
            + jnp.where(row == 2, three[2].astype(F32), 0.0)
        )
    pieces = [p.astype(BF) for p in pieces]
    lanes = -(-cap // WIDE) * WIDE
    spot = iota((lanes, rows), 0)
    spot = jnp.where(spot < cap, spot, -2 * experts * cap)
    for r in range(experts):
        hot = [jnp.where(spot + r * cap == place[k : k + 1, :], 1.0, 0.0).astype(BF) for k in range(TOP)]
        both = (hot[0] + hot[1])[0:cap, :]
        chunks[r][0:cap, :] = dot(both, normed3[...]).astype(BF)
        chunks[r][cap : cap + 16, :] = jnp.zeros((16, width), BF)
        chunks[r][cap : cap + 16, 0:lanes] = (
            dot_nt(pieces[0], hot[0]) + dot_nt(pieces[1], hot[1])
        ).astype(BF)
        if r:
            flush(6 + r)


def mlp(hid, gb, router, place, route, live, fc1, fc2, experts, cap, after):
    rows, width = hid.shape
    ff = fc1.shape[1]
    return call(
        functools.partial(mlp_kernel, experts, cap),
        [VM, VM, VM, VM, VM, VM, HB, HB],
        [
            shape((rows, width), BF),
            shape((rows, ff), BF),
            shape((rows, ff), BF),
            shape((rows, width), F32),
            shape((rows, width), BF),
            shape((8, rows), F32),
        ]
        + [shape((cap + 16, width), BF)] * experts,
        [
            pltpu.VMEM((width, ff), BF),
            pltpu.VMEM((ff, width), BF),
            pltpu.SemaphoreType.DMA((2,)),
        ],
        4 * rows * width * ff + 2 * rows * width * experts * cap,
        4 * width * ff + rows * (4 * ff + 12 * width),
        "dense_forward",
        after,
        flushed=(0, 1, 2, 3, 4) + tuple(range(7, 6 + experts)),
    )(hid, gb, router, place, route, live, fc1, fc2)


def expert_kernel(cap, n, s_ref, *refs, flush):
    rows_in, dys = refs[:n], refs[n : 2 * n]
    own, other = refs[2 * n : 2 * n + GROUP], refs[2 * n + GROUP : 2 * n + 2 * GROUP]
    outs = refs[2 * n + 2 * GROUP : -3]
    wu, wd, sems = refs[-3:]
    s = s_ref[0]
    width = wu.shape[1]
    half = width // 2
    copies = [
        [
            pltpu.make_async_copy(
                src[b].at[u],
                w.at[b, pl.ds(pl.multiple_of(side * half, half), half)],
                sems.at[4 * b + 2 * h + u],
            )
            for h, (side, src) in enumerate(((s, own), (1 - s, other)))
            for u, w in enumerate((wu, wd))
        ]
        for b in range(GROUP)
    ]
    for b in range(GROUP):
        for c in copies[b]:
            c.start()
    lanes = -(-cap // WIDE) * WIDE
    eye = iota((lanes, lanes), 0) == iota((lanes, lanes), 1)
    gates = []
    for i in range(n):
        back, out, act, dinner, gp = outs[5 * i : 5 * i + 5]
        g = jnp.sum(rows_in[i][cap : cap + 16, 0:lanes].astype(F32), axis=0, keepdims=True)
        gate = jnp.sum(jnp.where(eye, g, 0.0), axis=1, keepdims=True)[0:cap, :]
        gp[...] = (gate * dys[i][...].astype(F32)).astype(BF)
        gates.append(gate)
    sums = [None] * n
    backs = [None] * n
    for b in range(GROUP):
        for c in copies[b]:
            c.wait()
        at = slice(b * width, (b + 1) * width)
        for i in range(n):
            back, out, act, dinner, gp = outs[5 * i : 5 * i + 5]
            a, slope = gelu_pair(dot(rows_in[i][0:cap, :], wu[b]))
            act[:, at] = a.astype(BF)
            dinner[:, at] = (dot(gp[...], wd[b]) * slope).astype(BF)
            o = dot_nt(act[:, at], wd[b])
            d = dot_nt(dinner[:, at], wu[b])
            sums[i] = o if b == 0 else sums[i] + o
            backs[i] = d if b == 0 else backs[i] + d
    for i in range(n):
        back, out, act, dinner, gp = outs[5 * i : 5 * i + 5]
        out[...] = (gates[i] * sums[i]).astype(BF)
        flush(5 * i + 1)
        back[0:cap, :] = backs[i].astype(BF)
        dg = jnp.sum(dys[i][...].astype(F32) * sums[i], axis=1, keepdims=True)
        pad = jnp.where(eye[0:cap, :], dg, 0.0)
        dg_row = jnp.sum(pad, axis=0, keepdims=True)
        three = split3(dg_row)
        row = iota((16, lanes), 0)
        back[cap : cap + 16, :] = jnp.zeros((16, width), BF)
        back[cap : cap + 16, 0:lanes] = (
            jnp.where(row == 0, three[0].astype(F32), 0.0)
            + jnp.where(row == 1, three[1].astype(F32), 0.0)
            + jnp.where(row == 2, three[2].astype(F32), 0.0)
        ).astype(BF)
        flush(5 * i)


def expert(s, rows_in, dys, own, other, cap):
    n = len(rows_in)
    width = rows_in[0].shape[1]
    ff = GROUP * width
    res = call(
        functools.partial(expert_kernel, cap, n),
        [SM] + [VM] * (2 * n) + [HB] * (2 * GROUP),
        [
            shape((cap + 16, width), BF),
            shape((cap, width), BF),
            shape((cap, ff), BF),
            shape((cap, ff), BF),
            shape((cap, width), BF),
        ]
        * n,
        [
            pltpu.VMEM((GROUP, width, width), BF),
            pltpu.VMEM((GROUP, width, width), BF),
            pltpu.SemaphoreType.DMA((16,)),
        ],
        8 * n * cap * width * ff,
        4 * width * ff + n * cap * (4 * ff + 10 * width),
        "expert",
        flushed=tuple(range(0, 5 * n, 5)) + tuple(range(1, 5 * n, 5)),
    )(s, *rows_in, *dys, *own, *other)
    return [res[5 * i : 5 * i + 5] for i in range(n)]


def grad_kernel(n, skip, s_ref, *refs):
    lefts, rights, refs = refs[:n], refs[n : 2 * n], refs[2 * n + skip :]
    give, keep = refs[:2]
    if n == 1:
        left, right = lefts[0], rights[0]
    else:
        left, right = refs[2:]
        rows = lefts[0].shape[0]
        for i in range(n):
            left[i * rows : (i + 1) * rows, :] = lefts[i][...]
            right[i * rows : (i + 1) * rows, :] = rights[i][...]
    value = dot_tn(left[...], right[...]).astype(BF)

    @pl.when(pl.program_id(0) == 0)
    def _():
        give[0] = value

    @pl.when(pl.program_id(0) == 1)
    def _():
        keep[0] = value


def weight_grad(s, lefts, rights, rows=None, weight=16, stride=1, into=()):
    n = len(lefts)
    t = rows or lefts[0].shape[0]
    width = min(lefts[0].shape[1], rights[0].shape[1])
    high = width // 2
    m, nb = lefts[0].shape[1] // width, rights[0].shape[1] // width
    scratch = []
    if n > 1:
        scratch = [pltpu.VMEM((n * t, high), BF), pltpu.VMEM((n * t, width), BF)]
    left_at = lambda h, i, j, c: (0, jnp.where(h == 0, 1 - c[0], c[0]) * m + i)
    offset = 1 if into else 0

    def place_of(k, c):
        return ((k ^ c[1]) * stride + offset, 0, 0)

    give_at = lambda h, i, j, c: place_of(jnp.where(h == 0, i * nb + j, m * nb - 1), c)
    keep_at = lambda h, i, j, c: place_of(jnp.where(h == 0, 0, i * nb + j), c)
    return pl.pallas_call(
        functools.partial(grad_kernel, n, len(into)),
        grid_spec=pltpu.PrefetchScalarGridSpec(
            num_scalar_prefetch=1,
            grid=(2, m, nb),
            in_specs=[pl.BlockSpec((t, high), left_at)] * n
            + [pl.BlockSpec((t, width), lambda h, i, j, c: (0, j))] * n
            + [HB] * len(into),
            out_specs=[pl.BlockSpec((1, high, width), at) for at in (give_at, keep_at)],
            scratch_shapes=scratch,
        ),
        out_shape=[shape((m * nb * stride, high, width), BF)] * 2,
        input_output_aliases={1 + 2 * n + i: i for i in range(len(into))},
        compiler_params=pltpu.CompilerParams(vmem_limit_bytes=LIMIT),
        cost_estimate=pl.CostEstimate(
            flops=int(weight * 4) * n * t * m * high * width * nb,
            bytes_accessed=int(weight * 2) * (n * t * (2 * m * high + width * nb) + 2 * m * high * width * nb),
            transcendentals=0,
        ),
        name="weight_grad",
    )(s, *lefts, *rights, *into)


def attention_grad_kernel(s_ref, normed, context, dpacked, dattn, give, keep):
    j = pl.program_id(1)

    def write(value):
        @pl.when(pl.program_id(0) == 0)
        def _():
            give[0] = value

        @pl.when(pl.program_id(0) == 1)
        def _():
            keep[0] = value

    @pl.when(j < 3)
    def _():
        write(dot_tn(normed[...], dpacked[...]).astype(BF))

    @pl.when(j == 3)
    def _():
        write(dot_tn(context[...], dattn[...]).astype(BF))


def attention_grad(s, normed, context, dpacked, dattn):
    t, width = normed.shape
    high = width // 2
    half_at = lambda h, j, c: (0, jnp.where(h == 0, 1 - c[0], c[0]))
    return pl.pallas_call(
        attention_grad_kernel,
        grid_spec=pltpu.PrefetchScalarGridSpec(
            num_scalar_prefetch=1,
            grid=(2, 4),
            in_specs=[
                pl.BlockSpec((t, high), half_at),
                pl.BlockSpec((t, high), half_at),
                pl.BlockSpec((t, width), lambda h, j, c: (0, jnp.minimum(j, 2))),
                pl.BlockSpec((t, width), lambda h, j, c: (0, 0)),
            ],
            out_specs=[
                pl.BlockSpec((1, high, width), lambda h, j, c: (jnp.where(h == 0, j, 3), 0, 0)),
                pl.BlockSpec((1, high, width), lambda h, j, c: (jnp.where(h == 0, 0, j), 0, 0)),
            ],
        ),
        out_shape=[shape((4, high, width), BF)] * 2,
        compiler_params=pltpu.CompilerParams(vmem_limit_bytes=LIMIT),
        cost_estimate=pl.CostEstimate(
            flops=t * width * width, bytes_accessed=t * width, transcendentals=0
        ),
        name="attention_grad",
    )(s, normed, context, dpacked, dattn)


def back_kernel(
    experts, cap, dy, dense, hid, gb_ref, router, place, route, live, soft, normed3, slope, fc1, fc2, *refs
):
    homes = refs[:experts]
    dmlp, dpre, dhidden, tiny, drouter = refs[experts : experts + 5]
    w1, w2, ups, sems = refs[experts + 5 :]
    rows, width = hid.shape
    copies = [
        pltpu.make_async_copy(fc1, w1, sems.at[0]),
        pltpu.make_async_copy(fc2, w2, sems.at[1]),
    ]
    for c in copies:
        c.start()
    lanes = -(-cap // WIDE) * WIDE
    spot = iota((lanes, rows), 0)
    spot = jnp.where(spot < cap, spot, -2 * experts * cap)
    dgate = [jnp.zeros((16, rows), F32) for _ in range(TOP)]
    for r in range(experts):
        tail = homes[r][cap : cap + 16, 0:lanes]
        hot = [jnp.where(spot + r * cap == place[k : k + 1, :], 1.0, 0.0).astype(BF) for k in range(TOP)]
        for k in range(TOP):
            dgate[k] = dgate[k] + dot(tail, hot[k])
        term = dot_tn((hot[0] + hot[1])[0:cap, :], homes[r][0:cap, :])
        ups[...] = term if r == 0 else ups[...] + term
    dgate = [jnp.sum(d, axis=0, keepdims=True) * live[...] for d in dgate]
    mix = soft[0:1, :] * dgate[0] + soft[1:2, :] * dgate[1]
    dsoft = [soft[k : k + 1, :] * (dgate[k] - mix) for k in range(TOP)]
    index = iota((router.shape[0], rows), 0)
    dlogits = sum(jnp.where(index == route[k : k + 1, :], dsoft[k], 0.0) for k in range(TOP))
    dlogits = dlogits.astype(BF)
    drouter[...] = dot(dlogits, normed3[...])
    ups[...] += dot_tn(dlogits, router[...])
    tile = rows // 6
    tiny[...] = jnp.zeros_like(tiny)

    def norm_back(at, values, gain, bias_row, base):
        n, scale = normalize(values)
        u = ups[at, :]
        tiny[bias_row - 1 : bias_row, :] += jnp.sum(u * n, axis=0, keepdims=True)
        tiny[bias_row : bias_row + 1, :] += jnp.sum(u, axis=0, keepdims=True)
        ug = u * gain
        dv = scale * (
            ug
            - jnp.mean(ug, axis=-1, keepdims=True)
            - n * jnp.mean(ug * n, axis=-1, keepdims=True)
        )
        return base + dv

    @pl.loop(0, 6)
    def _(i):
        at = pl.ds(pl.multiple_of(i * tile, 16), tile)
        dd = norm_back(at, dense[at, :], gb_ref[4:5, :], 5, dy[at, :].astype(F32))
        dhidden[at, :] = dd
        dmlp[at, :] = dd.astype(BF)

    for c in copies:
        c.wait()
    ups[...] = jnp.zeros_like(ups)

    @pl.loop(0, w1.shape[1] // 512)
    def _(j):
        at = pl.ds(pl.multiple_of(j * 512, 512), 512)
        dpre[:, at] = (dot_nt(dmlp[...], w2[at, :]) * slope[:, at].astype(F32)).astype(BF)
        ups[...] += dot_nt(dpre[:, at], w1[:, at])

    @pl.loop(0, 6)
    def _(i):
        at = pl.ds(pl.multiple_of(i * tile, 16), tile)
        dhidden[at, :] = norm_back(at, hid[at, :], gb_ref[2:3, :], 3, dhidden[at, :])


def back(
    dy, dense, hid, gb, router, place, route, live, soft, normed3, slope, fc1, fc2, homes, experts, cap, after
):
    rows, width = hid.shape
    ff = fc1.shape[1]
    return call(
        functools.partial(back_kernel, experts, cap),
        [VM] * 11 + [HB] * 2 + [VM] * experts,
        [
            shape((rows, width), BF),
            shape((rows, ff), BF),
            shape((rows, width), F32),
            shape((8, width), F32),
            shape(router.shape, F32),
        ],
        [
            pltpu.VMEM((width, ff), BF),
            pltpu.VMEM((ff, width), BF),
            pltpu.VMEM((rows, width), F32),
            pltpu.SemaphoreType.DMA((2,)),
        ],
        4 * rows * width * ff + 2 * rows * width * experts * cap,
        4 * width * ff + rows * (4 * ff + 18 * width),
        "dense_backward",
        after,
    )(dy, dense, hid, gb, router, place, route, live, soft, normed3, slope, fc1, fc2, *homes)


def attend_back_kernel(
    s_ref, dhid, id_row, id_col, packed, lse, wo_a, wo_b, dattn, dpacked, wo, bias, dctx, sems
):
    s = s_ref[0]
    rows, width = dhid.shape
    copies = halves_into(s, wo_a, wo_b, wo, sems, 0)
    for c in copies:
        c.start()
    tile = rows // 6

    @pl.loop(0, 6)
    def _(i):
        at = pl.ds(pl.multiple_of(i * tile, 16), tile)
        dattn[at, :] = dhid[at, :].astype(BF)
        bias[at, :] = jnp.where(id_col[at, :] == id_row[...], 0.0, MASKED)

    copies[0].wait()
    copies[1].wait()

    @pl.loop(0, width // 256)
    def _(j):
        at = pl.ds(pl.multiple_of(j * 256, 256), 256)
        dctx[:, at] = dot_nt(dattn[...], wo[at, :]).astype(BF)

    lane = iota((1, WIDE), 1)

    @pl.loop(0, width // WIDE)
    def _(pair):
        col = pl.multiple_of(pair * WIDE, WIDE)
        q = packed[:, pl.ds(col, WIDE)] * jnp.asarray(HEAD**-0.5, BF)
        keys = packed[:, pl.ds(width + col, WIDE)]
        values = packed[:, pl.ds(2 * width + col, WIDE)]
        dc = dctx[:, pl.ds(col, WIDE)]
        dq, dk, dv = [], [], []
        for h in range(2):
            mine = (lane >= h * HEAD) & (lane < (h + 1) * HEAD)
            scores = dot_nt(jnp.where(mine, keys, jnp.zeros_like(keys)), q) + bias[...]
            p = jnp.exp(scores - lse[pl.ds(2 * pair + h, 1), :])
            dp = dot_nt(jnp.where(mine, values, jnp.zeros_like(values)), dc)
            inner = jnp.sum(p * dp, axis=0, keepdims=True)
            ds = (p * (dp - inner)).astype(BF)
            dv.append(dot(p.astype(BF), dc))
            dk.append(dot(ds, q))
            dq.append(dot_tn(ds, keys) * HEAD**-0.5)
        low = lane < HEAD
        dpacked[:, pl.ds(col, WIDE)] = jnp.where(low, dq[0], dq[1]).astype(BF)
        dpacked[:, pl.ds(width + col, WIDE)] = jnp.where(low, dk[0], dk[1]).astype(BF)
        dpacked[:, pl.ds(2 * width + col, WIDE)] = jnp.where(low, dv[0], dv[1]).astype(BF)


def input_kernel(s_ref, x_ref, dhid, gb_ref, dpacked, qkv_a, qkv_b, grad_in, tiny, wq, ups, sems):
    s = s_ref[0]
    rows, width = x_ref.shape
    tile = rows // 6
    copies = halves_into(s, qkv_a, qkv_b, wq, sems, 0)
    for c in copies:
        c.start()
    copies[0].wait()
    copies[1].wait()

    @pl.loop(0, width // 256)
    def _(j):
        at = pl.ds(pl.multiple_of(j * 256, 256), 256)
        ups[:, at] = dot_nt(dpacked[...], wq[at, :])

    tiny[...] = jnp.zeros_like(tiny)

    @pl.loop(0, 6)
    def _(i):
        at = pl.ds(pl.multiple_of(i * tile, 16), tile)
        n, scale = normalize(x_ref[at, :].astype(F32))
        u = ups[at, :]
        tiny[0:1, :] += jnp.sum(u * n, axis=0, keepdims=True)
        tiny[1:2, :] += jnp.sum(u, axis=0, keepdims=True)
        ug = u * gb_ref[0:1, :]
        grad_in[at, :] = dhid[at, :] + scale * (
            ug
            - jnp.mean(ug, axis=-1, keepdims=True)
            - n * jnp.mean(ug * n, axis=-1, keepdims=True)
        )


def attend_back(s, dhid, ids, packed, lse, wo, after):
    rows, width = dhid.shape
    n3 = packed.shape[1]
    return call(
        attend_back_kernel,
        [SM] + [VM] * 5 + [HB] * 2,
        [shape((rows, width), BF), shape((rows, n3), BF)],
        [
            pltpu.VMEM((width, width), BF),
            pltpu.VMEM((rows, rows), F32),
            pltpu.VMEM((rows, width), BF),
            pltpu.SemaphoreType.DMA((2,)),
        ],
        2 * rows * width * width + 20 * rows * rows * width,
        2 * (width * width + rows * (3 * width + 2 * n3)),
        "attention_backward",
        after,
    )(s, dhid, ids[None, :], ids[:, None], packed, lse, *wo)


def input_back(s, x, dhid, gb, dpacked, qkv, after):
    rows, width = x.shape
    n3 = dpacked.shape[1]
    return call(
        input_kernel,
        [SM] + [VM] * 4 + [HB] * 2,
        [shape((rows, width), F32), shape((8, width), F32)],
        [
            pltpu.VMEM((width, n3), BF),
            pltpu.VMEM((rows, width), F32),
            pltpu.SemaphoreType.DMA((2,)),
        ],
        2 * rows * width * n3,
        2 * (width * n3 + rows * n3) + 10 * rows * width,
        "input_backward",
        after,
    )(s, x, dhid, gb, dpacked, *qkv)


def merge_kernel(experts, cap, dense, place, *refs):
    outs, result = refs[:experts], refs[experts]
    rows = dense.shape[0]
    total = dense[...]
    spot = iota((cap, rows), 0)
    for r in range(experts):
        hot = sum(jnp.where(spot + r * cap == place[k : k + 1, :], 1.0, 0.0) for k in range(TOP))
        total = total + dot_tn(hot.astype(BF), outs[r][...])
    result[...] = total.astype(BF)


def merge(dense, place, outs, experts, cap):
    rows, width = dense.shape
    return call(
        functools.partial(merge_kernel, experts, cap),
        [VM] * (2 + experts),
        shape((rows, width), BF),
        [],
        2 * rows * width * experts * cap,
        rows * width * 6 + 2 * experts * cap * width,
        "merge",
        (),
        0.25,
    )(dense, place, *outs)


def hold_kernel(n, *refs):
    for i in range(n):
        refs[n + i][...] = refs[i][...]


def hold(chunks, after):
    n = len(chunks)
    dims = chunks[0].shape
    return call(
        functools.partial(hold_kernel, n),
        [VM] * n,
        [shape(dims, BF)] * n,
        [],
        0,
        4 * n * dims[0] * dims[1],
        "hold",
        after,
    )(*chunks)


def finish_kernel(columns, m_ref, mine, got, out):
    n, high, width = mine.shape
    for which, src in ((m_ref[0], mine), (1 - m_ref[0], got)):
        for i in range(n):
            value = src[i].astype(F32)
            if columns:
                out[:, pl.ds(pl.multiple_of((which * n + i) * width, width), width)] = value
            else:
                out[pl.ds(pl.multiple_of((which * n + i) * high, high), high), :] = value


def finish(m, mine, got, columns):
    n, high, width = mine.shape
    dims = (high, 2 * n * width) if columns else (2 * n * high, width)
    return call(
        functools.partial(finish_kernel, columns),
        [SM, VM, VM],
        shape(dims, F32),
        [],
        0,
        12 * n * high * width,
        "finish",
    )(m, mine, got)


def spread_kernel(experts, cap, rows_in, place, *chunks):
    spot = iota((cap, rows_in.shape[0]), 0)
    for r in range(experts):
        hot = sum(jnp.where(spot + r * cap == place[k : k + 1, :], 1.0, 0.0) for k in range(TOP))
        chunks[r][...] = dot(hot.astype(BF), rows_in[...]).astype(BF)


def spread(rows_in, place, experts, cap):
    rows, width = rows_in.shape
    return call(
        functools.partial(spread_kernel, experts, cap),
        [VM, VM],
        [shape((cap, width), BF)] * experts,
        [],
        2 * rows * width * experts * cap,
        2 * (rows + experts * cap) * width,
        "spread",
    )(rows_in, place)


def places_of(routes, live, experts, capacity):
    tokens = routes.shape[0]
    ids = jnp.arange(experts, dtype=jnp.int32)
    match = [
        ((routes[:, k : k + 1] == ids[None, :]) & live[:, None]).astype(F32) for k in range(TOP)
    ]
    order = jnp.arange(tokens, dtype=jnp.int32)
    below = (order[:, None] > order[None, :]).astype(BF)
    before = jnp.zeros((1, experts), F32)
    out = []
    for k in range(TOP):
        counts = dot(below, match[k].astype(BF)) + before
        before = before + jnp.sum(match[k], axis=0, keepdims=True)
        within = jnp.sum(counts * match[k], axis=1).astype(jnp.int32)
        out.append(jnp.where(live, routes[:, k] * capacity + within, experts * capacity))
    return out

def local(
    tokens,
    image_ids,
    routes,
    norm1_gain,
    norm1_bias,
    qkv_weight,
    attn_out_weight,
    norm2_gain,
    norm2_bias,
    fc1_weight,
    fc2_weight,
    norm3_gain,
    norm3_bias,
    router_weight,
    expert_up,
    expert_down,
    cotangent,
):
    s = lax.axis_index("section")
    e = lax.axis_index("dp") // GROUP
    q = lax.axis_index("dp") % GROUP
    dp_count = lax.axis_size("dp")
    experts = dp_count // GROUP
    cap = GROUP * ((21 * SLOTS + 10 * experts * GROUP - 1) // (10 * experts * GROUP))
    cap = -(-cap // 16) * 16
    half = tokens.shape[1]
    width = 2 * half
    few = experts <= 8
    planes = [[p * GROUP + i for p in range(experts)] for i in range(GROUP)]
    here, here_q = jnp.stack([s, 0 * s]), jnp.stack([s, q])
    quads = [[p * GROUP + i for i in range(GROUP)] for p in range(experts)]

    def swap(v):
        return lax.ppermute(v, "section", [(0, 1), (1, 0)])

    def over_q(v, bit):
        return lax.ppermute(v, "dp", [(i, i ^ bit) for i in range(dp_count)])

    def over_e(v, r):
        return lax.ppermute(
            v,
            "dp",
            [(i, ((i // GROUP + r) % experts) * GROUP + i % GROUP) for i in range(dp_count)],
        )

    def part(v, index, size, axis=0):
        return lax.dynamic_slice_in_dim(v, index * size, size, axis)

    def join(own, other, axis):
        return jnp.where(
            s == 0,
            jnp.concatenate([own, other], axis=axis),
            jnp.concatenate([other, own], axis=axis),
        )

    def add(a, b):
        return (a.astype(F32) + b.astype(F32)).astype(BF)

    def out_chunks(chunks):
        if not few:
            return list(lax.all_to_all(jnp.stack(chunks), "dp", 0, 0, axis_index_groups=planes))
        return [chunks[0]] + [over_e(chunks[r], r) for r in range(1, experts)]

    def home_chunks(chunks):
        if not few:
            return list(lax.all_to_all(jnp.stack(chunks), "dp", 0, 0, axis_index_groups=planes))
        return [chunks[0]] + [over_e(chunks[r], experts - r) for r in range(1, experts)]

    small = jnp.stack([norm1_gain, norm1_bias, norm2_gain, norm2_bias, norm3_gain, norm3_bias])
    small = jnp.concatenate([small, jnp.transpose(router_weight)])
    small = join(small, swap(small), 1)
    x = join(part(tokens, s, SLOTS), swap(part(tokens, 1 - s, SLOTS)), 1)
    dy = join(part(cotangent, s, SLOTS), swap(part(cotangent, 1 - s, SLOTS)), 1)
    ids = part(image_ids, s, 1).reshape(-1)
    route = part(routes, s, SLOTS)
    live = ids >= 0
    gb = jnp.concatenate([small[:6], jnp.zeros((2, width), BF)]).astype(F32)
    router_rows = -(-experts // 16) * 16
    router = jnp.concatenate([small[6 : 6 + experts], jnp.zeros((router_rows - experts, width), BF)])
    qkv, wo = (qkv_weight, swap(qkv_weight)), (attn_out_weight, swap(attn_out_weight))

    pair = jnp.stack([expert_up, expert_down])

    def gather(v, tiled):
        return lax.all_gather(v, "section", axis=0, tiled=tiled)

    tie = lax.optimization_barrier
    x, dy, qkv, wo, fc1_weight, fc2_weight, pair = tie(
        (x, dy, qkv, wo, fc1_weight, fc2_weight, pair)
    )
    fc1, fc2 = gather(fc1_weight, True), gather(fc2_weight, True)
    from_x, from_y, other_pair = over_q(pair, 1), over_q(pair, 2), swap(pair)

    if few:
        distance = (route - e) % experts
    else:
        distance = route
    spots = places_of(distance, live, experts, cap)
    place = jnp.stack(spots + [jnp.full_like(spots[0], -1)] * 6)
    route_rows = jnp.concatenate([jnp.transpose(route), jnp.full((6, SLOTS), -1, jnp.int32)])
    live_row = live.astype(F32)[None, :]
    dy_sent = spread(dy, place, experts, cap)
    dy_out = out_chunks(dy_sent)

    normed1, packed, context, lse, hidden = front(here, x, ids, gb, qkv, wo, dy_sent[:1])
    hidden, from_x, from_y, other_pair, *dy_out[:-1] = tie(
        (hidden, from_x, from_y, other_pair, *dy_out[:-1])
    )
    other_x, other_y = swap(from_x), swap(from_y)
    far = over_q(from_x, 2)
    normed2, act, slope, dense, normed3, soft, *sent = mlp(
        hidden, gb, router, place, route_rows, live_row, fc1, fc2, experts, cap, []
    )
    sent, other_x, other_y, dy_out[-1] = tie((sent, other_x, other_y, dy_out[-1]))
    got = out_chunks(sent)
    got[0], far = tie((got[0], far))
    own, other = [pair, from_x, from_y, far], [other_pair, other_x, other_y, swap(far)]

    step = max(1, experts // 4)
    results = [None] * experts
    previous, homes = None, [None] * experts
    order = [0, 3, 1, 2] if experts == 4 else list(range(0, experts, step))
    for place_in_order, i in enumerate(order):
        if i:
            got[i], results[previous] = tie((got[i], results[previous]))
        if few and place_in_order == 3:
            got[i], homes[order[1]] = tie((got[i], homes[order[1]]))
        results[i : i + step] = expert(
            here, got[i : i + step], dy_out[i : i + step], own, other, cap
        )
        previous = i
        homes[i] = over_e(results[i][0], experts - i) if few and i else results[i][0]
    if not few:
        homes = home_chunks([r[0] for r in results])
    acts, dinners, scaled = ([r[i] for r in results] for i in (2, 3, 4))

    if experts == 4:
        dinners, homes[1] = tie((dinners, homes[1]))
    up_grads = weight_grad(here_q, got, dinners, cap, stride=2)
    dmlp, dpre, dhidden, tiny23, drouter = back(
        dy, dense, hidden, gb, router, place, route_rows, live_row, soft, normed3, slope,
        fc1, fc2, homes, experts, cap, [],
    )
    outs = hold([r[1] for r in results], [dmlp])
    grads1, grads2 = weight_grad(here, [normed2], [dpre]), weight_grad(here, [act], [dmlp])
    acts, grads1, grads2 = tie((acts, grads1, grads2))
    expert_grads = weight_grad(here_q, scaled, acts, stride=2, into=up_grads)

    def fold(v, bit):
        mine, rows = (q // bit) % 2, v.shape[0] // 2
        return part(v, mine, rows), over_q(part(v, 1 - mine, rows), bit)

    def unfold(v, got, bit):
        return jnp.where(
            (q // bit) % 2 == 0, jnp.concatenate([v, got]), jnp.concatenate([got, v])
        )

    def plane_out(a, b):
        ab = jnp.stack([a, b])
        rows = a.shape[0] // experts
        if not few:
            return [lax.psum(ab, "dp", axis_index_groups=planes)]
        return [part(ab, (e + r) % experts, rows, 1) for r in range(experts)]

    def plane_sum(pieces):
        if not few:
            return pieces
        total = sum(p.astype(F32) for p in pieces).astype(BF)
        return [total] * experts

    def plane_move(pieces):
        return pieces[:1] + [over_e(p, r) for r, p in enumerate(pieces) if r]

    def plane_join(pieces):
        if not few:
            return pieces[0][0], pieces[0][1]
        rows = pieces[0].shape[1]
        whole = jnp.zeros((2, experts * rows, width), BF)
        for r, piece in enumerate(pieces):
            whole = lax.dynamic_update_slice_in_dim(whole, piece, ((e - r) % experts) * rows, 1)
        return whole[0], whole[1]

    away1, away2 = swap(grads1[0]), swap(grads2[0])
    dhidden, away1, away2, grads1, grads2, expert_grads = tie(
        (dhidden, away1, away2, grads1, grads2, expert_grads)
    )
    a, b = add(grads2[1], away2).reshape(-1, width), add(grads1[1], away1).reshape(-1, width)
    a, b = fold(a, 1), fold(b, 2)
    dattn, dpacked = attend_back(here, dhidden, ids, packed, lse, wo, [])
    home_outs = home_chunks(outs)
    give, keep = attention_grad(here, normed1, context, dpacked, dattn)
    give, keep, a, b, dpacked, home_outs = tie((give, keep, a, b, dpacked, home_outs))
    grad_in, tiny1 = input_back(here, x, dhidden, gb, dpacked, qkv, [])
    tiny = jnp.concatenate([tiny1[:2], tiny23[2:6], drouter[:experts]])

    def swapped(v):
        return part(v, s, half, 1), swap(part(v, 1 - s, half, 1))

    away = swap(give)
    a, b = fold(add(*a), 2), fold(add(*b), 1)
    sum_experts = add(expert_grads[1], swap(expert_grads[0]))
    tiny = swapped(tiny)
    away, a, b, grad_in, tiny, sum_experts = tie((away, a, b, grad_in, tiny, sum_experts))
    half_experts = lax.psum_scatter(
        sum_experts.reshape(GROUP, 2, half, -1),
        "dp", scatter_dimension=0, axis_index_groups=quads, tiled=False,
    )
    grad_in = swapped(grad_in)
    tiny = tiny[0] + tiny[1]

    ab = plane_move(plane_out(add(*a), add(*b)))
    t = add(keep, away).reshape(-1, width)
    ta, tb = fold(t[:width], 1), fold(t[width:], 2)
    ab, ta, tb = tie((ab, ta, tb))
    block_out = merge(dense, place, home_outs, experts, cap)

    ab = plane_move(plane_sum(ab))
    ta, tb = fold(add(*ta), 2), fold(add(*tb), 1)
    ab, ta, tb, block_out = tie((ab, ta, tb, block_out))

    a, b = plane_join(ab)
    a_got, b_got = over_q(a, 2), over_q(b, 1)
    tab = plane_move(plane_out(add(*ta), add(*tb)))
    a_got, b_got, tab = tie((a_got, b_got, tab))
    a, b = unfold(a, a_got, 2), unfold(b, b_got, 1)
    a_got, b_got = over_q(a, 1), over_q(b, 2)
    tab = plane_move(plane_sum(tab))
    a_got, b_got, tab = tie((a_got, b_got, tab))

    side_x, side_y = jnp.reshape(q % 2, (1,)), jnp.reshape(q // 2, (1,))

    def blocks(v):
        return v.reshape(-1, half, width)

    ta, tb = plane_join(tab)
    ta_got, tb_got = over_q(ta, 2), over_q(tb, 1)
    block_out = swapped(block_out)
    tiny_q = [over_q(tiny, bit) for bit in (1, 2, 3)]
    sum_fc2 = finish(side_x, blocks(a), blocks(a_got), False)
    sum_fc1 = finish(side_y, blocks(b), blocks(b_got), True)
    ta_got, tb_got, block_out, grad_in, tiny_q, sum_fc2, sum_fc1, half_experts = tie(
        (ta_got, tb_got, block_out, grad_in, tiny_q, sum_fc2, sum_fc1, half_experts)
    )
    half_up, half_down = half_experts[0].astype(F32), half_experts[1].astype(F32)
    ta, tb = unfold(ta, ta_got, 2), unfold(tb, tb_got, 1)
    ta_got, tb_got = over_q(ta, 1), over_q(tb, 2)
    tiny = tiny + tiny_q[0] + (tiny_q[1] + tiny_q[2])
    if few:
        total = sum(over_e(tiny, r) if r else tiny for r in range(experts))
    else:
        total = lax.psum(tiny, "dp", axis_index_groups=planes)
    q_and_k = finish(side_x, blocks(ta), blocks(ta_got), True)
    first = q // 2 == 0
    v_sum, sum_attn = (
        jnp.where(first, p, r).astype(F32) for p, r in ((tb, tb_got), (tb_got, tb))
    )
    sum_qkv = jnp.concatenate([q_and_k, v_sum], axis=1)
    return (
        join(*block_out, 0),
        join(*grad_in, 0),
        total[0],
        total[1],
        sum_qkv,
        sum_attn,
        total[2],
        total[3],
        sum_fc1,
        sum_fc2,
        total[4],
        total[5],
        jnp.transpose(total[6:]),
        half_up,
        half_down,
    )


def solution(mesh):
    placed = (
        P("dp", "section"),
        P("dp", None),
        P("dp", None),
        P("section"),
        P("section"),
        P("section", None),
        P("section", None),
        P("section"),
        P("section"),
        P("section", None),
        P("section", None),
        P("section"),
        P("section"),
        P("section", None),
        P("section", "dp"),
        P("section", "dp"),
        P("dp", "section"),
    )
    return jax.shard_map(
        local,
        mesh=mesh,
        in_specs=placed,
        out_specs=(
            P("dp", "section"),
            P("dp", "section"),
            P("section"),
            P("section"),
            P("section", None),
            P("section", None),
            P("section"),
            P("section"),
            P("section", None),
            P("section", None),
            P("section"),
            P("section"),
            P("section", None),
            P("section", "dp"),
            P("section", "dp"),
        ),
        check_vma=False,
    )
```

profile of v0, /device:TPU:0, one launch (start us, length us, event | category | flops | bytes accessed | tf_op | source)
XLA Modules:
  0.0 474.2 jit_solution(254296516202208139)
XLA Ops:
  33.1 21.3 %attention_forward.1 = (bf16[576,768]{1,0:T(8,128)(2,1)}, bf16[576,2304]{1,0:T(8,128)(2,1)}, bf16[576,768]{1,0:T(8,128)(2,1)}, f32[16,576]{1,0:T(8,128)S(1)}, f32[576,768]{1,0:T(8,128)S(1)}) custom-call(s32[2]{0:T(128)S(1)} %pad_add_fusion.refs_0_.s_ref, bf16[576,768]{1,0:T(8,128)(2,1)S(1)} %maximum_select_fusion.3.refs_1_, ...), custom_call_target="tpu_custom_call" | custom-call | flops 59793997824 | bytes 188743680 | tf_op jit(solution)/shard_map/attention_forward/pallas_call | solution.py:135
  67.7 18.9 %dense_forward.1 = (bf16[576,768]{1,0:T(8,128)(2,1)}, bf16[576,3072]{1,0:T(8,128)(2,1)}, bf16[576,3072]{1,0:T(8,128)(2,1)}, f32[576,768]{1,0:T(8,128)}, bf16[576...) custom-call(f32[576,768]{1,0:T(8,128)S(1)} %copy-done.41, ...), custom_call_target="tpu_custom_call" | custom-call | flops 104186511360 | bytes 349175808 | tf_op jit(solution)/shard_map/dense_forward/pallas_call | solution.py:135
  94.7 11.2 %expert.4 = (bf16[320,768]{1,0:T(8,128)(2,1)}, bf16[304,768]{1,0:T(8,128)(2,1)}, bf16[304,3072]{1,0:T(8,128)(2,1)S(1)}, bf16[304,3072]{1,0:T(8,128)(2,1)S(1)}, bf16[304,768]{1,0:T(8,128)(2,1)S(1)}) custom-call(s32[2]{0:T(128)S(1)} %pad_add_fusion.refs_0_.s_ref, bf16[320,768]{1,0:T(8,128)(2,1)S(1)} %copy-done.64, bf16[304,768]{1,0:T(8,128)(2,1)S(1)} %copy-done.38, ...), custom_call_target="tpu_custom_call" | custom-call | flops 91804925952 | bytes 248119296 | tf_op jit(solution)/shard_map/expert/pallas_call | solution.py:135
  108.0 7.7 %collective-permute-done.15.refs_1_.refs_3_ = bf16[320,768]{1,0:T(8,128)(2,1)S(1)} collective-permute-done((bf16[320,768]{1,0:T(8,128)(2,1)}, bf16[320,768]{1,0:T(8,128)(2,1)S(1)}, u32[]{:S(2)}, u32[]{:S(2)}) %collective-permute-start.15) | collective-permute-done | bytes 491552 | tf_op jit(solution)/shard_map/ppermute | solution.py:916
  115.6 11.4 %expert.5 = (bf16[320,768]{1,0:T(8,128)(2,1)}, bf16[304,768]{1,0:T(8,128)(2,1)}, bf16[304,3072]{1,0:T(8,128)(2,1)S(1)}, bf16[304,3072]{1,0:T(8,128)(2,1)S(1)}, bf16[304,768]{1,0:T(8,128)(2,1)S(1)}) custom-call(s32[2]{0:T(128)S(1)} %pad_add_fusion.refs_0_.s_ref, bf16[320,768]{1,0:T(8,128)(2,1)S(1)} %collective-permute-done.15.refs_1_.refs_3_, ...), custom_call_target="tpu_custom_call" | custom-call | flops 91804925952 | bytes 248119296 | tf_op jit(solution)/shard_map/expert/pallas_call | solution.py:135
  129.0 12.2 %expert.6 = (bf16[320,768]{1,0:T(8,128)(2,1)}, bf16[304,768]{1,0:T(8,128)(2,1)}, bf16[304,3072]{1,0:T(8,128)(2,1)S(1)}, bf16[304,3072]{1,0:T(8,128)(2,1)S(1)}, bf16[304,768]{1,0:T(8,128)(2,1)S(1)}) custom-call(s32[2]{0:T(128)S(1)} %pad_add_fusion.refs_0_.s_ref, bf16[320,768]{1,0:T(8,128)(2,1)} %collective-permute-done.17.refs_1_, ...), custom_call_target="tpu_custom_call" | custom-call | flops 91804925952 | bytes 248119296 | tf_op jit(solution)/shard_map/expert/pallas_call | solution.py:135
  147.2 12.2 %expert.7 = (bf16[320,768]{1,0:T(8,128)(2,1)}, bf16[304,768]{1,0:T(8,128)(2,1)}, bf16[304,3072]{1,0:T(8,128)(2,1)S(1)}, bf16[304,3072]{1,0:T(8,128)(2,1)S(1)}, bf16[304,768]{1,0:T(8,128)(2,1)S(1)}) custom-call(s32[2]{0:T(128)S(1)} %pad_add_fusion.refs_0_.s_ref, bf16[320,768]{1,0:T(8,128)(2,1)} %collective-permute-done.16.refs_1_.refs_2_, ...), custom_call_target="tpu_custom_call" | custom-call | flops 91804925952 | bytes 248119296 | tf_op jit(solution)/shard_map/expert/pallas_call | solution.py:135
  165.3 11.3 %weight_grad.6 = (bf16[8,384,768]{2,1,0:T(8,128)(2,1)S(1)}, bf16[8,384,768]{2,1,0:T(8,128)(2,1)S(1)}) custom-call(s32[2]{0:T(128)S(1)} %pad_add_fusion.1.s_ref, bf16[320,768]{1,0:T(8,128)(2,1)S(1)} %copy-done.65, bf16[320,768]{1,0:T(8,128)(2,1)} %collective-permute-done.17.refs_1_, bf16[320,768]{1,0:T(8,128)(2,1)} %collective-permute-done.16.refs_1_.refs_2_, ...), custom_call_target="tpu_custom_call" | custom-call | flops 91804925952 | bytes 224919552 | tf_op jit(solution)/shard_map/weight_grad/pallas_call | solution.py:475
  178.8 7.0 %collective-permute-done.20.refs_15_ = bf16[320,768]{1,0:T(8,128)(2,1)S(1)} collective-permute-done((bf16[320,768]{1,0:T(8,128)(2,1)}, bf16[320,768]{1,0:T(8,128)(2,1)S(1)}, u32[]{:S(2)}, u32[]{:S(2)}) %collective-permute-start.20) | collective-permute-done | bytes 491552 | tf_op jit(solution)/shard_map/ppermute | solution.py:916
  187.6 18.8 %dense_backward.1 = (bf16[576,768]{1,0:T(8,128)(2,1)S(1)}, bf16[576,3072]{1,0:T(8,128)(2,1)S(1)}, f32[576,768]{1,0:T(8,128)S(1)}, f32[8,768]{1,0:T(8,128)S(1)}, f32[16,768]{1,0:T(8,128)S(1)}) custom-call(bf16[576,768]{1,0:T(8,128)(2,1)S(1)} %maximum_select_fusion.4.refs_0_, f32[576,768]{1,0:T(8,128)S(1)} %copy-done, f32[576,768]{1,0:T(8,128)S(1)} %copy-done.42, ...), custom_call_target="tpu_custom_call" | custom-call | flops 104186511360 | bytes 391643136 | tf_op jit(solution)/shard_map/dense_backward/pallas_call | solution.py:135
  213.0 7.0 %weight_grad.5 = (bf16[4,384,768]{2,1,0:T(8,128)(2,1)S(1)}, bf16[4,384,768]{2,1,0:T(8,128)(2,1)S(1)}) custom-call(s32[2]{0:T(128)S(1)} %pad_add_fusion.refs_0_.s_ref, bf16[576,3072]{1,0:T(8,128)(2,1)S(1)} %copy-done.31, bf16[576,768]{1,0:T(8,128)(2,1)S(1)} %get-tuple-element.276.refs_1_.refs_4_), custom_call_target="tpu_custom_call" | custom-call | flops 43486543872 | bytes 146276352 | tf_op jit(solution)/shard_map/weight_grad/pallas_call | solution.py:475
  220.1 7.2 %weight_grad.4 = (bf16[4,384,768]{2,1,0:T(8,128)(2,1)S(1)}, bf16[4,384,768]{2,1,0:T(8,128)(2,1)S(1)}) custom-call(s32[2]{0:T(128)S(1)} %pad_add_fusion.refs_0_.s_ref, bf16[576,768]{1,0:T(8,128)(2,1)S(1)} %copy-done.43, bf16[576,3072]{1,0:T(8,128)(2,1)S(1)} %copy-done.33), custom_call_target="tpu_custom_call" | custom-call | flops 43486543872 | bytes 146276352 | tf_op jit(solution)/shard_map/weight_grad/pallas_call | solution.py:475
  228.0 10.6 %weight_grad.7 = (bf16[8,384,768]{2,1,0:T(8,128)(2,1)S(1)}, bf16[8,384,768]{2,1,0:T(8,128)(2,1)S(1)}) custom-call(s32[2]{0:T(128)S(1)} %pad_add_fusion.1.s_ref, bf16[304,768]{1,0:T(8,128)(2,1)S(1)} %copy-done.56, bf16[304,768]{1,0:T(8,128)(2,1)S(1)} %copy-done.60, bf16[304,768]{1,0:T(8,128)(2,1)S(1)} %copy-done.62, ...), custom_call_target="tpu_custom_call", output_to_operand_aliasing={{0}: (9, {}), {1}: (10, {})} | custom-call | flops 91804925952 | bytes 224919552 | tf_op jit(solution)/shard_map/weight_grad/pallas_call | solution.py:475
  244.7 17.4 %attention_backward.1 = (bf16[576,768]{1,0:T(8,128)(2,1)S(1)}, bf16[576,2304]{1,0:T(8,128)(2,1)S(1)}) custom-call(s32[2]{0:T(128)S(1)} %pad_add_fusion.refs_0_.s_ref, f32[576,768]{1,0:T(8,128)S(1)} %copy-done.35, s32[1,576]{1,0:T(1,128)S(1)} %get-tuple-element.394.refs_2_, s32[576,1]{1,0:T(8,128)S(1)} %copy.36.refs_3_, bf16[576,2304]{1,0:T(8,128)(2,1)S(1)} %copy-done.39, ...), custom_call_target="tpu_custom_call" | custom-call | flops 92408905728 | bytes 146276352 | tf_op jit(solution)/shard_map/attention_backward/pallas_call | solution.py:135
  262.1 7.3 %attention_grad.1 = (bf16[4,384,768]{2,1,0:T(8,128)(2,1)S(1)}, bf16[4,384,768]{2,1,0:T(8,128)(2,1)S(1)}) custom-call(s32[2]{0:T(128)S(1)} %pad_add_fusion.refs_0_.s_ref, bf16[576,768]{1,0:T(8,128)(2,1)S(1)} %copy-done.5, bf16[576,768]{1,0:T(8,128)(2,1)S(1)} %copy-done.6, bf16[576,2304]{1,0:T(8,128)(2,1)S(1)} %get-tuple-element.323.dpacked.refs_4_, ...), custom_call_target="tpu_custom_call" | custom-call | flops 339738624 | bytes 442368 | tf_op jit(solution)/shard_map/attention_grad/pallas_call | solution.py:523
  270.9 7.1 %input_backward.1 = (f32[576,768]{1,0:T(8,128)S(1)}, f32[8,768]{1,0:T(8,128)S(1)}) custom-call(s32[2]{0:T(128)S(1)} %pad_add_fusion.refs_0_.s_ref, bf16[576,768]{1,0:T(8,128)(2,1)S(1)} %copy-done.4, f32[576,768]{1,0:T(8,128)S(1)} %copy-done.35, f32[8,768]{1,0:T(8,128)S(1)} %fusion.19.refs_4_.refs_1_.refs_3_, ...), custom_call_target="tpu_custom_call" | custom-call | flops 32614907904 | bytes 169869312 | tf_op jit(solution)/shard_map/input_backward/pallas_call | solution.py:135
  284.3 5.9 %add_convert_fusion = bf16[8,384,768]{2,1,0:T(8,128)(2,1)} fusion(bf16[8,384,768]{2,1,0:T(8,128)(2,1)} %collective-permute-done.32, bf16[8,384,768]{2,1,0:T(8,128)(2,1)S(1)} %get-tuple-element.328), kind=kLoop, calls=%fused_computation | loop fusion | flops 9437184 | bytes 14155776 | tf_op jit(solution)/shard_map/convert_element_type | solution.py:933
  290.2 6.0 %collective-permute-done.30 = bf16[384,768]{1,0:T(8,128)(2,1)S(1)} collective-permute-done((bf16[384,768]{1,0:T(8,128)(2,1)}, bf16[384,768]{1,0:T(8,128)(2,1)S(1)}, u32[]{:S(2)}, u32[]{:S(2)}) %collective-permute-start.30) | collective-permute-done | bytes 589856 | tf_op jit(solution)/shard_map/ppermute | solution.py:913
  312.3 6.8 %collective-permute-done.33 = bf16[2,96,768]{2,1,0:T(8,128)(2,1)S(1)} collective-permute-done((bf16[2,96,768]{2,1,0:T(8,128)(2,1)}, bf16[2,96,768]{2,1,0:T(8,128)(2,1)S(1)}, u32[]{:S(2)}, u32[]{:S(2)}) %collective-permute-start.33) | collective-permute-done | bytes 294944 | tf_op jit(solution)/shard_map/ppermute | solution.py:916
  319.0 10.4 %collective-permute-done.34 = bf16[2,96,768]{2,1,0:T(8,128)(2,1)S(1)} collective-permute-done((bf16[2,96,768]{2,1,0:T(8,128)(2,1)}, bf16[2,96,768]{2,1,0:T(8,128)(2,1)S(1)}, u32[]{:S(2)}, u32[]{:S(2)}) %collective-permute-start.34) | collective-permute-done | bytes 294944 | tf_op jit(solution)/shard_map/ppermute | solution.py:916
  352.9 9.9 %collective-permute-done.39 = bf16[2,96,768]{2,1,0:T(8,128)(2,1)} collective-permute-done((bf16[2,96,768]{2,1,0:T(8,128)(2,1)}, bf16[2,96,768]{2,1,0:T(8,128)(2,1)}, u32[]{:S(2)}, u32[]{:S(2)}) %collective-permute-start.39) | collective-permute-done | bytes 294944 | tf_op jit(solution)/shard_map/ppermute | solution.py:916
  371.3 6.8 %collective-permute-start.45 = (bf16[2,48,768]{2,1,0:T(8,128)(2,1)S(1)}, bf16[2,48,768]{2,1,0:T(8,128)(2,1)S(1)}, u32[]{:S(2)}, u32[]{:S(2)}) collective-permute-start(bf16[2,48,768]{2,1,0:T(8,128)(2,1)S(1)} %get-tuple-element.432), channel_id=1, source_target_pairs={{0,4},{1,5},{2,6},{3,7},{4,8},{5,9},{6,10},{7,11},{8,12},{9,13},{1... | collective-permute-start | bytes 442376 | tf_op jit(solution)/shard_map/ppermute | solution.py:916
  410.2 9.4 %collective-permute-done.49 = bf16[768,768]{1,0:T(8,128)(2,1)} collective-permute-done((bf16[768,768]{1,0:T(8,128)(2,1)S(1)}, bf16[768,768]{1,0:T(8,128)(2,1)}, u32[]{:S(2)}, u32[]{:S(2)}) %collective-permute-start.49) | collective-permute-done | bytes 1179680 | tf_op jit(solution)/shard_map/ppermute | solution.py:913
  426.0 5.4 %collective-permute-done.57 = f32[10,384]{1,0:T(8,128)} collective-permute-done((f32[10,384]{1,0:T(8,128)}, f32[10,384]{1,0:T(8,128)}, u32[]{:S(2)}, u32[]{:S(2)}) %collective-permute-start.57) | collective-permute-done | bytes 15392 | tf_op jit(solution)/shard_map/ppermute | solution.py:913
  (439 shorter events, 209.7 us)
Async XLA Ops:
  7.2 54.3 %all-gather.3.cloned.1.call-start = ((), (), s32[]{:S(2)}) async-start(), calls=%async_computation.1 | async-start | bytes 7077888 | tf_op jit(solution)/shard_map/all_gather | solution.py:961
  15.2 46.3 %all-gather.5.cloned.1.call-start = ((), (), s32[]{:S(2)}) async-start(), calls=%async_computation.2 | async-start | bytes 7077888 | tf_op jit(solution)/shard_map/all_gather | solution.py:961
  18.0 42.7 %collective-permute-start.5 = (bf16[2,384,768]{2,1,0:T(8,128)(2,1)S(1)}, bf16[2,384,768]{2,1,0:T(8,128)(2,1)}, u32[]{:S(2)}, u32[]{:S(2)}) collective-permute-start(bf16[2,384,768]{2,1,0:T(8,128)(2,1)S(1)} %pad_maximum_fusion.1.refs_3_), channel_id=1, source_target_pairs={{0,1},{1,0},{2,3},{3,2},{4,5},{5,4},{6,7},{7,6},{8,9},{9,8},{10,11... | collective-permute-start | bytes 3538952 | tf_op jit(solution)/shard_map/ppermute | solution.py:913
  20.6 40.1 %collective-permute-start.6 = (bf16[2,384,768]{2,1,0:T(8,128)(2,1)S(1)}, bf16[2,384,768]{2,1,0:T(8,128)(2,1)}, u32[]{:S(2)}, u32[]{:S(2)}) collective-permute-start(bf16[2,384,768]{2,1,0:T(8,128)(2,1)S(1)} %pad_maximum_fusion.1.refs_3_), channel_id=1, source_target_pairs={{0,2},{1,3},{2,0},{3,1},{4,6},{5,7},{6,4},{7,5},{8,10},{9,11},{10,... | collective-permute-start | bytes 3538952 | tf_op jit(solution)/shard_map/ppermute | solution.py:913
  22.1 38.6 %collective-permute-start.7 = (bf16[2,384,768]{2,1,0:T(8,128)(2,1)S(1)}, bf16[2,384,768]{2,1,0:T(8,128)(2,1)}, u32[]{:S(2)}, u32[]{:S(2)}) collective-permute-start(bf16[2,384,768]{2,1,0:T(8,128)(2,1)S(1)} %pad_maximum_fusion.1.refs_3_), channel_id=1, source_target_pairs={{0,16},{16,0},{1,17},{17,1},{2,18},{18,2},{3,19},{19,3},{4,20},{20... | collective-permute-start | bytes 3538952 | tf_op jit(solution)/shard_map/ppermute | solution.py:910
  25.3 30.4 %collective-permute-start.8 = (bf16[304,768]{1,0:T(8,128)(2,1)}, bf16[304,768]{1,0:T(8,128)(2,1)}, u32[]{:S(2)}, u32[]{:S(2)}) collective-permute-start(bf16[304,768]{1,0:T(8,128)(2,1)} %get-tuple-element.211), channel_id=1, source_target_pairs={{0,4},{1,5},{2,6},{3,7},{4,8},{5,9},{6,10},{7,11},{8,12},{9,13},{1... | collective-permute-start | bytes 1400840 | tf_op jit(solution)/shard_map/ppermute | solution.py:916
  26.9 33.8 %collective-permute-start.9 = (bf16[304,768]{1,0:T(8,128)(2,1)}, bf16[304,768]{1,0:T(8,128)(2,1)}, u32[]{:S(2)}, u32[]{:S(2)}) collective-permute-start(bf16[304,768]{1,0:T(8,128)(2,1)} %get-tuple-element.212), channel_id=1, source_target_pairs={{0,8},{1,9},{2,10},{3,11},{4,12},{5,13},{6,14},{7,15},{8,0},{9,1},... | collective-permute-start | bytes 1400840 | tf_op jit(solution)/shard_map/ppermute | solution.py:916
  29.5 414.8 %reduce-scatter.4.cloned.1.call-start = ((), (), s32[]{:S(2)}) async-start(), calls=%async_computation.3 | async-start | bytes 5898240
  55.7 31.7 %collective-permute-start.12 = (bf16[304,768]{1,0:T(8,128)(2,1)}, bf16[304,768]{1,0:T(8,128)(2,1)S(1)}, u32[]{:S(2)}, u32[]{:S(2)}) collective-permute-start(bf16[304,768]{1,0:T(8,128)(2,1)} %get-tuple-element.226), channel_id=1, source_target_pairs={{0,12},{1,13},{2,14},{3,15},{4,0},{5,1},{6,2},{7,3},{8,4},{9,5},{1... | collective-permute-start | bytes 1400840 | tf_op jit(solution)/shard_map/ppermute | solution.py:916
  60.7 27.4 %collective-permute-start.10 = (bf16[2,384,768]{2,1,0:T(8,128)(2,1)}, bf16[2,384,768]{2,1,0:T(8,128)(2,1)}, u32[]{:S(2)}, u32[]{:S(2)}) collective-permute-start(bf16[2,384,768]{2,1,0:T(8,128)(2,1)} %collective-permute-done.5.refs_4_), channel_id=1, source_target_pairs={{0,16},{16,0},{1,17},{17,1},{2,18},{18,2},{3,19},{19,3},{4,20},{20... | collective-permute-start | bytes 3538952 | tf_op jit(solution)/shard_map/ppermute | solution.py:910
  60.8 28.7 %collective-permute-start.13 = (bf16[2,384,768]{2,1,0:T(8,128)(2,1)}, bf16[2,384,768]{2,1,0:T(8,128)(2,1)}, u32[]{:S(2)}, u32[]{:S(2)}) collective-permute-start(bf16[2,384,768]{2,1,0:T(8,128)(2,1)} %collective-permute-done.5.refs_4_), channel_id=1, source_target_pairs={{0,2},{1,3},{2,0},{3,1},{4,6},{5,7},{6,4},{7,5},{8,10},{9,11},{10,... | collective-permute-start | bytes 3538952 | tf_op jit(solution)/shard_map/ppermute | solution.py:913
  91.1 38.0 %collective-permute-start.17 = (bf16[320,768]{1,0:T(8,128)(2,1)}, bf16[320,768]{1,0:T(8,128)(2,1)}, u32[]{:S(2)}, u32[]{:S(2)}) collective-permute-start(bf16[320,768]{1,0:T(8,128)(2,1)} %get-tuple-element.242), channel_id=1, source_target_pairs={{0,4},{1,5},{2,6},{3,7},{4,8},{5,9},{6,10},{7,11},{8,12},{9,13},{1... | collective-permute-start | bytes 1474568 | tf_op jit(solution)/shard_map/ppermute | solution.py:916
  91.8 55.4 %collective-permute-start.16 = (bf16[320,768]{1,0:T(8,128)(2,1)}, bf16[320,768]{1,0:T(8,128)(2,1)}, u32[]{:S(2)}, u32[]{:S(2)}) collective-permute-start(bf16[320,768]{1,0:T(8,128)(2,1)} %get-tuple-element.241), channel_id=1, source_target_pairs={{0,8},{1,9},{2,10},{3,11},{4,12},{5,13},{6,14},{7,15},{8,0},{9,1},... | collective-permute-start | bytes 1474568 | tf_op jit(solution)/shard_map/ppermute | solution.py:916
  210.3 33.3 %collective-permute-start.25 = (bf16[304,768]{1,0:T(8,128)(2,1)}, bf16[304,768]{1,0:T(8,128)(2,1)}, u32[]{:S(2)}, u32[]{:S(2)}) collective-permute-start(bf16[304,768]{1,0:T(8,128)(2,1)} %get-tuple-element.315), channel_id=1, source_target_pairs={{0,12},{1,13},{2,14},{3,15},{4,0},{5,1},{6,2},{7,3},{8,4},{9,5},{1... | collective-permute-start | bytes 1400840 | tf_op jit(solution)/shard_map/ppermute | solution.py:916
  212.4 57.0 %collective-permute-start.26 = (bf16[304,768]{1,0:T(8,128)(2,1)}, bf16[304,768]{1,0:T(8,128)(2,1)}, u32[]{:S(2)}, u32[]{:S(2)}) collective-permute-start(bf16[304,768]{1,0:T(8,128)(2,1)} %get-tuple-element.316), channel_id=1, source_target_pairs={{0,8},{1,9},{2,10},{3,11},{4,12},{5,13},{6,14},{7,15},{8,0},{9,1},... | collective-permute-start | bytes 1400840 | tf_op jit(solution)/shard_map/ppermute | solution.py:916
  212.4 57.0 %collective-permute-start.27 = (bf16[304,768]{1,0:T(8,128)(2,1)}, bf16[304,768]{1,0:T(8,128)(2,1)}, u32[]{:S(2)}, u32[]{:S(2)}) collective-permute-start(bf16[304,768]{1,0:T(8,128)(2,1)} %get-tuple-element.317), channel_id=1, source_target_pairs={{0,4},{1,5},{2,6},{3,7},{4,8},{5,9},{6,10},{7,11},{8,12},{9,13},{1... | collective-permute-start | bytes 1400840 | tf_op jit(solution)/shard_map/ppermute | solution.py:916
  242.6 28.0 %collective-permute-start.24 = (bf16[768,768]{1,0:T(8,128)(2,1)S(1)}, bf16[768,768]{1,0:T(8,128)(2,1)S(1)}, u32[]{:S(2)}, u32[]{:S(2)}) collective-permute-start(bf16[768,768]{1,0:T(8,128)(2,1)S(1)} %get-tuple-element.397), channel_id=1, source_target_pairs={{0,2},{1,3},{2,0},{3,1},{4,6},{5,7},{6,4},{7,5},{8,10},{9,11},{10,... | collective-permute-start | bytes 3538952 | tf_op jit(solution)/shard_map/ppermute | solution.py:913
  243.2 27.8 %collective-permute-start.23 = (bf16[768,768]{1,0:T(8,128)(2,1)S(1)}, bf16[768,768]{1,0:T(8,128)(2,1)S(1)}, u32[]{:S(2)}, u32[]{:S(2)}) collective-permute-start(bf16[768,768]{1,0:T(8,128)(2,1)S(1)} %get-tuple-element.399), channel_id=1, source_target_pairs={{0,1},{1,0},{2,3},{3,2},{4,5},{5,4},{6,7},{7,6},{8,9},{9,8},{10,11... | collective-permute-start | bytes 3538952 | tf_op jit(solution)/shard_map/ppermute | solution.py:913
  243.6 40.7 %collective-permute-start.32 = (bf16[8,384,768]{2,1,0:T(8,128)(2,1)S(1)}, bf16[8,384,768]{2,1,0:T(8,128)(2,1)}, u32[]{:S(2)}, u32[]{:S(2)}) collective-permute-start(bf16[8,384,768]{2,1,0:T(8,128)(2,1)S(1)} %get-tuple-element.329), channel_id=1, source_target_pairs={{0,16},{16,0},{1,17},{17,1},{2,18},{18,2},{3,19},{19,3},{4,20},{20... | collective-permute-start | bytes 14155784 | tf_op jit(solution)/shard_map/ppermute | solution.py:910
  301.6 27.9 %collective-permute-start.37 = (bf16[384,768]{1,0:T(8,128)(2,1)}, bf16[384,768]{1,0:T(8,128)(2,1)}, u32[]{:S(2)}, u32[]{:S(2)}) collective-permute-start(bf16[384,768]{1,0:T(8,128)(2,1)} %get-tuple-element.409), channel_id=1, source_target_pairs={{0,2},{1,3},{2,0},{3,1},{4,6},{5,7},{6,4},{7,5},{8,10},{9,11},{10,... | collective-permute-start | bytes 1769480 | tf_op jit(solution)/shard_map/ppermute | solution.py:913
  391.7 28.0 %collective-permute-start.49 = (bf16[768,768]{1,0:T(8,128)(2,1)S(1)}, bf16[768,768]{1,0:T(8,128)(2,1)}, u32[]{:S(2)}, u32[]{:S(2)}) collective-permute-start(bf16[768,768]{1,0:T(8,128)(2,1)S(1)} %maximum_select_fusion.2), channel_id=1, source_target_pairs={{0,2},{1,3},{2,0},{3,1},{4,6},{5,7},{6,4},{7,5},{8,10},{9,11},{10,... | collective-permute-start | bytes 3538952 | tf_op jit(solution)/shard_map/ppermute | solution.py:913
  393.7 27.7 %collective-permute-start.48 = (bf16[768,768]{1,0:T(8,128)(2,1)S(1)}, bf16[768,768]{1,0:T(8,128)(2,1)}, u32[]{:S(2)}, u32[]{:S(2)}) collective-permute-start(bf16[768,768]{1,0:T(8,128)(2,1)S(1)} %maximum_select_fusion.1), channel_id=1, source_target_pairs={{0,1},{1,0},{2,3},{3,2},{4,5},{5,4},{6,7},{7,6},{8,9},{9,8},{10,11... | collective-permute-start | bytes 3538952 | tf_op jit(solution)/shard_map/ppermute | solution.py:913
  406.1 38.1 %collective-permute-start.56 = (f32[576,384]{1,0:T(8,128)}, f32[576,384]{1,0:T(8,128)}, u32[]{:S(2)}, u32[]{:S(2)}) collective-permute-start(f32[576,384]{1,0:T(8,128)} %get-tuple-element.401), channel_id=1, source_target_pairs={{0,16},{16,0},{1,17},{17,1},{2,18},{18,2},{3,19},{19,3},{4,20},{20... | collective-permute-start | bytes 2654216 | tf_op jit(solution)/shard_map/ppermute | solution.py:910
  410.2 34.1 %collective-permute-start.55 = (bf16[576,384]{1,0:T(8,128)(2,1)}, bf16[576,384]{1,0:T(8,128)(2,1)}, u32[]{:S(2)}, u32[]{:S(2)}) collective-permute-start(bf16[576,384]{1,0:T(8,128)(2,1)} %get-tuple-element.421), channel_id=1, source_target_pairs={{0,16},{16,0},{1,17},{17,1},{2,18},{18,2},{3,19},{19,3},{4,20},{20... | collective-permute-start | bytes 1327112 | tf_op jit(solution)/shard_map/ppermute | solution.py:910
  (149 other events, 1296.4 us)
Sparse Core Ops, SparseCore 0:
  15.4 17.0 all-gather.2
  34.0 15.5 all-gather.4
  298.4 75.6 reduce-scatter.3
where the time goes:
time: 481 us; the launch traced here: 474 us
  Pallas kernels  189 us (39%)
  waiting for transfers between devices  95.1 us (20%)
  starting transfers between devices  76.7 us (16%)
  local copies, waits for them, and re-layouts  56.6 us (12%)
  other arithmetic  41.4 us (9%)
  between operations  15.5 us (3%)
    pallas_call x15, Pallas kernels, call(): return lambda *operands: made(*operands, *after)  145 us
    ppermute x27, waiting for transfers between devices, over_e(): lax.ppermute(v, 'dp', [(i, (i // GROUP + r) % experts * GROUP + i % GROUP...  60.8 us
    ppermute x27, starting transfers between devices, over_e(): lax.ppermute(v, 'dp', [(i, (i // GROUP + r) % experts * GROUP + i % GROUP...  49.3 us
    unnamed x210, local copies, waits for them, and re-layouts  38 us
    pallas_call x4, Pallas kernels, weight_grad(): pl.pallas_call(functools.partial(grad_kernel, n, len(into)), grid_spec=pl...  36.1 us
    ppermute x22, waiting for transfers between devices, over_q(): return lax.ppermute(v, 'dp', [(i, i ^ bit) for i in range(dp_count)])  33.3 us
    ppermute x22, starting transfers between devices, over_q(): return lax.ppermute(v, 'dp', [(i, i ^ bit) for i in range(dp_count)])  24.8 us
    convert_element_type x7, other arithmetic, add(): return (a.astype(F32) + b.astype(F32)).astype(BF)  15 us
  transfers between devices with their start and end apart: 68, of which 24 were waited for; matrix products, arithmetic and copies ran while one was open for 12% of the time, Pallas kernels for 36%

commit v1 on v0

--- a/solution.py
+++ b/solution.py
@@ -1084,13 +1084,17 @@
     grad_in = swapped(grad_in)
     tiny = tiny[0] + tiny[1]
 
-    ab = plane_move(plane_out(add(*a), add(*b)))
+    ab = plane_out(add(*a), add(*b))
+    keep, away, ab = tie((keep, away, ab))
+    ab = plane_move(ab)
     t = add(keep, away).reshape(-1, width)
     ta, tb = fold(t[:width], 1), fold(t[width:], 2)
     ab, ta, tb = tie((ab, ta, tb))
     block_out = merge(dense, place, home_outs, experts, cap)
 
-    ab = plane_move(plane_sum(ab))
+    ab = plane_sum(ab)
+    ta, tb, ab = tie((ta, tb, ab))
+    ab = plane_move(ab)
     ta, tb = fold(add(*ta), 2), fold(add(*tb), 1)
     ab, ta, tb, block_out = tie((ab, ta, tb, block_out))
 
@@ -1101,7 +1105,8 @@
     a, b = unfold(a, a_got, 2), unfold(b, b_got, 1)
     a_got, b_got = over_q(a, 1), over_q(b, 2)
     tab = plane_move(plane_sum(tab))
-    a_got, b_got, tab = tie((a_got, b_got, tab))
+    tiny_q = [over_q(tiny, bit) for bit in (1, 2, 3)]
+    a_got, b_got, tab, tiny_q = tie((a_got, b_got, tab, tiny_q))
 
     side_x, side_y = jnp.reshape(q % 2, (1,)), jnp.reshape(q // 2, (1,))
 
@@ -1111,20 +1116,20 @@
     ta, tb = plane_join(tab)
     ta_got, tb_got = over_q(ta, 2), over_q(tb, 1)
     block_out = swapped(block_out)
-    tiny_q = [over_q(tiny, bit) for bit in (1, 2, 3)]
+    tiny = tiny + tiny_q[0] + (tiny_q[1] + tiny_q[2])
+    if few:
+        tiny = [over_e(tiny, r) if r else tiny for r in range(experts)]
+    else:
+        tiny = [lax.psum(tiny, "dp", axis_index_groups=planes)]
     sum_fc2 = finish(side_x, blocks(a), blocks(a_got), False)
     sum_fc1 = finish(side_y, blocks(b), blocks(b_got), True)
-    ta_got, tb_got, block_out, grad_in, tiny_q, sum_fc2, sum_fc1, half_experts = tie(
-        (ta_got, tb_got, block_out, grad_in, tiny_q, sum_fc2, sum_fc1, half_experts)
+    ta_got, tb_got, tiny, sum_fc2, sum_fc1, half_experts = tie(
+        (ta_got, tb_got, tiny, sum_fc2, sum_fc1, half_experts)
     )
     half_up, half_down = half_experts[0].astype(F32), half_experts[1].astype(F32)
     ta, tb = unfold(ta, ta_got, 2), unfold(tb, tb_got, 1)
     ta_got, tb_got = over_q(ta, 1), over_q(tb, 2)
-    tiny = tiny + tiny_q[0] + (tiny_q[1] + tiny_q[2])
-    if few:
-        total = sum(over_e(tiny, r) if r else tiny for r in range(experts))
-    else:
-        total = lax.psum(tiny, "dp", axis_index_groups=planes)
+    total = sum(tiny)
     q_and_k = finish(side_x, blocks(ta), blocks(ta_got), True)
     first = q // 2 == 0
     v_sum, sum_attn = (

time: 481 us -> 481 us (level)
  waiting for transfers between devices: 95.1 us -> 105 us
  local copies, waits for them, and re-layouts: 56.6 us -> 48.3 us
  other arithmetic: 41.4 us -> 34.2 us
    ppermute x22, waiting for transfers between devices: 33.3 us -> 46.8 us  [over_q(): return lax.ppermute(v, 'dp', [(i, i ^ bit) for i in range(dp_count)])]
    unnamed x210 -> x202, local copies, waits for them, and re-layouts: 38 us -> 32.9 us
  transfers between devices with their start and end apart: 68 -> 68, of which waited for: 24 -> 23; matrix products, arithmetic and copies ran while one was open for 12% -> 10% of each run, Pallas kernels for 36% -> 33%
where the time goes in v1:
time: 481 us; the launch traced here: 475 us
  Pallas kernels  190 us (40%)
  waiting for transfers between devices  105 us (22%)
  starting transfers between devices  81.3 us (17%)
  local copies, waits for them, and re-layouts  48.3 us (10%)
  other arithmetic  34.2 us (7%)
  between operations  15.4 us (3%)
    pallas_call x15, Pallas kernels, call(): return lambda *operands: made(*operands, *after)  144 us
    ppermute x27, waiting for transfers between devices, over_e(): lax.ppermute(v, 'dp', [(i, (i // GROUP + r) % experts * GROUP + i % GROUP...  57.2 us
    ppermute x27, starting transfers between devices, over_e(): lax.ppermute(v, 'dp', [(i, (i // GROUP + r) % experts * GROUP + i % GROUP...  51.9 us
    ppermute x22, waiting for transfers between devices, over_q(): return lax.ppermute(v, 'dp', [(i, i ^ bit) for i in range(dp_count)])  46.8 us
    pallas_call x4, Pallas kernels, weight_grad(): pl.pallas_call(functools.partial(grad_kernel, n, len(into)), grid_spec=pl...  38.2 us
    unnamed x202, local copies, waits for them, and re-layouts  32.9 us
    ppermute x22, starting transfers between devices, over_q(): return lax.ppermute(v, 'dp', [(i, i ^ bit) for i in range(dp_count)])  26.8 us
    convert_element_type x7, other arithmetic, add(): return (a.astype(F32) + b.astype(F32)).astype(BF)  11.6 us
  transfers between devices with their start and end apart: 68, of which 23 were waited for; matrix products, arithmetic and copies ran while one was open for 10% of the time, Pallas kernels for 33%

profile of v1, /device:TPU:0, one launch (start us, length us, event | category | flops | bytes accessed | tf_op | source)
XLA Modules:
  0.0 474.8 jit_solution(4081701762647986356)
XLA Ops:
  33.3 21.3 %attention_forward.1 = (bf16[576,768]{1,0:T(8,128)(2,1)}, bf16[576,2304]{1,0:T(8,128)(2,1)}, bf16[576,768]{1,0:T(8,128)(2,1)}, f32[16,576]{1,0:T(8,128)S(1)}, f32[576,768]{1,0:T(8,128)S(1)}) custom-call(s32[2]{0:T(128)S(1)} %pad_add_fusion.refs_0_.s_ref, bf16[576,768]{1,0:T(8,128)(2,1)S(1)} %maximum_select_fusion.3.refs_1_, ...), custom_call_target="tpu_custom_call" | custom-call | flops 59793997824 | bytes 188743680 | tf_op jit(solution)/shard_map/attention_forward/pallas_call | solution.py:135
  67.8 18.9 %dense_forward.1 = (bf16[576,768]{1,0:T(8,128)(2,1)}, bf16[576,3072]{1,0:T(8,128)(2,1)}, bf16[576,3072]{1,0:T(8,128)(2,1)}, f32[576,768]{1,0:T(8,128)}, bf16[576...) custom-call(f32[576,768]{1,0:T(8,128)S(1)} %copy-done.39, ...), custom_call_target="tpu_custom_call" | custom-call | flops 104186511360 | bytes 349175808 | tf_op jit(solution)/shard_map/dense_forward/pallas_call | solution.py:135
  94.9 11.2 %expert.4 = (bf16[320,768]{1,0:T(8,128)(2,1)}, bf16[304,768]{1,0:T(8,128)(2,1)}, bf16[304,3072]{1,0:T(8,128)(2,1)S(1)}, bf16[304,3072]{1,0:T(8,128)(2,1)S(1)}, bf16[304,768]{1,0:T(8,128)(2,1)S(1)}) custom-call(s32[2]{0:T(128)S(1)} %pad_add_fusion.refs_0_.s_ref, bf16[320,768]{1,0:T(8,128)(2,1)S(1)} %copy-done.60, bf16[304,768]{1,0:T(8,128)(2,1)S(1)} %copy-done.36, ...), custom_call_target="tpu_custom_call" | custom-call | flops 91804925952 | bytes 248119296 | tf_op jit(solution)/shard_map/expert/pallas_call | solution.py:135
  108.1 7.7 %collective-permute-done.15.refs_1_.refs_3_ = bf16[320,768]{1,0:T(8,128)(2,1)S(1)} collective-permute-done((bf16[320,768]{1,0:T(8,128)(2,1)}, bf16[320,768]{1,0:T(8,128)(2,1)S(1)}, u32[]{:S(2)}, u32[]{:S(2)}) %collective-permute-start.15) | collective-permute-done | bytes 491552 | tf_op jit(solution)/shard_map/ppermute | solution.py:916
  115.8 11.3 %expert.5 = (bf16[320,768]{1,0:T(8,128)(2,1)}, bf16[304,768]{1,0:T(8,128)(2,1)}, bf16[304,3072]{1,0:T(8,128)(2,1)S(1)}, bf16[304,3072]{1,0:T(8,128)(2,1)S(1)}, bf16[304,768]{1,0:T(8,128)(2,1)S(1)}) custom-call(s32[2]{0:T(128)S(1)} %pad_add_fusion.refs_0_.s_ref, bf16[320,768]{1,0:T(8,128)(2,1)S(1)} %collective-permute-done.15.refs_1_.refs_3_, ...), custom_call_target="tpu_custom_call" | custom-call | flops 91804925952 | bytes 248119296 | tf_op jit(solution)/shard_map/expert/pallas_call | solution.py:135
  129.1 12.0 %expert.6 = (bf16[320,768]{1,0:T(8,128)(2,1)}, bf16[304,768]{1,0:T(8,128)(2,1)}, bf16[304,3072]{1,0:T(8,128)(2,1)S(1)}, bf16[304,3072]{1,0:T(8,128)(2,1)S(1)}, bf16[304,768]{1,0:T(8,128)(2,1)S(1)}) custom-call(s32[2]{0:T(128)S(1)} %pad_add_fusion.refs_0_.s_ref, bf16[320,768]{1,0:T(8,128)(2,1)} %collective-permute-done.17.refs_1_, ...), custom_call_target="tpu_custom_call" | custom-call | flops 91804925952 | bytes 248119296 | tf_op jit(solution)/shard_map/expert/pallas_call | solution.py:135
  146.2 12.5 %expert.7 = (bf16[320,768]{1,0:T(8,128)(2,1)}, bf16[304,768]{1,0:T(8,128)(2,1)}, bf16[304,3072]{1,0:T(8,128)(2,1)S(1)}, bf16[304,3072]{1,0:T(8,128)(2,1)S(1)}, bf16[304,768]{1,0:T(8,128)(2,1)S(1)}) custom-call(s32[2]{0:T(128)S(1)} %pad_add_fusion.refs_0_.s_ref, bf16[320,768]{1,0:T(8,128)(2,1)} %collective-permute-done.16.refs_1_.refs_2_, ...), custom_call_target="tpu_custom_call" | custom-call | flops 91804925952 | bytes 248119296 | tf_op jit(solution)/shard_map/expert/pallas_call | solution.py:135
  160.0 12.3 %weight_grad.6 = (bf16[8,384,768]{2,1,0:T(8,128)(2,1)}, bf16[8,384,768]{2,1,0:T(8,128)(2,1)S(1)}) custom-call(s32[2]{0:T(128)S(1)} %pad_add_fusion.1.s_ref, bf16[320,768]{1,0:T(8,128)(2,1)S(1)} %copy-done.61, bf16[320,768]{1,0:T(8,128)(2,1)} %collective-permute-done.17.refs_1_, bf16[320,768]{1,0:T(8,128)(2,1)} %collective-permute-done.16.refs_1_.refs_2_, ...), custom_call_target="tpu_custom_call" | custom-call | flops 91804925952 | bytes 224919552 | tf_op jit(solution)/shard_map/weight_grad/pallas_call | solution.py:475
  172.3 9.8 %collective-permute-done.20.refs_15_ = bf16[320,768]{1,0:T(8,128)(2,1)S(1)} collective-permute-done((bf16[320,768]{1,0:T(8,128)(2,1)}, bf16[320,768]{1,0:T(8,128)(2,1)S(1)}, u32[]{:S(2)}, u32[]{:S(2)}) %collective-permute-start.20) | collective-permute-done | bytes 491552 | tf_op jit(solution)/shard_map/ppermute | solution.py:916
  183.6 18.4 %dense_backward.1 = (bf16[576,768]{1,0:T(8,128)(2,1)S(1)}, bf16[576,3072]{1,0:T(8,128)(2,1)S(1)}, f32[576,768]{1,0:T(8,128)S(1)}, f32[8,768]{1,0:T(8,128)S(1)}, f32[16,768]{1,0:T(8,128)S(1)}) custom-call(bf16[576,768]{1,0:T(8,128)(2,1)S(1)} %maximum_select_fusion.4.refs_0_, f32[576,768]{1,0:T(8,128)S(1)} %copy-done, f32[576,768]{1,0:T(8,128)S(1)} %copy-done.40, ...), custom_call_target="tpu_custom_call" | custom-call | flops 104186511360 | bytes 391643136 | tf_op jit(solution)/shard_map/dense_backward/pallas_call | solution.py:135
  202.0 7.0 %weight_grad.5 = (bf16[4,384,768]{2,1,0:T(8,128)(2,1)S(1)}, bf16[4,384,768]{2,1,0:T(8,128)(2,1)S(1)}) custom-call(s32[2]{0:T(128)S(1)} %pad_add_fusion.refs_0_.s_ref, bf16[576,3072]{1,0:T(8,128)(2,1)S(1)} %copy-done.29, bf16[576,768]{1,0:T(8,128)(2,1)S(1)} %get-tuple-element.290.refs_1_.refs_4_), custom_call_target="tpu_custom_call" | custom-call | flops 43486543872 | bytes 146276352 | tf_op jit(solution)/shard_map/weight_grad/pallas_call | solution.py:475
  211.1 7.2 %weight_grad.4 = (bf16[4,384,768]{2,1,0:T(8,128)(2,1)S(1)}, bf16[4,384,768]{2,1,0:T(8,128)(2,1)S(1)}) custom-call(s32[2]{0:T(128)S(1)} %pad_add_fusion.refs_0_.s_ref, bf16[576,768]{1,0:T(8,128)(2,1)S(1)} %copy-done.41, bf16[576,3072]{1,0:T(8,128)(2,1)S(1)} %copy-done.31), custom_call_target="tpu_custom_call" | custom-call | flops 43486543872 | bytes 146276352 | tf_op jit(solution)/shard_map/weight_grad/pallas_call | solution.py:475
  223.7 11.8 %weight_grad.7 = (bf16[8,384,768]{2,1,0:T(8,128)(2,1)}, bf16[8,384,768]{2,1,0:T(8,128)(2,1)S(1)}) custom-call(s32[2]{0:T(128)S(1)} %copy-done.28, bf16[304,768]{1,0:T(8,128)(2,1)S(1)} %copy-done.52, bf16[304,768]{1,0:T(8,128)(2,1)S(1)} %copy-done.56, bf16[304,768]{1,0:T(8,128)(2,1)S(1)} %copy-done.58, ...), custom_call_target="tpu_custom_call", output_to_operand_aliasing={{0}: (9, {}), {1}: (10, {})} | custom-call | flops 91804925952 | bytes 224919552 | tf_op jit(solution)/shard_map/weight_grad/pallas_call | solution.py:475
  241.0 17.3 %attention_backward.1 = (bf16[576,768]{1,0:T(8,128)(2,1)S(1)}, bf16[576,2304]{1,0:T(8,128)(2,1)S(1)}) custom-call(s32[2]{0:T(128)S(1)} %pad_add_fusion.refs_0_.s_ref, f32[576,768]{1,0:T(8,128)S(1)} %copy-done.33, s32[1,576]{1,0:T(1,128)S(1)} %get-tuple-element.422.refs_2_, s32[576,1]{1,0:T(8,128)S(1)} %copy.36.refs_3_, bf16[576,2304]{1,0:T(8,128)(2,1)S(1)} %copy-done.37, ...), custom_call_target="tpu_custom_call" | custom-call | flops 92408905728 | bytes 146276352 | tf_op jit(solution)/shard_map/attention_backward/pallas_call | solution.py:135
  258.3 7.3 %attention_grad.1 = (bf16[4,384,768]{2,1,0:T(8,128)(2,1)S(1)}, bf16[4,384,768]{2,1,0:T(8,128)(2,1)S(1)}) custom-call(s32[2]{0:T(128)S(1)} %pad_add_fusion.refs_0_.s_ref, bf16[576,768]{1,0:T(8,128)(2,1)S(1)} %copy-done.6, bf16[576,768]{1,0:T(8,128)(2,1)S(1)} %copy-done.7, bf16[576,2304]{1,0:T(8,128)(2,1)S(1)} %get-tuple-element.338.dpacked.refs_4_, ...), custom_call_target="tpu_custom_call" | custom-call | flops 339738624 | bytes 442368 | tf_op jit(solution)/shard_map/attention_grad/pallas_call | solution.py:523
  267.6 7.0 %input_backward.1 = (f32[576,768]{1,0:T(8,128)S(1)}, f32[8,768]{1,0:T(8,128)S(1)}) custom-call(s32[2]{0:T(128)S(1)} %pad_add_fusion.refs_0_.s_ref, bf16[576,768]{1,0:T(8,128)(2,1)S(1)} %copy-done.5, f32[576,768]{1,0:T(8,128)S(1)} %copy-done.33, f32[8,768]{1,0:T(8,128)S(1)} %fusion.19.refs_4_.refs_1_.refs_3_, ...), custom_call_target="tpu_custom_call" | custom-call | flops 32614907904 | bytes 169869312 | tf_op jit(solution)/shard_map/input_backward/pallas_call | solution.py:135
  280.0 5.9 %add_convert_fusion = bf16[8,384,768]{2,1,0:T(8,128)(2,1)} fusion(bf16[8,384,768]{2,1,0:T(8,128)(2,1)} %collective-permute-done.32, bf16[8,384,768]{2,1,0:T(8,128)(2,1)S(1)} %get-tuple-element.343), kind=kLoop, calls=%fused_computation | loop fusion | flops 9437184 | bytes 14155776 | tf_op jit(solution)/shard_map/convert_element_type | solution.py:933
  285.8 5.9 %collective-permute-done.30 = bf16[384,768]{1,0:T(8,128)(2,1)} collective-permute-done((bf16[384,768]{1,0:T(8,128)(2,1)S(1)}, bf16[384,768]{1,0:T(8,128)(2,1)}, u32[]{:S(2)}, u32[]{:S(2)}) %collective-permute-start.30) | collective-permute-done | bytes 589856 | tf_op jit(solution)/shard_map/ppermute | solution.py:913
  309.0 6.8 %collective-permute-done.33 = bf16[2,96,768]{2,1,0:T(8,128)(2,1)} collective-permute-done((bf16[2,96,768]{2,1,0:T(8,128)(2,1)}, bf16[2,96,768]{2,1,0:T(8,128)(2,1)}, u32[]{:S(2)}, u32[]{:S(2)}) %collective-permute-start.33) | collective-permute-done | bytes 294944 | tf_op jit(solution)/shard_map/ppermute | solution.py:916
  315.8 10.4 %collective-permute-done.34 = bf16[2,96,768]{2,1,0:T(8,128)(2,1)} collective-permute-done((bf16[2,96,768]{2,1,0:T(8,128)(2,1)}, bf16[2,96,768]{2,1,0:T(8,128)(2,1)}, u32[]{:S(2)}, u32[]{:S(2)}) %collective-permute-start.34) | collective-permute-done | bytes 294944 | tf_op jit(solution)/shard_map/ppermute | solution.py:916
  349.0 9.6 %collective-permute-done.39 = bf16[2,96,768]{2,1,0:T(8,128)(2,1)} collective-permute-done((bf16[2,96,768]{2,1,0:T(8,128)(2,1)}, bf16[2,96,768]{2,1,0:T(8,128)(2,1)}, u32[]{:S(2)}, u32[]{:S(2)}) %collective-permute-start.39) | collective-permute-done | bytes 294944 | tf_op jit(solution)/shard_map/ppermute | solution.py:916
  368.0 6.8 %collective-permute-start.47 = (bf16[2,48,768]{2,1,0:T(8,128)(2,1)S(1)}, bf16[2,48,768]{2,1,0:T(8,128)(2,1)S(1)}, u32[]{:S(2)}, u32[]{:S(2)}) collective-permute-start(bf16[2,48,768]{2,1,0:T(8,128)(2,1)S(1)} %get-tuple-element.460), channel_id=1, source_target_pairs={{0,4},{1,5},{2,6},{3,7},{4,8},{5,9},{6,10},{7,11},{8,12},{9,13},{1... | collective-permute-start | bytes 442376 | tf_op jit(solution)/shard_map/ppermute | solution.py:916
  392.7 23.4 %collective-permute-done.55 = f32[10,384]{1,0:T(8,128)S(1)} collective-permute-done((f32[10,384]{1,0:T(8,128)S(1)}, f32[10,384]{1,0:T(8,128)S(1)}, u32[]{:S(2)}, u32[]{:S(2)}) %collective-permute-start.55) | collective-permute-done | bytes 15392 | tf_op jit(solution)/shard_map/ppermute | solution.py:913
  455.7 7.7 %collective-permute-done.63 = bf16[384,768]{1,0:T(8,128)(2,1)S(1)} collective-permute-done((bf16[384,768]{1,0:T(8,128)(2,1)S(1)}, bf16[384,768]{1,0:T(8,128)(2,1)S(1)}, u32[]{:S(2)}, u32[]{:S(2)}) %collective-permute-start.63) | collective-permute-done | bytes 589856 | tf_op jit(solution)/shard_map/ppermute | solution.py:913
  (430 shorter events, 190.0 us)
Async XLA Ops:
  7.2 54.5 %all-gather.3.cloned.1.call-start = ((), (), s32[]{:S(2)}) async-start(), calls=%async_computation.1 | async-start | bytes 7077888 | tf_op jit(solution)/shard_map/all_gather | solution.py:961
  15.1 46.6 %all-gather.5.cloned.1.call-start = ((), (), s32[]{:S(2)}) async-start(), calls=%async_computation.2 | async-start | bytes 7077888 | tf_op jit(solution)/shard_map/all_gather | solution.py:961
  18.1 42.7 %collective-permute-start.5 = (bf16[2,384,768]{2,1,0:T(8,128)(2,1)S(1)}, bf16[2,384,768]{2,1,0:T(8,128)(2,1)}, u32[]{:S(2)}, u32[]{:S(2)}) collective-permute-start(bf16[2,384,768]{2,1,0:T(8,128)(2,1)S(1)} %pad_maximum_fusion.1.refs_3_), channel_id=1, source_target_pairs={{0,1},{1,0},{2,3},{3,2},{4,5},{5,4},{6,7},{7,6},{8,9},{9,8},{10,11... | collective-permute-start | bytes 3538952 | tf_op jit(solution)/shard_map/ppermute | solution.py:913
  20.7 40.1 %collective-permute-start.6 = (bf16[2,384,768]{2,1,0:T(8,128)(2,1)S(1)}, bf16[2,384,768]{2,1,0:T(8,128)(2,1)}, u32[]{:S(2)}, u32[]{:S(2)}) collective-permute-start(bf16[2,384,768]{2,1,0:T(8,128)(2,1)S(1)} %pad_maximum_fusion.1.refs_3_), channel_id=1, source_target_pairs={{0,2},{1,3},{2,0},{3,1},{4,6},{5,7},{6,4},{7,5},{8,10},{9,11},{10,... | collective-permute-start | bytes 3538952 | tf_op jit(solution)/shard_map/ppermute | solution.py:913
  22.3 38.6 %collective-permute-start.7 = (bf16[2,384,768]{2,1,0:T(8,128)(2,1)S(1)}, bf16[2,384,768]{2,1,0:T(8,128)(2,1)}, u32[]{:S(2)}, u32[]{:S(2)}) collective-permute-start(bf16[2,384,768]{2,1,0:T(8,128)(2,1)S(1)} %pad_maximum_fusion.1.refs_3_), channel_id=1, source_target_pairs={{0,16},{16,0},{1,17},{17,1},{2,18},{18,2},{3,19},{19,3},{4,20},{20... | collective-permute-start | bytes 3538952 | tf_op jit(solution)/shard_map/ppermute | solution.py:910
  25.4 30.4 %collective-permute-start.8 = (bf16[304,768]{1,0:T(8,128)(2,1)}, bf16[304,768]{1,0:T(8,128)(2,1)}, u32[]{:S(2)}, u32[]{:S(2)}) collective-permute-start(bf16[304,768]{1,0:T(8,128)(2,1)} %get-tuple-element.225), channel_id=1, source_target_pairs={{0,4},{1,5},{2,6},{3,7},{4,8},{5,9},{6,10},{7,11},{8,12},{9,13},{1... | collective-permute-start | bytes 1400840 | tf_op jit(solution)/shard_map/ppermute | solution.py:916
  27.0 33.8 %collective-permute-start.9 = (bf16[304,768]{1,0:T(8,128)(2,1)}, bf16[304,768]{1,0:T(8,128)(2,1)}, u32[]{:S(2)}, u32[]{:S(2)}) collective-permute-start(bf16[304,768]{1,0:T(8,128)(2,1)} %get-tuple-element.226), channel_id=1, source_target_pairs={{0,8},{1,9},{2,10},{3,11},{4,12},{5,13},{6,14},{7,15},{8,0},{9,1},... | collective-permute-start | bytes 1400840 | tf_op jit(solution)/shard_map/ppermute | solution.py:916
  29.6 419.3 %reduce-scatter.4.cloned.1.call-start = ((), (), s32[]{:S(2)}) async-start(), calls=%async_computation.3 | async-start | bytes 5898240
  55.8 31.7 %collective-permute-start.12 = (bf16[304,768]{1,0:T(8,128)(2,1)}, bf16[304,768]{1,0:T(8,128)(2,1)S(1)}, u32[]{:S(2)}, u32[]{:S(2)}) collective-permute-start(bf16[304,768]{1,0:T(8,128)(2,1)} %get-tuple-element.240), channel_id=1, source_target_pairs={{0,12},{1,13},{2,14},{3,15},{4,0},{5,1},{6,2},{7,3},{8,4},{9,5},{1... | collective-permute-start | bytes 1400840 | tf_op jit(solution)/shard_map/ppermute | solution.py:916
  60.9 27.4 %collective-permute-start.10 = (bf16[2,384,768]{2,1,0:T(8,128)(2,1)}, bf16[2,384,768]{2,1,0:T(8,128)(2,1)}, u32[]{:S(2)}, u32[]{:S(2)}) collective-permute-start(bf16[2,384,768]{2,1,0:T(8,128)(2,1)} %collective-permute-done.5.refs_4_), channel_id=1, source_target_pairs={{0,16},{16,0},{1,17},{17,1},{2,18},{18,2},{3,19},{19,3},{4,20},{20... | collective-permute-start | bytes 3538952 | tf_op jit(solution)/shard_map/ppermute | solution.py:910
  60.9 28.7 %collective-permute-start.13 = (bf16[2,384,768]{2,1,0:T(8,128)(2,1)}, bf16[2,384,768]{2,1,0:T(8,128)(2,1)}, u32[]{:S(2)}, u32[]{:S(2)}) collective-permute-start(bf16[2,384,768]{2,1,0:T(8,128)(2,1)} %collective-permute-done.5.refs_4_), channel_id=1, source_target_pairs={{0,2},{1,3},{2,0},{3,1},{4,6},{5,7},{6,4},{7,5},{8,10},{9,11},{10,... | collective-permute-start | bytes 3538952 | tf_op jit(solution)/shard_map/ppermute | solution.py:913
  91.2 37.9 %collective-permute-start.17 = (bf16[320,768]{1,0:T(8,128)(2,1)}, bf16[320,768]{1,0:T(8,128)(2,1)}, u32[]{:S(2)}, u32[]{:S(2)}) collective-permute-start(bf16[320,768]{1,0:T(8,128)(2,1)} %get-tuple-element.256), channel_id=1, source_target_pairs={{0,4},{1,5},{2,6},{3,7},{4,8},{5,9},{6,10},{7,11},{8,12},{9,13},{1... | collective-permute-start | bytes 1474568 | tf_op jit(solution)/shard_map/ppermute | solution.py:916
  91.9 54.2 %collective-permute-start.16 = (bf16[320,768]{1,0:T(8,128)(2,1)}, bf16[320,768]{1,0:T(8,128)(2,1)}, u32[]{:S(2)}, u32[]{:S(2)}) collective-permute-start(bf16[320,768]{1,0:T(8,128)(2,1)} %get-tuple-element.255), channel_id=1, source_target_pairs={{0,8},{1,9},{2,10},{3,11},{4,12},{5,13},{6,14},{7,15},{8,0},{9,1},... | collective-permute-start | bytes 1474568 | tf_op jit(solution)/shard_map/ppermute | solution.py:916
  223.0 42.6 %collective-permute-start.26 = (bf16[304,768]{1,0:T(8,128)(2,1)}, bf16[304,768]{1,0:T(8,128)(2,1)}, u32[]{:S(2)}, u32[]{:S(2)}) collective-permute-start(bf16[304,768]{1,0:T(8,128)(2,1)} %get-tuple-element.330), channel_id=1, source_target_pairs={{0,8},{1,9},{2,10},{3,11},{4,12},{5,13},{6,14},{7,15},{8,0},{9,1},... | collective-permute-start | bytes 1400840 | tf_op jit(solution)/shard_map/ppermute | solution.py:916
  223.0 42.6 %collective-permute-start.27 = (bf16[304,768]{1,0:T(8,128)(2,1)}, bf16[304,768]{1,0:T(8,128)(2,1)}, u32[]{:S(2)}, u32[]{:S(2)}) collective-permute-start(bf16[304,768]{1,0:T(8,128)(2,1)} %get-tuple-element.331), channel_id=1, source_target_pairs={{0,4},{1,5},{2,6},{3,7},{4,8},{5,9},{6,10},{7,11},{8,12},{9,13},{1... | collective-permute-start | bytes 1400840 | tf_op jit(solution)/shard_map/ppermute | solution.py:916
  235.5 44.5 %collective-permute-start.32 = (bf16[8,384,768]{2,1,0:T(8,128)(2,1)}, bf16[8,384,768]{2,1,0:T(8,128)(2,1)}, u32[]{:S(2)}, u32[]{:S(2)}) collective-permute-start(bf16[8,384,768]{2,1,0:T(8,128)(2,1)} %get-tuple-element.344), channel_id=1, source_target_pairs={{0,16},{16,0},{1,17},{17,1},{2,18},{18,2},{3,19},{19,3},{4,20},{20... | collective-permute-start | bytes 14155784 | tf_op jit(solution)/shard_map/ppermute | solution.py:910
  238.9 28.4 %collective-permute-start.24 = (bf16[768,768]{1,0:T(8,128)(2,1)S(1)}, bf16[768,768]{1,0:T(8,128)(2,1)S(1)}, u32[]{:S(2)}, u32[]{:S(2)}) collective-permute-start(bf16[768,768]{1,0:T(8,128)(2,1)S(1)} %get-tuple-element.425), channel_id=1, source_target_pairs={{0,2},{1,3},{2,0},{3,1},{4,6},{5,7},{6,4},{7,5},{8,10},{9,11},{10,... | collective-permute-start | bytes 3538952 | tf_op jit(solution)/shard_map/ppermute | solution.py:913
  239.3 28.3 %collective-permute-start.23 = (bf16[768,768]{1,0:T(8,128)(2,1)S(1)}, bf16[768,768]{1,0:T(8,128)(2,1)S(1)}, u32[]{:S(2)}, u32[]{:S(2)}) collective-permute-start(bf16[768,768]{1,0:T(8,128)(2,1)S(1)} %get-tuple-element.427), channel_id=1, source_target_pairs={{0,1},{1,0},{2,3},{3,2},{4,5},{5,4},{6,7},{7,6},{8,9},{9,8},{10,11... | collective-permute-start | bytes 3538952 | tf_op jit(solution)/shard_map/ppermute | solution.py:913
  299.1 27.1 %collective-permute-start.37 = (bf16[384,768]{1,0:T(8,128)(2,1)S(1)}, bf16[384,768]{1,0:T(8,128)(2,1)S(1)}, u32[]{:S(2)}, u32[]{:S(2)}) collective-permute-start(bf16[384,768]{1,0:T(8,128)(2,1)S(1)} %get-tuple-element.437), channel_id=1, source_target_pairs={{0,2},{1,3},{2,0},{3,1},{4,6},{5,7},{6,4},{7,5},{8,10},{9,11},{10,... | collective-permute-start | bytes 1769480 | tf_op jit(solution)/shard_map/ppermute | solution.py:913
  301.8 27.2 %collective-permute-start.36 = (bf16[384,768]{1,0:T(8,128)(2,1)S(1)}, bf16[384,768]{1,0:T(8,128)(2,1)S(1)}, u32[]{:S(2)}, u32[]{:S(2)}) collective-permute-start(bf16[384,768]{1,0:T(8,128)(2,1)S(1)} %get-tuple-element.439), channel_id=1, source_target_pairs={{0,1},{1,0},{2,3},{3,2},{4,5},{5,4},{6,7},{7,6},{8,9},{9,8},{10,11... | collective-permute-start | bytes 1769480 | tf_op jit(solution)/shard_map/ppermute | solution.py:913
  382.0 41.5 %collective-permute-start.44 = (f32[576,384]{1,0:T(8,128)}, f32[576,384]{1,0:T(8,128)}, u32[]{:S(2)}, u32[]{:S(2)}) collective-permute-start(f32[576,384]{1,0:T(8,128)} %get-tuple-element.430), channel_id=1, source_target_pairs={{0,16},{16,0},{1,17},{17,1},{2,18},{18,2},{3,19},{19,3},{4,20},{20... | collective-permute-start | bytes 2654216 | tf_op jit(solution)/shard_map/ppermute | solution.py:910
  387.1 44.5 %collective-permute-start.51 = (bf16[768,768]{1,0:T(8,128)(2,1)S(1)}, bf16[768,768]{1,0:T(8,128)(2,1)}, u32[]{:S(2)}, u32[]{:S(2)}) collective-permute-start(bf16[768,768]{1,0:T(8,128)(2,1)S(1)} %maximum_select_fusion.2), channel_id=1, source_target_pairs={{0,2},{1,3},{2,0},{3,1},{4,6},{5,7},{6,4},{7,5},{8,10},{9,11},{10,... | collective-permute-start | bytes 3538952 | tf_op jit(solution)/shard_map/ppermute | solution.py:913
  388.0 43.6 %collective-permute-start.50 = (bf16[768,768]{1,0:T(8,128)(2,1)S(1)}, bf16[768,768]{1,0:T(8,128)(2,1)}, u32[]{:S(2)}, u32[]{:S(2)}) collective-permute-start(bf16[768,768]{1,0:T(8,128)(2,1)S(1)} %maximum_select_fusion.1), channel_id=1, source_target_pairs={{0,1},{1,0},{2,3},{3,2},{4,5},{5,4},{6,7},{7,6},{8,9},{9,8},{10,11... | collective-permute-start | bytes 3538952 | tf_op jit(solution)/shard_map/ppermute | solution.py:913
  390.9 26.8 %collective-permute-start.56 = (f32[10,384]{1,0:T(8,128)S(1)}, f32[10,384]{1,0:T(8,128)S(1)}, u32[]{:S(2)}, u32[]{:S(2)}) collective-permute-start(f32[10,384]{1,0:T(8,128)S(1)} %add.354), channel_id=1, source_target_pairs={{0,2},{1,3},{2,0},{3,1},{4,6},{5,7},{6,4},{7,5},{8,10},{9,11},{10,... | collective-permute-start | bytes 46088 | tf_op jit(solution)/shard_map/ppermute | solution.py:913
  (145 other events, 1385.5 us)
Sparse Core Ops, SparseCore 0:
  15.2 17.0 all-gather.2
  33.8 15.6 all-gather.4
  294.8 78.9 reduce-scatter.3

commit v2 on v1

--- a/solution.py
+++ b/solution.py
@@ -1096,17 +1096,19 @@
     ta, tb, ab = tie((ta, tb, ab))
     ab = plane_move(ab)
     ta, tb = fold(add(*ta), 2), fold(add(*tb), 1)
-    ab, ta, tb, block_out = tie((ab, ta, tb, block_out))
+    tiny_x = over_q(tiny, 1)
+    ab, ta, tb, block_out, tiny_x = tie((ab, ta, tb, block_out, tiny_x))
+    tiny = tiny + tiny_x
+    tiny_y = over_q(tiny, 2)
 
     a, b = plane_join(ab)
     a_got, b_got = over_q(a, 2), over_q(b, 1)
     tab = plane_move(plane_out(add(*ta), add(*tb)))
-    a_got, b_got, tab = tie((a_got, b_got, tab))
+    a_got, b_got, tab, tiny_y = tie((a_got, b_got, tab, tiny_y))
     a, b = unfold(a, a_got, 2), unfold(b, b_got, 1)
     a_got, b_got = over_q(a, 1), over_q(b, 2)
     tab = plane_move(plane_sum(tab))
-    tiny_q = [over_q(tiny, bit) for bit in (1, 2, 3)]
-    a_got, b_got, tab, tiny_q = tie((a_got, b_got, tab, tiny_q))
+    a_got, b_got, tab = tie((a_got, b_got, tab))
 
     side_x, side_y = jnp.reshape(q % 2, (1,)), jnp.reshape(q // 2, (1,))
 
@@ -1116,7 +1118,7 @@
     ta, tb = plane_join(tab)
     ta_got, tb_got = over_q(ta, 2), over_q(tb, 1)
     block_out = swapped(block_out)
-    tiny = tiny + tiny_q[0] + (tiny_q[1] + tiny_q[2])
+    tiny = tiny + tiny_y
     if few:
         tiny = [over_e(tiny, r) if r else tiny for r in range(experts)]
     else:

time: 481 us -> 474 us (0.985)
  waiting for transfers between devices: 105 us -> 98.1 us
    ppermute x22 -> x21, waiting for transfers between devices: 46.8 us -> 34.6 us  [over_q(): return lax.ppermute(v, 'dp', [(i, i ^ bit) for i in range(dp_count)])]
    ppermute x27, waiting for transfers between devices: 57.2 us -> 62.1 us  [over_e(): lax.ppermute(v, 'dp', [(i, (i // GROUP + r) % experts * GROUP + i % GROUP...]
    ppermute x22 -> x21, starting transfers between devices: 26.8 us -> 23.7 us  [over_q(): return lax.ppermute(v, 'dp', [(i, i ^ bit) for i in range(dp_count)])]
    unnamed x202 -> x216, local copies, waits for them, and re-layouts: 32.9 us -> 33.5 us
  transfers between devices with their start and end apart: 68 -> 67, of which waited for: 23 -> 27; matrix products, arithmetic and copies ran while one was open for 10% -> 11% of each run, Pallas kernels for 33% -> 34%
where the time goes in v2:
time: 474 us; the launch traced here: 467 us
  Pallas kernels  190 us (40%)
  waiting for transfers between devices  98.1 us (21%)
  starting transfers between devices  77.1 us (16%)
  local copies, waits for them, and re-layouts  50.1 us (11%)
  other arithmetic  35.8 us (8%)
  between operations  15.5 us (3%)
    pallas_call x15, Pallas kernels, call(): return lambda *operands: made(*operands, *after)  144 us
    ppermute x27, waiting for transfers between devices, over_e(): lax.ppermute(v, 'dp', [(i, (i // GROUP + r) % experts * GROUP + i % GROUP...  62.1 us
    ppermute x27, starting transfers between devices, over_e(): lax.ppermute(v, 'dp', [(i, (i // GROUP + r) % experts * GROUP + i % GROUP...  50.7 us
    pallas_call x4, Pallas kernels, weight_grad(): pl.pallas_call(functools.partial(grad_kernel, n, len(into)), grid_spec=pl...  38.2 us
    ppermute x21, waiting for transfers between devices, over_q(): return lax.ppermute(v, 'dp', [(i, i ^ bit) for i in range(dp_count)])  34.6 us
    unnamed x216, local copies, waits for them, and re-layouts  33.5 us
    ppermute x21, starting transfers between devices, over_q(): return lax.ppermute(v, 'dp', [(i, i ^ bit) for i in range(dp_count)])  23.7 us
    convert_element_type x7, other arithmetic, add(): return (a.astype(F32) + b.astype(F32)).astype(BF)  11.6 us
  transfers between devices with their start and end apart: 67, of which 27 were waited for; matrix products, arithmetic and copies ran while one was open for 11% of the time, Pallas kernels for 34%

profile of v2, /device:TPU:0, one launch (start us, length us, event | category | flops | bytes accessed | tf_op | source)
XLA Modules:
  0.0 466.9 jit_solution(8999321310441189515)
XLA Ops:
  33.3 21.3 %attention_forward.1 = (bf16[576,768]{1,0:T(8,128)(2,1)}, bf16[576,2304]{1,0:T(8,128)(2,1)}, bf16[576,768]{1,0:T(8,128)(2,1)}, f32[16,576]{1,0:T(8,128)S(1)}, f32[576,768]{1,0:T(8,128)S(1)}) custom-call(s32[2]{0:T(128)S(1)} %pad_add_fusion.refs_0_.s_ref, bf16[576,768]{1,0:T(8,128)(2,1)S(1)} %maximum_select_fusion.3.refs_1_, ...), custom_call_target="tpu_custom_call" | custom-call | flops 59793997824 | bytes 188743680 | tf_op jit(solution)/shard_map/attention_forward/pallas_call | solution.py:135
  67.9 18.9 %dense_forward.1 = (bf16[576,768]{1,0:T(8,128)(2,1)}, bf16[576,3072]{1,0:T(8,128)(2,1)}, bf16[576,3072]{1,0:T(8,128)(2,1)}, f32[576,768]{1,0:T(8,128)}, bf16[576...) custom-call(f32[576,768]{1,0:T(8,128)S(1)} %copy-done.39, ...), custom_call_target="tpu_custom_call" | custom-call | flops 104186511360 | bytes 349175808 | tf_op jit(solution)/shard_map/dense_forward/pallas_call | solution.py:135
  95.0 11.2 %expert.4 = (bf16[320,768]{1,0:T(8,128)(2,1)}, bf16[304,768]{1,0:T(8,128)(2,1)}, bf16[304,3072]{1,0:T(8,128)(2,1)S(1)}, bf16[304,3072]{1,0:T(8,128)(2,1)S(1)}, bf16[304,768]{1,0:T(8,128)(2,1)S(1)}) custom-call(s32[2]{0:T(128)S(1)} %pad_add_fusion.refs_0_.s_ref, bf16[320,768]{1,0:T(8,128)(2,1)S(1)} %copy-done.60, bf16[304,768]{1,0:T(8,128)(2,1)S(1)} %copy-done.36, ...), custom_call_target="tpu_custom_call" | custom-call | flops 91804925952 | bytes 248119296 | tf_op jit(solution)/shard_map/expert/pallas_call | solution.py:135
  108.2 7.6 %collective-permute-done.15.refs_1_.refs_3_ = bf16[320,768]{1,0:T(8,128)(2,1)S(1)} collective-permute-done((bf16[320,768]{1,0:T(8,128)(2,1)}, bf16[320,768]{1,0:T(8,128)(2,1)S(1)}, u32[]{:S(2)}, u32[]{:S(2)}) %collective-permute-start.15) | collective-permute-done | bytes 491552 | tf_op jit(solution)/shard_map/ppermute | solution.py:916
  115.9 11.3 %expert.5 = (bf16[320,768]{1,0:T(8,128)(2,1)}, bf16[304,768]{1,0:T(8,128)(2,1)}, bf16[304,3072]{1,0:T(8,128)(2,1)S(1)}, bf16[304,3072]{1,0:T(8,128)(2,1)S(1)}, bf16[304,768]{1,0:T(8,128)(2,1)S(1)}) custom-call(s32[2]{0:T(128)S(1)} %pad_add_fusion.refs_0_.s_ref, bf16[320,768]{1,0:T(8,128)(2,1)S(1)} %collective-permute-done.15.refs_1_.refs_3_, ...), custom_call_target="tpu_custom_call" | custom-call | flops 91804925952 | bytes 248119296 | tf_op jit(solution)/shard_map/expert/pallas_call | solution.py:135
  129.2 12.0 %expert.6 = (bf16[320,768]{1,0:T(8,128)(2,1)}, bf16[304,768]{1,0:T(8,128)(2,1)}, bf16[304,3072]{1,0:T(8,128)(2,1)S(1)}, bf16[304,3072]{1,0:T(8,128)(2,1)S(1)}, bf16[304,768]{1,0:T(8,128)(2,1)S(1)}) custom-call(s32[2]{0:T(128)S(1)} %pad_add_fusion.refs_0_.s_ref, bf16[320,768]{1,0:T(8,128)(2,1)} %collective-permute-done.17.refs_1_, ...), custom_call_target="tpu_custom_call" | custom-call | flops 91804925952 | bytes 248119296 | tf_op jit(solution)/shard_map/expert/pallas_call | solution.py:135
  146.3 12.4 %expert.7 = (bf16[320,768]{1,0:T(8,128)(2,1)}, bf16[304,768]{1,0:T(8,128)(2,1)}, bf16[304,3072]{1,0:T(8,128)(2,1)S(1)}, bf16[304,3072]{1,0:T(8,128)(2,1)S(1)}, bf16[304,768]{1,0:T(8,128)(2,1)S(1)}) custom-call(s32[2]{0:T(128)S(1)} %pad_add_fusion.refs_0_.s_ref, bf16[320,768]{1,0:T(8,128)(2,1)} %collective-permute-done.16.refs_1_.refs_2_, ...), custom_call_target="tpu_custom_call" | custom-call | flops 91804925952 | bytes 248119296 | tf_op jit(solution)/shard_map/expert/pallas_call | solution.py:135
  160.1 12.3 %weight_grad.6 = (bf16[8,384,768]{2,1,0:T(8,128)(2,1)}, bf16[8,384,768]{2,1,0:T(8,128)(2,1)S(1)}) custom-call(s32[2]{0:T(128)S(1)} %pad_add_fusion.1.s_ref, bf16[320,768]{1,0:T(8,128)(2,1)S(1)} %copy-done.61, bf16[320,768]{1,0:T(8,128)(2,1)} %collective-permute-done.17.refs_1_, bf16[320,768]{1,0:T(8,128)(2,1)} %collective-permute-done.16.refs_1_.refs_2_, ...), custom_call_target="tpu_custom_call" | custom-call | flops 91804925952 | bytes 224919552 | tf_op jit(solution)/shard_map/weight_grad/pallas_call | solution.py:475
  172.4 9.8 %collective-permute-done.20.refs_15_ = bf16[320,768]{1,0:T(8,128)(2,1)S(1)} collective-permute-done((bf16[320,768]{1,0:T(8,128)(2,1)}, bf16[320,768]{1,0:T(8,128)(2,1)S(1)}, u32[]{:S(2)}, u32[]{:S(2)}) %collective-permute-start.20) | collective-permute-done | bytes 491552 | tf_op jit(solution)/shard_map/ppermute | solution.py:916
  183.7 18.4 %dense_backward.1 = (bf16[576,768]{1,0:T(8,128)(2,1)S(1)}, bf16[576,3072]{1,0:T(8,128)(2,1)S(1)}, f32[576,768]{1,0:T(8,128)S(1)}, f32[8,768]{1,0:T(8,128)S(1)}, f32[16,768]{1,0:T(8,128)S(1)}) custom-call(bf16[576,768]{1,0:T(8,128)(2,1)S(1)} %maximum_select_fusion.4.refs_0_, f32[576,768]{1,0:T(8,128)S(1)} %copy-done, f32[576,768]{1,0:T(8,128)S(1)} %copy-done.40, ...), custom_call_target="tpu_custom_call" | custom-call | flops 104186511360 | bytes 391643136 | tf_op jit(solution)/shard_map/dense_backward/pallas_call | solution.py:135
  202.1 7.0 %weight_grad.5 = (bf16[4,384,768]{2,1,0:T(8,128)(2,1)S(1)}, bf16[4,384,768]{2,1,0:T(8,128)(2,1)S(1)}) custom-call(s32[2]{0:T(128)S(1)} %pad_add_fusion.refs_0_.s_ref, bf16[576,3072]{1,0:T(8,128)(2,1)S(1)} %copy-done.29, bf16[576,768]{1,0:T(8,128)(2,1)S(1)} %get-tuple-element.289.refs_1_.refs_4_), custom_call_target="tpu_custom_call" | custom-call | flops 43486543872 | bytes 146276352 | tf_op jit(solution)/shard_map/weight_grad/pallas_call | solution.py:475
  211.2 7.2 %weight_grad.4 = (bf16[4,384,768]{2,1,0:T(8,128)(2,1)S(1)}, bf16[4,384,768]{2,1,0:T(8,128)(2,1)S(1)}) custom-call(s32[2]{0:T(128)S(1)} %pad_add_fusion.refs_0_.s_ref, bf16[576,768]{1,0:T(8,128)(2,1)S(1)} %copy-done.41, bf16[576,3072]{1,0:T(8,128)(2,1)S(1)} %copy-done.31), custom_call_target="tpu_custom_call" | custom-call | flops 43486543872 | bytes 146276352 | tf_op jit(solution)/shard_map/weight_grad/pallas_call | solution.py:475
  223.7 11.8 %weight_grad.7 = (bf16[8,384,768]{2,1,0:T(8,128)(2,1)}, bf16[8,384,768]{2,1,0:T(8,128)(2,1)S(1)}) custom-call(s32[2]{0:T(128)S(1)} %copy-done.28, bf16[304,768]{1,0:T(8,128)(2,1)S(1)} %copy-done.52, bf16[304,768]{1,0:T(8,128)(2,1)S(1)} %copy-done.56, bf16[304,768]{1,0:T(8,128)(2,1)S(1)} %copy-done.58, ...), custom_call_target="tpu_custom_call", output_to_operand_aliasing={{0}: (9, {}), {1}: (10, {})} | custom-call | flops 91804925952 | bytes 224919552 | tf_op jit(solution)/shard_map/weight_grad/pallas_call | solution.py:475
  241.0 17.3 %attention_backward.1 = (bf16[576,768]{1,0:T(8,128)(2,1)S(1)}, bf16[576,2304]{1,0:T(8,128)(2,1)S(1)}) custom-call(s32[2]{0:T(128)S(1)} %pad_add_fusion.refs_0_.s_ref, f32[576,768]{1,0:T(8,128)S(1)} %copy-done.33, s32[1,576]{1,0:T(1,128)S(1)} %get-tuple-element.420.refs_2_, s32[576,1]{1,0:T(8,128)S(1)} %copy.36.refs_3_, bf16[576,2304]{1,0:T(8,128)(2,1)S(1)} %copy-done.37, ...), custom_call_target="tpu_custom_call" | custom-call | flops 92408905728 | bytes 146276352 | tf_op jit(solution)/shard_map/attention_backward/pallas_call | solution.py:135
  258.4 7.3 %attention_grad.1 = (bf16[4,384,768]{2,1,0:T(8,128)(2,1)S(1)}, bf16[4,384,768]{2,1,0:T(8,128)(2,1)S(1)}) custom-call(s32[2]{0:T(128)S(1)} %pad_add_fusion.refs_0_.s_ref, bf16[576,768]{1,0:T(8,128)(2,1)S(1)} %copy-done.6, bf16[576,768]{1,0:T(8,128)(2,1)S(1)} %copy-done.7, bf16[576,2304]{1,0:T(8,128)(2,1)S(1)} %get-tuple-element.337.dpacked.refs_4_, ...), custom_call_target="tpu_custom_call" | custom-call | flops 339738624 | bytes 442368 | tf_op jit(solution)/shard_map/attention_grad/pallas_call | solution.py:523
  267.6 7.0 %input_backward.1 = (f32[576,768]{1,0:T(8,128)S(1)}, f32[8,768]{1,0:T(8,128)S(1)}) custom-call(s32[2]{0:T(128)S(1)} %pad_add_fusion.refs_0_.s_ref, bf16[576,768]{1,0:T(8,128)(2,1)S(1)} %copy-done.5, f32[576,768]{1,0:T(8,128)S(1)} %copy-done.33, f32[8,768]{1,0:T(8,128)S(1)} %fusion.19.refs_4_.refs_1_.refs_3_, ...), custom_call_target="tpu_custom_call" | custom-call | flops 32614907904 | bytes 169869312 | tf_op jit(solution)/shard_map/input_backward/pallas_call | solution.py:135
  279.6 5.9 %add_convert_fusion = bf16[8,384,768]{2,1,0:T(8,128)(2,1)} fusion(bf16[8,384,768]{2,1,0:T(8,128)(2,1)} %collective-permute-done.32, bf16[8,384,768]{2,1,0:T(8,128)(2,1)S(1)} %get-tuple-element.342), kind=kLoop, calls=%fused_computation | loop fusion | flops 9437184 | bytes 14155776 | tf_op jit(solution)/shard_map/convert_element_type | solution.py:933
  285.4 6.3 %collective-permute-done.30 = bf16[384,768]{1,0:T(8,128)(2,1)} collective-permute-done((bf16[384,768]{1,0:T(8,128)(2,1)S(1)}, bf16[384,768]{1,0:T(8,128)(2,1)}, u32[]{:S(2)}, u32[]{:S(2)}) %collective-permute-start.30) | collective-permute-done | bytes 589856 | tf_op jit(solution)/shard_map/ppermute | solution.py:913
  308.9 6.8 %collective-permute-done.33 = bf16[2,96,768]{2,1,0:T(8,128)(2,1)} collective-permute-done((bf16[2,96,768]{2,1,0:T(8,128)(2,1)}, bf16[2,96,768]{2,1,0:T(8,128)(2,1)}, u32[]{:S(2)}, u32[]{:S(2)}) %collective-permute-start.33) | collective-permute-done | bytes 294944 | tf_op jit(solution)/shard_map/ppermute | solution.py:916
  316.3 9.9 %collective-permute-done.34 = bf16[2,96,768]{2,1,0:T(8,128)(2,1)} collective-permute-done((bf16[2,96,768]{2,1,0:T(8,128)(2,1)}, bf16[2,96,768]{2,1,0:T(8,128)(2,1)}, u32[]{:S(2)}, u32[]{:S(2)}) %collective-permute-start.34) | collective-permute-done | bytes 294944 | tf_op jit(solution)/shard_map/ppermute | solution.py:916
  349.2 9.3 %collective-permute-done.39 = bf16[2,96,768]{2,1,0:T(8,128)(2,1)} collective-permute-done((bf16[2,96,768]{2,1,0:T(8,128)(2,1)}, bf16[2,96,768]{2,1,0:T(8,128)(2,1)}, u32[]{:S(2)}, u32[]{:S(2)}) %collective-permute-start.39) | collective-permute-done | bytes 294944 | tf_op jit(solution)/shard_map/ppermute | solution.py:916
  368.3 6.8 %collective-permute-start.48 = (bf16[2,48,768]{2,1,0:T(8,128)(2,1)S(1)}, bf16[2,48,768]{2,1,0:T(8,128)(2,1)S(1)}, u32[]{:S(2)}, u32[]{:S(2)}) collective-permute-start(bf16[2,48,768]{2,1,0:T(8,128)(2,1)S(1)} %get-tuple-element.458), channel_id=1, source_target_pairs={{0,4},{1,5},{2,6},{3,7},{4,8},{5,9},{6,10},{7,11},{8,12},{9,13},{1... | collective-permute-start | bytes 442376 | tf_op jit(solution)/shard_map/ppermute | solution.py:916
  408.4 7.8 %collective-permute-done.53 = bf16[768,768]{1,0:T(8,128)(2,1)} collective-permute-done((bf16[768,768]{1,0:T(8,128)(2,1)S(1)}, bf16[768,768]{1,0:T(8,128)(2,1)}, u32[]{:S(2)}, u32[]{:S(2)}) %collective-permute-start.53) | collective-permute-done | bytes 1179680 | tf_op jit(solution)/shard_map/ppermute | solution.py:913
  448.7 5.5 %collective-permute-done.62 = bf16[384,768]{1,0:T(8,128)(2,1)S(1)} collective-permute-done((bf16[384,768]{1,0:T(8,128)(2,1)S(1)}, bf16[384,768]{1,0:T(8,128)(2,1)S(1)}, u32[]{:S(2)}, u32[]{:S(2)}) %collective-permute-start.62) | collective-permute-done | bytes 589856 | tf_op jit(solution)/shard_map/ppermute | solution.py:913
  (443 shorter events, 200.4 us)
Async XLA Ops:
  7.2 54.6 %all-gather.3.cloned.1.call-start = ((), (), s32[]{:S(2)}) async-start(), calls=%async_computation.1 | async-start | bytes 7077888 | tf_op jit(solution)/shard_map/all_gather | solution.py:961
  15.2 46.6 %all-gather.5.cloned.1.call-start = ((), (), s32[]{:S(2)}) async-start(), calls=%async_computation.2 | async-start | bytes 7077888 | tf_op jit(solution)/shard_map/all_gather | solution.py:961
  18.2 42.8 %collective-permute-start.5 = (bf16[2,384,768]{2,1,0:T(8,128)(2,1)S(1)}, bf16[2,384,768]{2,1,0:T(8,128)(2,1)}, u32[]{:S(2)}, u32[]{:S(2)}) collective-permute-start(bf16[2,384,768]{2,1,0:T(8,128)(2,1)S(1)} %pad_maximum_fusion.1.refs_3_), channel_id=1, source_target_pairs={{0,1},{1,0},{2,3},{3,2},{4,5},{5,4},{6,7},{7,6},{8,9},{9,8},{10,11... | collective-permute-start | bytes 3538952 | tf_op jit(solution)/shard_map/ppermute | solution.py:913
  20.8 40.1 %collective-permute-start.6 = (bf16[2,384,768]{2,1,0:T(8,128)(2,1)S(1)}, bf16[2,384,768]{2,1,0:T(8,128)(2,1)}, u32[]{:S(2)}, u32[]{:S(2)}) collective-permute-start(bf16[2,384,768]{2,1,0:T(8,128)(2,1)S(1)} %pad_maximum_fusion.1.refs_3_), channel_id=1, source_target_pairs={{0,2},{1,3},{2,0},{3,1},{4,6},{5,7},{6,4},{7,5},{8,10},{9,11},{10,... | collective-permute-start | bytes 3538952 | tf_op jit(solution)/shard_map/ppermute | solution.py:913
  22.3 38.6 %collective-permute-start.7 = (bf16[2,384,768]{2,1,0:T(8,128)(2,1)S(1)}, bf16[2,384,768]{2,1,0:T(8,128)(2,1)}, u32[]{:S(2)}, u32[]{:S(2)}) collective-permute-start(bf16[2,384,768]{2,1,0:T(8,128)(2,1)S(1)} %pad_maximum_fusion.1.refs_3_), channel_id=1, source_target_pairs={{0,16},{16,0},{1,17},{17,1},{2,18},{18,2},{3,19},{19,3},{4,20},{20... | collective-permute-start | bytes 3538952 | tf_op jit(solution)/shard_map/ppermute | solution.py:910
  25.5 30.4 %collective-permute-start.8 = (bf16[304,768]{1,0:T(8,128)(2,1)}, bf16[304,768]{1,0:T(8,128)(2,1)}, u32[]{:S(2)}, u32[]{:S(2)}) collective-permute-start(bf16[304,768]{1,0:T(8,128)(2,1)} %get-tuple-element.224), channel_id=1, source_target_pairs={{0,4},{1,5},{2,6},{3,7},{4,8},{5,9},{6,10},{7,11},{8,12},{9,13},{1... | collective-permute-start | bytes 1400840 | tf_op jit(solution)/shard_map/ppermute | solution.py:916
  27.1 33.8 %collective-permute-start.9 = (bf16[304,768]{1,0:T(8,128)(2,1)}, bf16[304,768]{1,0:T(8,128)(2,1)}, u32[]{:S(2)}, u32[]{:S(2)}) collective-permute-start(bf16[304,768]{1,0:T(8,128)(2,1)} %get-tuple-element.225), channel_id=1, source_target_pairs={{0,8},{1,9},{2,10},{3,11},{4,12},{5,13},{6,14},{7,15},{8,0},{9,1},... | collective-permute-start | bytes 1400840 | tf_op jit(solution)/shard_map/ppermute | solution.py:916
  29.7 411.2 %reduce-scatter.4.cloned.1.call-start = ((), (), s32[]{:S(2)}) async-start(), calls=%async_computation.3 | async-start | bytes 5898240
  55.9 31.7 %collective-permute-start.12 = (bf16[304,768]{1,0:T(8,128)(2,1)}, bf16[304,768]{1,0:T(8,128)(2,1)S(1)}, u32[]{:S(2)}, u32[]{:S(2)}) collective-permute-start(bf16[304,768]{1,0:T(8,128)(2,1)} %get-tuple-element.239), channel_id=1, source_target_pairs={{0,12},{1,13},{2,14},{3,15},{4,0},{5,1},{6,2},{7,3},{8,4},{9,5},{1... | collective-permute-start | bytes 1400840 | tf_op jit(solution)/shard_map/ppermute | solution.py:916
  60.9 27.4 %collective-permute-start.10 = (bf16[2,384,768]{2,1,0:T(8,128)(2,1)}, bf16[2,384,768]{2,1,0:T(8,128)(2,1)}, u32[]{:S(2)}, u32[]{:S(2)}) collective-permute-start(bf16[2,384,768]{2,1,0:T(8,128)(2,1)} %collective-permute-done.5.refs_4_), channel_id=1, source_target_pairs={{0,16},{16,0},{1,17},{17,1},{2,18},{18,2},{3,19},{19,3},{4,20},{20... | collective-permute-start | bytes 3538952 | tf_op jit(solution)/shard_map/ppermute | solution.py:910
  61.0 28.7 %collective-permute-start.13 = (bf16[2,384,768]{2,1,0:T(8,128)(2,1)}, bf16[2,384,768]{2,1,0:T(8,128)(2,1)}, u32[]{:S(2)}, u32[]{:S(2)}) collective-permute-start(bf16[2,384,768]{2,1,0:T(8,128)(2,1)} %collective-permute-done.5.refs_4_), channel_id=1, source_target_pairs={{0,2},{1,3},{2,0},{3,1},{4,6},{5,7},{6,4},{7,5},{8,10},{9,11},{10,... | collective-permute-start | bytes 3538952 | tf_op jit(solution)/shard_map/ppermute | solution.py:913
  61.6 26.8 %collective-permute-start.11 = (bf16[2,384,768]{2,1,0:T(8,128)(2,1)}, bf16[2,384,768]{2,1,0:T(8,128)(2,1)}, u32[]{:S(2)}, u32[]{:S(2)}) collective-permute-start(bf16[2,384,768]{2,1,0:T(8,128)(2,1)} %collective-permute-done.6.refs_5_), channel_id=1, source_target_pairs={{0,16},{16,0},{1,17},{17,1},{2,18},{18,2},{3,19},{19,3},{4,20},{20... | collective-permute-start | bytes 3538952 | tf_op jit(solution)/shard_map/ppermute | solution.py:910
  89.8 26.1 %collective-permute-start.15 = (bf16[320,768]{1,0:T(8,128)(2,1)}, bf16[320,768]{1,0:T(8,128)(2,1)S(1)}, u32[]{:S(2)}, u32[]{:S(2)}) collective-permute-start(bf16[320,768]{1,0:T(8,128)(2,1)} %get-tuple-element.248), channel_id=1, source_target_pairs={{0,12},{1,13},{2,14},{3,15},{4,0},{5,1},{6,2},{7,3},{8,4},{9,5},{1... | collective-permute-start | bytes 1474568 | tf_op jit(solution)/shard_map/ppermute | solution.py:916
  91.3 37.9 %collective-permute-start.17 = (bf16[320,768]{1,0:T(8,128)(2,1)}, bf16[320,768]{1,0:T(8,128)(2,1)}, u32[]{:S(2)}, u32[]{:S(2)}) collective-permute-start(bf16[320,768]{1,0:T(8,128)(2,1)} %get-tuple-element.255), channel_id=1, source_target_pairs={{0,4},{1,5},{2,6},{3,7},{4,8},{5,9},{6,10},{7,11},{8,12},{9,13},{1... | collective-permute-start | bytes 1474568 | tf_op jit(solution)/shard_map/ppermute | solution.py:916
  92.0 54.3 %collective-permute-start.16 = (bf16[320,768]{1,0:T(8,128)(2,1)}, bf16[320,768]{1,0:T(8,128)(2,1)}, u32[]{:S(2)}, u32[]{:S(2)}) collective-permute-start(bf16[320,768]{1,0:T(8,128)(2,1)} %get-tuple-element.254), channel_id=1, source_target_pairs={{0,8},{1,9},{2,10},{3,11},{4,12},{5,13},{6,14},{7,15},{8,0},{9,1},... | collective-permute-start | bytes 1474568 | tf_op jit(solution)/shard_map/ppermute | solution.py:916
  223.0 42.7 %collective-permute-start.26 = (bf16[304,768]{1,0:T(8,128)(2,1)}, bf16[304,768]{1,0:T(8,128)(2,1)}, u32[]{:S(2)}, u32[]{:S(2)}) collective-permute-start(bf16[304,768]{1,0:T(8,128)(2,1)} %get-tuple-element.329), channel_id=1, source_target_pairs={{0,8},{1,9},{2,10},{3,11},{4,12},{5,13},{6,14},{7,15},{8,0},{9,1},... | collective-permute-start | bytes 1400840 | tf_op jit(solution)/shard_map/ppermute | solution.py:916
  223.0 42.7 %collective-permute-start.27 = (bf16[304,768]{1,0:T(8,128)(2,1)}, bf16[304,768]{1,0:T(8,128)(2,1)}, u32[]{:S(2)}, u32[]{:S(2)}) collective-permute-start(bf16[304,768]{1,0:T(8,128)(2,1)} %get-tuple-element.330), channel_id=1, source_target_pairs={{0,4},{1,5},{2,6},{3,7},{4,8},{5,9},{6,10},{7,11},{8,12},{9,13},{1... | collective-permute-start | bytes 1400840 | tf_op jit(solution)/shard_map/ppermute | solution.py:916
  235.4 44.1 %collective-permute-start.32 = (bf16[8,384,768]{2,1,0:T(8,128)(2,1)}, bf16[8,384,768]{2,1,0:T(8,128)(2,1)}, u32[]{:S(2)}, u32[]{:S(2)}) collective-permute-start(bf16[8,384,768]{2,1,0:T(8,128)(2,1)} %get-tuple-element.343), channel_id=1, source_target_pairs={{0,16},{16,0},{1,17},{17,1},{2,18},{18,2},{3,19},{19,3},{4,20},{20... | collective-permute-start | bytes 14155784 | tf_op jit(solution)/shard_map/ppermute | solution.py:910
  238.9 28.4 %collective-permute-start.24 = (bf16[768,768]{1,0:T(8,128)(2,1)S(1)}, bf16[768,768]{1,0:T(8,128)(2,1)S(1)}, u32[]{:S(2)}, u32[]{:S(2)}) collective-permute-start(bf16[768,768]{1,0:T(8,128)(2,1)S(1)} %get-tuple-element.423), channel_id=1, source_target_pairs={{0,2},{1,3},{2,0},{3,1},{4,6},{5,7},{6,4},{7,5},{8,10},{9,11},{10,... | collective-permute-start | bytes 3538952 | tf_op jit(solution)/shard_map/ppermute | solution.py:913
  239.4 28.2 %collective-permute-start.23 = (bf16[768,768]{1,0:T(8,128)(2,1)S(1)}, bf16[768,768]{1,0:T(8,128)(2,1)S(1)}, u32[]{:S(2)}, u32[]{:S(2)}) collective-permute-start(bf16[768,768]{1,0:T(8,128)(2,1)S(1)} %get-tuple-element.425), channel_id=1, source_target_pairs={{0,1},{1,0},{2,3},{3,2},{4,5},{5,4},{6,7},{7,6},{8,9},{9,8},{10,11... | collective-permute-start | bytes 3538952 | tf_op jit(solution)/shard_map/ppermute | solution.py:913
  299.3 27.0 %collective-permute-start.37 = (bf16[384,768]{1,0:T(8,128)(2,1)S(1)}, bf16[384,768]{1,0:T(8,128)(2,1)S(1)}, u32[]{:S(2)}, u32[]{:S(2)}) collective-permute-start(bf16[384,768]{1,0:T(8,128)(2,1)S(1)} %get-tuple-element.435), channel_id=1, source_target_pairs={{0,2},{1,3},{2,0},{3,1},{4,6},{5,7},{6,4},{7,5},{8,10},{9,11},{10,... | collective-permute-start | bytes 1769480 | tf_op jit(solution)/shard_map/ppermute | solution.py:913
  301.9 27.5 %collective-permute-start.36 = (bf16[384,768]{1,0:T(8,128)(2,1)S(1)}, bf16[384,768]{1,0:T(8,128)(2,1)S(1)}, u32[]{:S(2)}, u32[]{:S(2)}) collective-permute-start(bf16[384,768]{1,0:T(8,128)(2,1)S(1)} %get-tuple-element.437), channel_id=1, source_target_pairs={{0,1},{1,0},{2,3},{3,2},{4,5},{5,4},{6,7},{7,6},{8,9},{9,8},{10,11... | collective-permute-start | bytes 1769480 | tf_op jit(solution)/shard_map/ppermute | solution.py:913
  388.7 27.5 %collective-permute-start.53 = (bf16[768,768]{1,0:T(8,128)(2,1)S(1)}, bf16[768,768]{1,0:T(8,128)(2,1)}, u32[]{:S(2)}, u32[]{:S(2)}) collective-permute-start(bf16[768,768]{1,0:T(8,128)(2,1)S(1)} %maximum_select_fusion.2), channel_id=1, source_target_pairs={{0,2},{1,3},{2,0},{3,1},{4,6},{5,7},{6,4},{7,5},{8,10},{9,11},{10,... | collective-permute-start | bytes 3538952 | tf_op jit(solution)/shard_map/ppermute | solution.py:913
  392.1 27.2 %collective-permute-start.52 = (bf16[768,768]{1,0:T(8,128)(2,1)S(1)}, bf16[768,768]{1,0:T(8,128)(2,1)}, u32[]{:S(2)}, u32[]{:S(2)}) collective-permute-start(bf16[768,768]{1,0:T(8,128)(2,1)S(1)} %maximum_select_fusion.1), channel_id=1, source_target_pairs={{0,1},{1,0},{2,3},{3,2},{4,5},{5,4},{6,7},{7,6},{8,9},{9,8},{10,11... | collective-permute-start | bytes 3538952 | tf_op jit(solution)/shard_map/ppermute | solution.py:913
  (151 other events, 1317.3 us)
Sparse Core Ops, SparseCore 0:
  15.3 17.0 all-gather.2
  33.9 15.6 all-gather.4
  294.9 79.6 reduce-scatter.3

commit v3 on v2

--- a/solution.py
+++ b/solution.py
@@ -1123,15 +1123,15 @@
         tiny = [over_e(tiny, r) if r else tiny for r in range(experts)]
     else:
         tiny = [lax.psum(tiny, "dp", axis_index_groups=planes)]
-    sum_fc2 = finish(side_x, blocks(a), blocks(a_got), False)
-    sum_fc1 = finish(side_y, blocks(b), blocks(b_got), True)
-    ta_got, tb_got, tiny, sum_fc2, sum_fc1, half_experts = tie(
-        (ta_got, tb_got, tiny, sum_fc2, sum_fc1, half_experts)
+    ta_got, tb_got, tiny, a, a_got, b, b_got, grad_in, block_out, half_experts = tie(
+        (ta_got, tb_got, tiny, a, a_got, b, b_got, grad_in, block_out, half_experts)
     )
     half_up, half_down = half_experts[0].astype(F32), half_experts[1].astype(F32)
     ta, tb = unfold(ta, ta_got, 2), unfold(tb, tb_got, 1)
     ta_got, tb_got = over_q(ta, 1), over_q(tb, 2)
     total = sum(tiny)
+    sum_fc2 = finish(side_x, blocks(a), blocks(a_got), False)
+    sum_fc1 = finish(side_y, blocks(b), blocks(b_got), True)
     q_and_k = finish(side_x, blocks(ta), blocks(ta_got), True)
     first = q // 2 == 0
     v_sum, sum_attn = (

time: 474 us -> 467 us (0.985)
  waiting for transfers between devices: 98.1 us -> 90.1 us
    ppermute x21, waiting for transfers between devices: 34.6 us -> 27.8 us  [over_q(): return lax.ppermute(v, 'dp', [(i, i ^ bit) for i in range(dp_count)])]
    unnamed x216 -> x194, local copies, waits for them, and re-layouts: 33.5 us -> 33.4 us
  transfers between devices with their start and end apart: 67 -> 67, of which waited for: 27 -> 25; matrix products, arithmetic and copies ran while one was open for 11% -> 11% of each run, Pallas kernels for 34% -> 34%
where the time goes in v3:
time: 467 us; the launch traced here: 460 us
  Pallas kernels  190 us (41%)
  waiting for transfers between devices  90.1 us (19%)
  starting transfers between devices  75.6 us (16%)
  local copies, waits for them, and re-layouts  49.2 us (11%)
  other arithmetic  39.3 us (8%)
  between operations  15.4 us (3%)
    pallas_call x15, Pallas kernels, call(): return lambda *operands: made(*operands, *after)  144 us
    ppermute x27, waiting for transfers between devices, over_e(): lax.ppermute(v, 'dp', [(i, (i // GROUP + r) % experts * GROUP + i % GROUP...  61.3 us
    ppermute x27, starting transfers between devices, over_e(): lax.ppermute(v, 'dp', [(i, (i // GROUP + r) % experts * GROUP + i % GROUP...  49.4 us
    pallas_call x4, Pallas kernels, weight_grad(): pl.pallas_call(functools.partial(grad_kernel, n, len(into)), grid_spec=pl...  38.2 us
    unnamed x194, local copies, waits for them, and re-layouts  33.4 us
    ppermute x21, waiting for transfers between devices, over_q(): return lax.ppermute(v, 'dp', [(i, i ^ bit) for i in range(dp_count)])  27.8 us
    ppermute x21, starting transfers between devices, over_q(): return lax.ppermute(v, 'dp', [(i, i ^ bit) for i in range(dp_count)])  23.4 us
    convert_element_type x7, other arithmetic, add(): return (a.astype(F32) + b.astype(F32)).astype(BF)  11.6 us
  transfers between devices with their start and end apart: 67, of which 25 were waited for; matrix products, arithmetic and copies ran while one was open for 11% of the time, Pallas kernels for 34%

profile of v3, /device:TPU:0, one launch (start us, length us, event | category | flops | bytes accessed | tf_op | source)
XLA Modules:
  0.0 460.0 jit_solution(3224783751140425344)
XLA Ops:
  33.1 21.3 %attention_forward.1 = (bf16[576,768]{1,0:T(8,128)(2,1)}, bf16[576,2304]{1,0:T(8,128)(2,1)}, bf16[576,768]{1,0:T(8,128)(2,1)}, f32[16,576]{1,0:T(8,128)S(1)}, f32[576,768]{1,0:T(8,128)S(1)}) custom-call(s32[2]{0:T(128)S(1)} %pad_add_fusion.refs_0_.s_ref, bf16[576,768]{1,0:T(8,128)(2,1)S(1)} %maximum_select_fusion.3.refs_1_, ...), custom_call_target="tpu_custom_call" | custom-call | flops 59793997824 | bytes 188743680 | tf_op jit(solution)/shard_map/attention_forward/pallas_call | solution.py:135
  67.7 18.9 %dense_forward.1 = (bf16[576,768]{1,0:T(8,128)(2,1)}, bf16[576,3072]{1,0:T(8,128)(2,1)}, bf16[576,3072]{1,0:T(8,128)(2,1)}, f32[576,768]{1,0:T(8,128)}, bf16[576...) custom-call(f32[576,768]{1,0:T(8,128)S(1)} %copy-done.38, ...), custom_call_target="tpu_custom_call" | custom-call | flops 104186511360 | bytes 349175808 | tf_op jit(solution)/shard_map/dense_forward/pallas_call | solution.py:135
  94.7 11.2 %expert.4 = (bf16[320,768]{1,0:T(8,128)(2,1)}, bf16[304,768]{1,0:T(8,128)(2,1)}, bf16[304,3072]{1,0:T(8,128)(2,1)S(1)}, bf16[304,3072]{1,0:T(8,128)(2,1)S(1)}, bf16[304,768]{1,0:T(8,128)(2,1)S(1)}) custom-call(s32[2]{0:T(128)S(1)} %pad_add_fusion.refs_0_.s_ref, bf16[320,768]{1,0:T(8,128)(2,1)S(1)} %copy-done.59, bf16[304,768]{1,0:T(8,128)(2,1)S(1)} %copy-done.35, ...), custom_call_target="tpu_custom_call" | custom-call | flops 91804925952 | bytes 248119296 | tf_op jit(solution)/shard_map/expert/pallas_call | solution.py:135
  108.0 7.7 %collective-permute-done.15.refs_1_.refs_3_ = bf16[320,768]{1,0:T(8,128)(2,1)S(1)} collective-permute-done((bf16[320,768]{1,0:T(8,128)(2,1)}, bf16[320,768]{1,0:T(8,128)(2,1)S(1)}, u32[]{:S(2)}, u32[]{:S(2)}) %collective-permute-start.15) | collective-permute-done | bytes 491552 | tf_op jit(solution)/shard_map/ppermute | solution.py:916
  115.6 11.3 %expert.5 = (bf16[320,768]{1,0:T(8,128)(2,1)}, bf16[304,768]{1,0:T(8,128)(2,1)}, bf16[304,3072]{1,0:T(8,128)(2,1)S(1)}, bf16[304,3072]{1,0:T(8,128)(2,1)S(1)}, bf16[304,768]{1,0:T(8,128)(2,1)S(1)}) custom-call(s32[2]{0:T(128)S(1)} %pad_add_fusion.refs_0_.s_ref, bf16[320,768]{1,0:T(8,128)(2,1)S(1)} %collective-permute-done.15.refs_1_.refs_3_, ...), custom_call_target="tpu_custom_call" | custom-call | flops 91804925952 | bytes 248119296 | tf_op jit(solution)/shard_map/expert/pallas_call | solution.py:135
  129.0 12.0 %expert.6 = (bf16[320,768]{1,0:T(8,128)(2,1)}, bf16[304,768]{1,0:T(8,128)(2,1)}, bf16[304,3072]{1,0:T(8,128)(2,1)S(1)}, bf16[304,3072]{1,0:T(8,128)(2,1)S(1)}, bf16[304,768]{1,0:T(8,128)(2,1)S(1)}) custom-call(s32[2]{0:T(128)S(1)} %pad_add_fusion.refs_0_.s_ref, bf16[320,768]{1,0:T(8,128)(2,1)} %collective-permute-done.17.refs_1_, ...), custom_call_target="tpu_custom_call" | custom-call | flops 91804925952 | bytes 248119296 | tf_op jit(solution)/shard_map/expert/pallas_call | solution.py:135
  146.0 12.5 %expert.7 = (bf16[320,768]{1,0:T(8,128)(2,1)}, bf16[304,768]{1,0:T(8,128)(2,1)}, bf16[304,3072]{1,0:T(8,128)(2,1)S(1)}, bf16[304,3072]{1,0:T(8,128)(2,1)S(1)}, bf16[304,768]{1,0:T(8,128)(2,1)S(1)}) custom-call(s32[2]{0:T(128)S(1)} %pad_add_fusion.refs_0_.s_ref, bf16[320,768]{1,0:T(8,128)(2,1)} %collective-permute-done.16.refs_1_.refs_2_, ...), custom_call_target="tpu_custom_call" | custom-call | flops 91804925952 | bytes 248119296 | tf_op jit(solution)/shard_map/expert/pallas_call | solution.py:135
  159.9 12.3 %weight_grad.6 = (bf16[8,384,768]{2,1,0:T(8,128)(2,1)}, bf16[8,384,768]{2,1,0:T(8,128)(2,1)S(1)}) custom-call(s32[2]{0:T(128)S(1)} %pad_add_fusion.1.s_ref, bf16[320,768]{1,0:T(8,128)(2,1)S(1)} %copy-done.60, bf16[320,768]{1,0:T(8,128)(2,1)} %collective-permute-done.17.refs_1_, bf16[320,768]{1,0:T(8,128)(2,1)} %collective-permute-done.16.refs_1_.refs_2_, ...), custom_call_target="tpu_custom_call" | custom-call | flops 91804925952 | bytes 224919552 | tf_op jit(solution)/shard_map/weight_grad/pallas_call | solution.py:475
  172.2 9.8 %collective-permute-done.20.refs_15_ = bf16[320,768]{1,0:T(8,128)(2,1)S(1)} collective-permute-done((bf16[320,768]{1,0:T(8,128)(2,1)}, bf16[320,768]{1,0:T(8,128)(2,1)S(1)}, u32[]{:S(2)}, u32[]{:S(2)}) %collective-permute-start.20) | collective-permute-done | bytes 491552 | tf_op jit(solution)/shard_map/ppermute | solution.py:916
  183.5 18.4 %dense_backward.1 = (bf16[576,768]{1,0:T(8,128)(2,1)S(1)}, bf16[576,3072]{1,0:T(8,128)(2,1)S(1)}, f32[576,768]{1,0:T(8,128)S(1)}, f32[8,768]{1,0:T(8,128)S(1)}, f32[16,768]{1,0:T(8,128)S(1)}) custom-call(bf16[576,768]{1,0:T(8,128)(2,1)S(1)} %maximum_select_fusion.4.refs_0_, f32[576,768]{1,0:T(8,128)S(1)} %copy-done, f32[576,768]{1,0:T(8,128)S(1)} %copy-done.39, ...), custom_call_target="tpu_custom_call" | custom-call | flops 104186511360 | bytes 391643136 | tf_op jit(solution)/shard_map/dense_backward/pallas_call | solution.py:135
  201.9 7.0 %weight_grad.5 = (bf16[4,384,768]{2,1,0:T(8,128)(2,1)S(1)}, bf16[4,384,768]{2,1,0:T(8,128)(2,1)S(1)}) custom-call(s32[2]{0:T(128)S(1)} %pad_add_fusion.refs_0_.s_ref, bf16[576,3072]{1,0:T(8,128)(2,1)S(1)} %copy-done.28, bf16[576,768]{1,0:T(8,128)(2,1)S(1)} %get-tuple-element.295.refs_1_.refs_4_), custom_call_target="tpu_custom_call" | custom-call | flops 43486543872 | bytes 146276352 | tf_op jit(solution)/shard_map/weight_grad/pallas_call | solution.py:475
  211.0 7.2 %weight_grad.4 = (bf16[4,384,768]{2,1,0:T(8,128)(2,1)S(1)}, bf16[4,384,768]{2,1,0:T(8,128)(2,1)S(1)}) custom-call(s32[2]{0:T(128)S(1)} %pad_add_fusion.refs_0_.s_ref, bf16[576,768]{1,0:T(8,128)(2,1)S(1)} %copy-done.40, bf16[576,3072]{1,0:T(8,128)(2,1)S(1)} %copy-done.30), custom_call_target="tpu_custom_call" | custom-call | flops 43486543872 | bytes 146276352 | tf_op jit(solution)/shard_map/weight_grad/pallas_call | solution.py:475
  223.4 11.8 %weight_grad.7 = (bf16[8,384,768]{2,1,0:T(8,128)(2,1)}, bf16[8,384,768]{2,1,0:T(8,128)(2,1)S(1)}) custom-call(s32[2]{0:T(128)S(1)} %copy-done.27, bf16[304,768]{1,0:T(8,128)(2,1)S(1)} %copy-done.51, bf16[304,768]{1,0:T(8,128)(2,1)S(1)} %copy-done.55, bf16[304,768]{1,0:T(8,128)(2,1)S(1)} %copy-done.57, ...), custom_call_target="tpu_custom_call", output_to_operand_aliasing={{0}: (9, {}), {1}: (10, {})} | custom-call | flops 91804925952 | bytes 224919552 | tf_op jit(solution)/shard_map/weight_grad/pallas_call | solution.py:475
  240.6 17.3 %attention_backward.1 = (bf16[576,768]{1,0:T(8,128)(2,1)S(1)}, bf16[576,2304]{1,0:T(8,128)(2,1)S(1)}) custom-call(s32[2]{0:T(128)S(1)} %pad_add_fusion.refs_0_.s_ref, f32[576,768]{1,0:T(8,128)S(1)} %copy-done.32, s32[1,576]{1,0:T(1,128)S(1)} %get-tuple-element.432.refs_2_, s32[576,1]{1,0:T(8,128)S(1)} %copy.36.refs_3_, bf16[576,2304]{1,0:T(8,128)(2,1)S(1)} %copy-done.36, ...), custom_call_target="tpu_custom_call" | custom-call | flops 92408905728 | bytes 146276352 | tf_op jit(solution)/shard_map/attention_backward/pallas_call | solution.py:135
  258.0 7.3 %attention_grad.1 = (bf16[4,384,768]{2,1,0:T(8,128)(2,1)S(1)}, bf16[4,384,768]{2,1,0:T(8,128)(2,1)S(1)}) custom-call(s32[2]{0:T(128)S(1)} %pad_add_fusion.refs_0_.s_ref, bf16[576,768]{1,0:T(8,128)(2,1)S(1)} %copy-done.5, bf16[576,768]{1,0:T(8,128)(2,1)S(1)} %copy-done.6, bf16[576,2304]{1,0:T(8,128)(2,1)S(1)} %get-tuple-element.343.dpacked.refs_4_, ...), custom_call_target="tpu_custom_call" | custom-call | flops 339738624 | bytes 442368 | tf_op jit(solution)/shard_map/attention_grad/pallas_call | solution.py:523
  267.3 7.0 %input_backward.1 = (f32[576,768]{1,0:T(8,128)S(1)}, f32[8,768]{1,0:T(8,128)S(1)}) custom-call(s32[2]{0:T(128)S(1)} %pad_add_fusion.refs_0_.s_ref, bf16[576,768]{1,0:T(8,128)(2,1)S(1)} %copy-done.4, f32[576,768]{1,0:T(8,128)S(1)} %copy-done.32, f32[8,768]{1,0:T(8,128)S(1)} %fusion.19.refs_4_.refs_1_.refs_3_, ...), custom_call_target="tpu_custom_call" | custom-call | flops 32614907904 | bytes 169869312 | tf_op jit(solution)/shard_map/input_backward/pallas_call | solution.py:135
  279.3 5.8 %add_convert_fusion = bf16[8,384,768]{2,1,0:T(8,128)(2,1)} fusion(bf16[8,384,768]{2,1,0:T(8,128)(2,1)} %collective-permute-done.32, bf16[8,384,768]{2,1,0:T(8,128)(2,1)S(1)} %get-tuple-element.348), kind=kLoop, calls=%fused_computation | loop fusion | flops 9437184 | bytes 14155776 | tf_op jit(solution)/shard_map/convert_element_type | solution.py:933
  285.1 6.4 %collective-permute-done.30 = bf16[384,768]{1,0:T(8,128)(2,1)} collective-permute-done((bf16[384,768]{1,0:T(8,128)(2,1)S(1)}, bf16[384,768]{1,0:T(8,128)(2,1)}, u32[]{:S(2)}, u32[]{:S(2)}) %collective-permute-start.30) | collective-permute-done | bytes 589856 | tf_op jit(solution)/shard_map/ppermute | solution.py:913
  308.7 6.8 %collective-permute-done.33 = bf16[2,96,768]{2,1,0:T(8,128)(2,1)} collective-permute-done((bf16[2,96,768]{2,1,0:T(8,128)(2,1)}, bf16[2,96,768]{2,1,0:T(8,128)(2,1)}, u32[]{:S(2)}, u32[]{:S(2)}) %collective-permute-start.33) | collective-permute-done | bytes 294944 | tf_op jit(solution)/shard_map/ppermute | solution.py:916
  316.0 9.9 %collective-permute-done.34 = bf16[2,96,768]{2,1,0:T(8,128)(2,1)} collective-permute-done((bf16[2,96,768]{2,1,0:T(8,128)(2,1)}, bf16[2,96,768]{2,1,0:T(8,128)(2,1)}, u32[]{:S(2)}, u32[]{:S(2)}) %collective-permute-start.34) | collective-permute-done | bytes 294944 | tf_op jit(solution)/shard_map/ppermute | solution.py:916
  349.0 9.3 %collective-permute-done.39 = bf16[2,96,768]{2,1,0:T(8,128)(2,1)} collective-permute-done((bf16[2,96,768]{2,1,0:T(8,128)(2,1)}, bf16[2,96,768]{2,1,0:T(8,128)(2,1)}, u32[]{:S(2)}, u32[]{:S(2)}) %collective-permute-start.39) | collective-permute-done | bytes 294944 | tf_op jit(solution)/shard_map/ppermute | solution.py:916
  368.0 6.8 %collective-permute-start.46 = (bf16[2,48,768]{2,1,0:T(8,128)(2,1)S(1)}, bf16[2,48,768]{2,1,0:T(8,128)(2,1)S(1)}, u32[]{:S(2)}, u32[]{:S(2)}) collective-permute-start(bf16[2,48,768]{2,1,0:T(8,128)(2,1)S(1)} %get-tuple-element.470), channel_id=1, source_target_pairs={{0,4},{1,5},{2,6},{3,7},{4,8},{5,9},{6,10},{7,11},{8,12},{9,13},{1... | collective-permute-start | bytes 442376 | tf_op jit(solution)/shard_map/ppermute | solution.py:916
  402.4 4.4 collective-permute-done.53
  406.8 9.1 %collective-permute-done.51 = bf16[768,768]{1,0:T(8,128)(2,1)} collective-permute-done((bf16[768,768]{1,0:T(8,128)(2,1)S(1)}, bf16[768,768]{1,0:T(8,128)(2,1)}, u32[]{:S(2)}, u32[]{:S(2)}) %collective-permute-start.51) | collective-permute-done | bytes 1179680 | tf_op jit(solution)/shard_map/ppermute | solution.py:913
  (421 shorter events, 193.2 us)
Async XLA Ops:
  7.2 54.3 %all-gather.3.cloned.1.call-start = ((), (), s32[]{:S(2)}) async-start(), calls=%async_computation.1 | async-start | bytes 7077888 | tf_op jit(solution)/shard_map/all_gather | solution.py:961
  15.2 46.3 %all-gather.5.cloned.1.call-start = ((), (), s32[]{:S(2)}) async-start(), calls=%async_computation.2 | async-start | bytes 7077888 | tf_op jit(solution)/shard_map/all_gather | solution.py:961
  18.0 42.7 %collective-permute-start.5 = (bf16[2,384,768]{2,1,0:T(8,128)(2,1)S(1)}, bf16[2,384,768]{2,1,0:T(8,128)(2,1)}, u32[]{:S(2)}, u32[]{:S(2)}) collective-permute-start(bf16[2,384,768]{2,1,0:T(8,128)(2,1)S(1)} %pad_maximum_fusion.1.refs_3_), channel_id=1, source_target_pairs={{0,1},{1,0},{2,3},{3,2},{4,5},{5,4},{6,7},{7,6},{8,9},{9,8},{10,11... | collective-permute-start | bytes 3538952 | tf_op jit(solution)/shard_map/ppermute | solution.py:913
  20.6 40.1 %collective-permute-start.6 = (bf16[2,384,768]{2,1,0:T(8,128)(2,1)S(1)}, bf16[2,384,768]{2,1,0:T(8,128)(2,1)}, u32[]{:S(2)}, u32[]{:S(2)}) collective-permute-start(bf16[2,384,768]{2,1,0:T(8,128)(2,1)S(1)} %pad_maximum_fusion.1.refs_3_), channel_id=1, source_target_pairs={{0,2},{1,3},{2,0},{3,1},{4,6},{5,7},{6,4},{7,5},{8,10},{9,11},{10,... | collective-permute-start | bytes 3538952 | tf_op jit(solution)/shard_map/ppermute | solution.py:913
  22.1 38.6 %collective-permute-start.7 = (bf16[2,384,768]{2,1,0:T(8,128)(2,1)S(1)}, bf16[2,384,768]{2,1,0:T(8,128)(2,1)}, u32[]{:S(2)}, u32[]{:S(2)}) collective-permute-start(bf16[2,384,768]{2,1,0:T(8,128)(2,1)S(1)} %pad_maximum_fusion.1.refs_3_), channel_id=1, source_target_pairs={{0,16},{16,0},{1,17},{17,1},{2,18},{18,2},{3,19},{19,3},{4,20},{20... | collective-permute-start | bytes 3538952 | tf_op jit(solution)/shard_map/ppermute | solution.py:910
  25.3 30.4 %collective-permute-start.8 = (bf16[304,768]{1,0:T(8,128)(2,1)}, bf16[304,768]{1,0:T(8,128)(2,1)}, u32[]{:S(2)}, u32[]{:S(2)}) collective-permute-start(bf16[304,768]{1,0:T(8,128)(2,1)} %get-tuple-element.230), channel_id=1, source_target_pairs={{0,4},{1,5},{2,6},{3,7},{4,8},{5,9},{6,10},{7,11},{8,12},{9,13},{1... | collective-permute-start | bytes 1400840 | tf_op jit(solution)/shard_map/ppermute | solution.py:916
  26.9 33.8 %collective-permute-start.9 = (bf16[304,768]{1,0:T(8,128)(2,1)}, bf16[304,768]{1,0:T(8,128)(2,1)}, u32[]{:S(2)}, u32[]{:S(2)}) collective-permute-start(bf16[304,768]{1,0:T(8,128)(2,1)} %get-tuple-element.231), channel_id=1, source_target_pairs={{0,8},{1,9},{2,10},{3,11},{4,12},{5,13},{6,14},{7,15},{8,0},{9,1},... | collective-permute-start | bytes 1400840 | tf_op jit(solution)/shard_map/ppermute | solution.py:916
  29.5 400.1 %reduce-scatter.4.cloned.1.call-start = ((), (), s32[]{:S(2)}) async-start(), calls=%async_computation.3 | async-start | bytes 5898240
  55.7 31.7 %collective-permute-start.12 = (bf16[304,768]{1,0:T(8,128)(2,1)}, bf16[304,768]{1,0:T(8,128)(2,1)S(1)}, u32[]{:S(2)}, u32[]{:S(2)}) collective-permute-start(bf16[304,768]{1,0:T(8,128)(2,1)} %get-tuple-element.245), channel_id=1, source_target_pairs={{0,12},{1,13},{2,14},{3,15},{4,0},{5,1},{6,2},{7,3},{8,4},{9,5},{1... | collective-permute-start | bytes 1400840 | tf_op jit(solution)/shard_map/ppermute | solution.py:916
  60.7 27.5 %collective-permute-start.10 = (bf16[2,384,768]{2,1,0:T(8,128)(2,1)}, bf16[2,384,768]{2,1,0:T(8,128)(2,1)}, u32[]{:S(2)}, u32[]{:S(2)}) collective-permute-start(bf16[2,384,768]{2,1,0:T(8,128)(2,1)} %collective-permute-done.5.refs_4_), channel_id=1, source_target_pairs={{0,16},{16,0},{1,17},{17,1},{2,18},{18,2},{3,19},{19,3},{4,20},{20... | collective-permute-start | bytes 3538952 | tf_op jit(solution)/shard_map/ppermute | solution.py:910
  60.8 28.7 %collective-permute-start.13 = (bf16[2,384,768]{2,1,0:T(8,128)(2,1)}, bf16[2,384,768]{2,1,0:T(8,128)(2,1)}, u32[]{:S(2)}, u32[]{:S(2)}) collective-permute-start(bf16[2,384,768]{2,1,0:T(8,128)(2,1)} %collective-permute-done.5.refs_4_), channel_id=1, source_target_pairs={{0,2},{1,3},{2,0},{3,1},{4,6},{5,7},{6,4},{7,5},{8,10},{9,11},{10,... | collective-permute-start | bytes 3538952 | tf_op jit(solution)/shard_map/ppermute | solution.py:913
  61.4 26.8 %collective-permute-start.11 = (bf16[2,384,768]{2,1,0:T(8,128)(2,1)}, bf16[2,384,768]{2,1,0:T(8,128)(2,1)}, u32[]{:S(2)}, u32[]{:S(2)}) collective-permute-start(bf16[2,384,768]{2,1,0:T(8,128)(2,1)} %collective-permute-done.6.refs_5_), channel_id=1, source_target_pairs={{0,16},{16,0},{1,17},{17,1},{2,18},{18,2},{3,19},{19,3},{4,20},{20... | collective-permute-start | bytes 3538952 | tf_op jit(solution)/shard_map/ppermute | solution.py:910
  89.6 26.1 %collective-permute-start.15 = (bf16[320,768]{1,0:T(8,128)(2,1)}, bf16[320,768]{1,0:T(8,128)(2,1)S(1)}, u32[]{:S(2)}, u32[]{:S(2)}) collective-permute-start(bf16[320,768]{1,0:T(8,128)(2,1)} %get-tuple-element.254), channel_id=1, source_target_pairs={{0,12},{1,13},{2,14},{3,15},{4,0},{5,1},{6,2},{7,3},{8,4},{9,5},{1... | collective-permute-start | bytes 1474568 | tf_op jit(solution)/shard_map/ppermute | solution.py:916
  91.1 37.9 %collective-permute-start.17 = (bf16[320,768]{1,0:T(8,128)(2,1)}, bf16[320,768]{1,0:T(8,128)(2,1)}, u32[]{:S(2)}, u32[]{:S(2)}) collective-permute-start(bf16[320,768]{1,0:T(8,128)(2,1)} %get-tuple-element.261), channel_id=1, source_target_pairs={{0,4},{1,5},{2,6},{3,7},{4,8},{5,9},{6,10},{7,11},{8,12},{9,13},{1... | collective-permute-start | bytes 1474568 | tf_op jit(solution)/shard_map/ppermute | solution.py:916
  91.7 54.3 %collective-permute-start.16 = (bf16[320,768]{1,0:T(8,128)(2,1)}, bf16[320,768]{1,0:T(8,128)(2,1)}, u32[]{:S(2)}, u32[]{:S(2)}) collective-permute-start(bf16[320,768]{1,0:T(8,128)(2,1)} %get-tuple-element.260), channel_id=1, source_target_pairs={{0,8},{1,9},{2,10},{3,11},{4,12},{5,13},{6,14},{7,15},{8,0},{9,1},... | collective-permute-start | bytes 1474568 | tf_op jit(solution)/shard_map/ppermute | solution.py:916
  222.8 42.6 %collective-permute-start.26 = (bf16[304,768]{1,0:T(8,128)(2,1)}, bf16[304,768]{1,0:T(8,128)(2,1)}, u32[]{:S(2)}, u32[]{:S(2)}) collective-permute-start(bf16[304,768]{1,0:T(8,128)(2,1)} %get-tuple-element.335), channel_id=1, source_target_pairs={{0,8},{1,9},{2,10},{3,11},{4,12},{5,13},{6,14},{7,15},{8,0},{9,1},... | collective-permute-start | bytes 1400840 | tf_op jit(solution)/shard_map/ppermute | solution.py:916
  222.8 42.6 %collective-permute-start.27 = (bf16[304,768]{1,0:T(8,128)(2,1)}, bf16[304,768]{1,0:T(8,128)(2,1)}, u32[]{:S(2)}, u32[]{:S(2)}) collective-permute-start(bf16[304,768]{1,0:T(8,128)(2,1)} %get-tuple-element.336), channel_id=1, source_target_pairs={{0,4},{1,5},{2,6},{3,7},{4,8},{5,9},{6,10},{7,11},{8,12},{9,13},{1... | collective-permute-start | bytes 1400840 | tf_op jit(solution)/shard_map/ppermute | solution.py:916
  235.2 44.1 %collective-permute-start.32 = (bf16[8,384,768]{2,1,0:T(8,128)(2,1)}, bf16[8,384,768]{2,1,0:T(8,128)(2,1)}, u32[]{:S(2)}, u32[]{:S(2)}) collective-permute-start(bf16[8,384,768]{2,1,0:T(8,128)(2,1)} %get-tuple-element.349), channel_id=1, source_target_pairs={{0,16},{16,0},{1,17},{17,1},{2,18},{18,2},{3,19},{19,3},{4,20},{20... | collective-permute-start | bytes 14155784 | tf_op jit(solution)/shard_map/ppermute | solution.py:910
  238.6 28.4 %collective-permute-start.24 = (bf16[768,768]{1,0:T(8,128)(2,1)S(1)}, bf16[768,768]{1,0:T(8,128)(2,1)S(1)}, u32[]{:S(2)}, u32[]{:S(2)}) collective-permute-start(bf16[768,768]{1,0:T(8,128)(2,1)S(1)} %get-tuple-element.435), channel_id=1, source_target_pairs={{0,2},{1,3},{2,0},{3,1},{4,6},{5,7},{6,4},{7,5},{8,10},{9,11},{10,... | collective-permute-start | bytes 3538952 | tf_op jit(solution)/shard_map/ppermute | solution.py:913
  238.9 28.4 %collective-permute-start.23 = (bf16[768,768]{1,0:T(8,128)(2,1)S(1)}, bf16[768,768]{1,0:T(8,128)(2,1)S(1)}, u32[]{:S(2)}, u32[]{:S(2)}) collective-permute-start(bf16[768,768]{1,0:T(8,128)(2,1)S(1)} %get-tuple-element.437), channel_id=1, source_target_pairs={{0,1},{1,0},{2,3},{3,2},{4,5},{5,4},{6,7},{7,6},{8,9},{9,8},{10,11... | collective-permute-start | bytes 3538952 | tf_op jit(solution)/shard_map/ppermute | solution.py:913
  299.0 27.0 %collective-permute-start.37 = (bf16[384,768]{1,0:T(8,128)(2,1)S(1)}, bf16[384,768]{1,0:T(8,128)(2,1)S(1)}, u32[]{:S(2)}, u32[]{:S(2)}) collective-permute-start(bf16[384,768]{1,0:T(8,128)(2,1)S(1)} %get-tuple-element.447), channel_id=1, source_target_pairs={{0,2},{1,3},{2,0},{3,1},{4,6},{5,7},{6,4},{7,5},{8,10},{9,11},{10,... | collective-permute-start | bytes 1769480 | tf_op jit(solution)/shard_map/ppermute | solution.py:913
  301.6 27.5 %collective-permute-start.36 = (bf16[384,768]{1,0:T(8,128)(2,1)S(1)}, bf16[384,768]{1,0:T(8,128)(2,1)S(1)}, u32[]{:S(2)}, u32[]{:S(2)}) collective-permute-start(bf16[384,768]{1,0:T(8,128)(2,1)S(1)} %get-tuple-element.449), channel_id=1, source_target_pairs={{0,1},{1,0},{2,3},{3,2},{4,5},{5,4},{6,7},{7,6},{8,9},{9,8},{10,11... | collective-permute-start | bytes 1769480 | tf_op jit(solution)/shard_map/ppermute | solution.py:913
  388.4 27.5 %collective-permute-start.51 = (bf16[768,768]{1,0:T(8,128)(2,1)S(1)}, bf16[768,768]{1,0:T(8,128)(2,1)}, u32[]{:S(2)}, u32[]{:S(2)}) collective-permute-start(bf16[768,768]{1,0:T(8,128)(2,1)S(1)} %maximum_select_fusion.2), channel_id=1, source_target_pairs={{0,2},{1,3},{2,0},{3,1},{4,6},{5,7},{6,4},{7,5},{8,10},{9,11},{10,... | collective-permute-start | bytes 3538952 | tf_op jit(solution)/shard_map/ppermute | solution.py:913
  391.7 27.2 %collective-permute-start.50 = (bf16[768,768]{1,0:T(8,128)(2,1)S(1)}, bf16[768,768]{1,0:T(8,128)(2,1)}, u32[]{:S(2)}, u32[]{:S(2)}) collective-permute-start(bf16[768,768]{1,0:T(8,128)(2,1)S(1)} %maximum_select_fusion.1), channel_id=1, source_target_pairs={{0,1},{1,0},{2,3},{3,2},{4,5},{5,4},{6,7},{7,6},{8,9},{9,8},{10,11... | collective-permute-start | bytes 3538952 | tf_op jit(solution)/shard_map/ppermute | solution.py:913
  (140 other events, 1225.5 us)
Sparse Core Ops, SparseCore 0:
  15.4 17.0 all-gather.2
  34.0 15.6 all-gather.4
  294.6 79.6 reduce-scatter.3

commit v4 on v3

--- a/solution.py
+++ b/solution.py
@@ -1108,7 +1108,8 @@
     a, b = unfold(a, a_got, 2), unfold(b, b_got, 1)
     a_got, b_got = over_q(a, 1), over_q(b, 2)
     tab = plane_move(plane_sum(tab))
-    a_got, b_got, tab = tie((a_got, b_got, tab))
+    grad_in, block_out = join(*grad_in, 0), join(*swapped(block_out), 0)
+    a_got, b_got, tab, grad_in, block_out = tie((a_got, b_got, tab, grad_in, block_out))
 
     side_x, side_y = jnp.reshape(q % 2, (1,)), jnp.reshape(q // 2, (1,))
 
@@ -1117,14 +1118,13 @@
 
     ta, tb = plane_join(tab)
     ta_got, tb_got = over_q(ta, 2), over_q(tb, 1)
-    block_out = swapped(block_out)
     tiny = tiny + tiny_y
     if few:
         tiny = [over_e(tiny, r) if r else tiny for r in range(experts)]
     else:
         tiny = [lax.psum(tiny, "dp", axis_index_groups=planes)]
-    ta_got, tb_got, tiny, a, a_got, b, b_got, grad_in, block_out, half_experts = tie(
-        (ta_got, tb_got, tiny, a, a_got, b, b_got, grad_in, block_out, half_experts)
+    ta_got, tb_got, tiny, a, a_got, b, b_got, half_experts = tie(
+        (ta_got, tb_got, tiny, a, a_got, b, b_got, half_experts)
     )
     half_up, half_down = half_experts[0].astype(F32), half_experts[1].astype(F32)
     ta, tb = unfold(ta, ta_got, 2), unfold(tb, tb_got, 1)
@@ -1139,8 +1139,8 @@
     )
     sum_qkv = jnp.concatenate([q_and_k, v_sum], axis=1)
     return (
-        join(*block_out, 0),
-        join(*grad_in, 0),
+        block_out,
+        grad_in,
         total[0],
         total[1],
         sum_qkv,

time: 467 us -> 471 us (level)
    unnamed x194 -> x202, local copies, waits for them, and re-layouts: 33.4 us -> 34 us
where the time goes in v4:
time: 471 us; the launch traced here: 464 us
  Pallas kernels  190 us (40%)
  waiting for transfers between devices  92.2 us (20%)
  starting transfers between devices  79.5 us (17%)
  local copies, waits for them, and re-layouts  47.9 us (10%)
  other arithmetic  38.6 us (8%)
  between operations  15.5 us (3%)
    pallas_call x15, Pallas kernels, call(): return lambda *operands: made(*operands, *after)  144 us
    ppermute x27, waiting for transfers between devices, over_e(): lax.ppermute(v, 'dp', [(i, (i // GROUP + r) % experts * GROUP + i % GROUP...  64.9 us
    ppermute x27, starting transfers between devices, over_e(): lax.ppermute(v, 'dp', [(i, (i // GROUP + r) % experts * GROUP + i % GROUP...  51.2 us
    pallas_call x4, Pallas kernels, weight_grad(): pl.pallas_call(functools.partial(grad_kernel, n, len(into)), grid_spec=pl...  38.2 us
    unnamed x202, local copies, waits for them, and re-layouts  34 us
    ppermute x21, waiting for transfers between devices, over_q(): return lax.ppermute(v, 'dp', [(i, i ^ bit) for i in range(dp_count)])  26.3 us
    ppermute x21, starting transfers between devices, over_q(): return lax.ppermute(v, 'dp', [(i, i ^ bit) for i in range(dp_count)])  25.5 us
    convert_element_type x7, other arithmetic, add(): return (a.astype(F32) + b.astype(F32)).astype(BF)  11.6 us
  transfers between devices with their start and end apart: 67, of which 25 were waited for; matrix products, arithmetic and copies ran while one was open for 11% of the time, Pallas kernels for 34%

profile of v4, /device:TPU:0, one launch (start us, length us, event | category | flops | bytes accessed | tf_op | source)
XLA Modules:
  0.0 464.0 jit_solution(7665141785417292033)
XLA Ops:
  33.1 21.3 %attention_forward.1 = (bf16[576,768]{1,0:T(8,128)(2,1)}, bf16[576,2304]{1,0:T(8,128)(2,1)}, bf16[576,768]{1,0:T(8,128)(2,1)}, f32[16,576]{1,0:T(8,128)S(1)}, f32[576,768]{1,0:T(8,128)S(1)}) custom-call(s32[2]{0:T(128)S(1)} %pad_add_fusion.refs_0_.s_ref, bf16[576,768]{1,0:T(8,128)(2,1)S(1)} %maximum_select_fusion.3.refs_1_, ...), custom_call_target="tpu_custom_call" | custom-call | flops 59793997824 | bytes 188743680 | tf_op jit(solution)/shard_map/attention_forward/pallas_call | solution.py:135
  67.7 18.9 %dense_forward.1 = (bf16[576,768]{1,0:T(8,128)(2,1)}, bf16[576,3072]{1,0:T(8,128)(2,1)}, bf16[576,3072]{1,0:T(8,128)(2,1)}, f32[576,768]{1,0:T(8,128)}, bf16[576...) custom-call(f32[576,768]{1,0:T(8,128)S(1)} %copy-done.39, ...), custom_call_target="tpu_custom_call" | custom-call | flops 104186511360 | bytes 349175808 | tf_op jit(solution)/shard_map/dense_forward/pallas_call | solution.py:135
  94.7 11.2 %expert.4 = (bf16[320,768]{1,0:T(8,128)(2,1)}, bf16[304,768]{1,0:T(8,128)(2,1)}, bf16[304,3072]{1,0:T(8,128)(2,1)S(1)}, bf16[304,3072]{1,0:T(8,128)(2,1)S(1)}, bf16[304,768]{1,0:T(8,128)(2,1)S(1)}) custom-call(s32[2]{0:T(128)S(1)} %pad_add_fusion.refs_0_.s_ref, bf16[320,768]{1,0:T(8,128)(2,1)S(1)} %copy-done.60, bf16[304,768]{1,0:T(8,128)(2,1)S(1)} %copy-done.36, ...), custom_call_target="tpu_custom_call" | custom-call | flops 91804925952 | bytes 248119296 | tf_op jit(solution)/shard_map/expert/pallas_call | solution.py:135
  107.9 7.7 %collective-permute-done.15.refs_1_.refs_3_ = bf16[320,768]{1,0:T(8,128)(2,1)S(1)} collective-permute-done((bf16[320,768]{1,0:T(8,128)(2,1)}, bf16[320,768]{1,0:T(8,128)(2,1)S(1)}, u32[]{:S(2)}, u32[]{:S(2)}) %collective-permute-start.15) | collective-permute-done | bytes 491552 | tf_op jit(solution)/shard_map/ppermute | solution.py:916
  115.6 11.3 %expert.5 = (bf16[320,768]{1,0:T(8,128)(2,1)}, bf16[304,768]{1,0:T(8,128)(2,1)}, bf16[304,3072]{1,0:T(8,128)(2,1)S(1)}, bf16[304,3072]{1,0:T(8,128)(2,1)S(1)}, bf16[304,768]{1,0:T(8,128)(2,1)S(1)}) custom-call(s32[2]{0:T(128)S(1)} %pad_add_fusion.refs_0_.s_ref, bf16[320,768]{1,0:T(8,128)(2,1)S(1)} %collective-permute-done.15.refs_1_.refs_3_, ...), custom_call_target="tpu_custom_call" | custom-call | flops 91804925952 | bytes 248119296 | tf_op jit(solution)/shard_map/expert/pallas_call | solution.py:135
  129.0 12.0 %expert.6 = (bf16[320,768]{1,0:T(8,128)(2,1)}, bf16[304,768]{1,0:T(8,128)(2,1)}, bf16[304,3072]{1,0:T(8,128)(2,1)S(1)}, bf16[304,3072]{1,0:T(8,128)(2,1)S(1)}, bf16[304,768]{1,0:T(8,128)(2,1)S(1)}) custom-call(s32[2]{0:T(128)S(1)} %pad_add_fusion.refs_0_.s_ref, bf16[320,768]{1,0:T(8,128)(2,1)} %collective-permute-done.17.refs_1_, ...), custom_call_target="tpu_custom_call" | custom-call | flops 91804925952 | bytes 248119296 | tf_op jit(solution)/shard_map/expert/pallas_call | solution.py:135
  146.0 12.5 %expert.7 = (bf16[320,768]{1,0:T(8,128)(2,1)}, bf16[304,768]{1,0:T(8,128)(2,1)}, bf16[304,3072]{1,0:T(8,128)(2,1)S(1)}, bf16[304,3072]{1,0:T(8,128)(2,1)S(1)}, bf16[304,768]{1,0:T(8,128)(2,1)S(1)}) custom-call(s32[2]{0:T(128)S(1)} %pad_add_fusion.refs_0_.s_ref, bf16[320,768]{1,0:T(8,128)(2,1)} %collective-permute-done.16.refs_1_.refs_2_, ...), custom_call_target="tpu_custom_call" | custom-call | flops 91804925952 | bytes 248119296 | tf_op jit(solution)/shard_map/expert/pallas_call | solution.py:135
  159.8 12.3 %weight_grad.6 = (bf16[8,384,768]{2,1,0:T(8,128)(2,1)}, bf16[8,384,768]{2,1,0:T(8,128)(2,1)S(1)}) custom-call(s32[2]{0:T(128)S(1)} %pad_add_fusion.1.s_ref, bf16[320,768]{1,0:T(8,128)(2,1)S(1)} %copy-done.61, bf16[320,768]{1,0:T(8,128)(2,1)} %collective-permute-done.17.refs_1_, bf16[320,768]{1,0:T(8,128)(2,1)} %collective-permute-done.16.refs_1_.refs_2_, ...), custom_call_target="tpu_custom_call" | custom-call | flops 91804925952 | bytes 224919552 | tf_op jit(solution)/shard_map/weight_grad/pallas_call | solution.py:475
  172.1 9.8 %collective-permute-done.20.refs_15_ = bf16[320,768]{1,0:T(8,128)(2,1)S(1)} collective-permute-done((bf16[320,768]{1,0:T(8,128)(2,1)}, bf16[320,768]{1,0:T(8,128)(2,1)S(1)}, u32[]{:S(2)}, u32[]{:S(2)}) %collective-permute-start.20) | collective-permute-done | bytes 491552 | tf_op jit(solution)/shard_map/ppermute | solution.py:916
  183.5 18.4 %dense_backward.1 = (bf16[576,768]{1,0:T(8,128)(2,1)S(1)}, bf16[576,3072]{1,0:T(8,128)(2,1)S(1)}, f32[576,768]{1,0:T(8,128)S(1)}, f32[8,768]{1,0:T(8,128)S(1)}, f32[16,768]{1,0:T(8,128)S(1)}) custom-call(bf16[576,768]{1,0:T(8,128)(2,1)S(1)} %maximum_select_fusion.4.refs_0_, f32[576,768]{1,0:T(8,128)S(1)} %copy-done, f32[576,768]{1,0:T(8,128)S(1)} %copy-done.40, ...), custom_call_target="tpu_custom_call" | custom-call | flops 104186511360 | bytes 391643136 | tf_op jit(solution)/shard_map/dense_backward/pallas_call | solution.py:135
  201.9 7.0 %weight_grad.5 = (bf16[4,384,768]{2,1,0:T(8,128)(2,1)S(1)}, bf16[4,384,768]{2,1,0:T(8,128)(2,1)S(1)}) custom-call(s32[2]{0:T(128)S(1)} %pad_add_fusion.refs_0_.s_ref, bf16[576,3072]{1,0:T(8,128)(2,1)S(1)} %copy-done.29, bf16[576,768]{1,0:T(8,128)(2,1)S(1)} %get-tuple-element.293.refs_1_.refs_4_), custom_call_target="tpu_custom_call" | custom-call | flops 43486543872 | bytes 146276352 | tf_op jit(solution)/shard_map/weight_grad/pallas_call | solution.py:475
  211.0 7.2 %weight_grad.4 = (bf16[4,384,768]{2,1,0:T(8,128)(2,1)S(1)}, bf16[4,384,768]{2,1,0:T(8,128)(2,1)S(1)}) custom-call(s32[2]{0:T(128)S(1)} %pad_add_fusion.refs_0_.s_ref, bf16[576,768]{1,0:T(8,128)(2,1)S(1)} %copy-done.41, bf16[576,3072]{1,0:T(8,128)(2,1)S(1)} %copy-done.31), custom_call_target="tpu_custom_call" | custom-call | flops 43486543872 | bytes 146276352 | tf_op jit(solution)/shard_map/weight_grad/pallas_call | solution.py:475
  223.4 11.8 %weight_grad.7 = (bf16[8,384,768]{2,1,0:T(8,128)(2,1)}, bf16[8,384,768]{2,1,0:T(8,128)(2,1)S(1)}) custom-call(s32[2]{0:T(128)S(1)} %copy-done.28, bf16[304,768]{1,0:T(8,128)(2,1)S(1)} %copy-done.52, bf16[304,768]{1,0:T(8,128)(2,1)S(1)} %copy-done.56, bf16[304,768]{1,0:T(8,128)(2,1)S(1)} %copy-done.58, ...), custom_call_target="tpu_custom_call", output_to_operand_aliasing={{0}: (9, {}), {1}: (10, {})} | custom-call | flops 91804925952 | bytes 224919552 | tf_op jit(solution)/shard_map/weight_grad/pallas_call | solution.py:475
  240.5 17.3 %attention_backward.1 = (bf16[576,768]{1,0:T(8,128)(2,1)S(1)}, bf16[576,2304]{1,0:T(8,128)(2,1)S(1)}) custom-call(s32[2]{0:T(128)S(1)} %pad_add_fusion.refs_0_.s_ref, f32[576,768]{1,0:T(8,128)S(1)} %copy-done.33, s32[1,576]{1,0:T(1,128)S(1)} %get-tuple-element.428.refs_2_, s32[576,1]{1,0:T(8,128)S(1)} %copy.36.refs_3_, bf16[576,2304]{1,0:T(8,128)(2,1)S(1)} %copy-done.37, ...), custom_call_target="tpu_custom_call" | custom-call | flops 92408905728 | bytes 146276352 | tf_op jit(solution)/shard_map/attention_backward/pallas_call | solution.py:135
  257.9 7.3 %attention_grad.1 = (bf16[4,384,768]{2,1,0:T(8,128)(2,1)S(1)}, bf16[4,384,768]{2,1,0:T(8,128)(2,1)S(1)}) custom-call(s32[2]{0:T(128)S(1)} %pad_add_fusion.refs_0_.s_ref, bf16[576,768]{1,0:T(8,128)(2,1)S(1)} %copy-done.6, bf16[576,768]{1,0:T(8,128)(2,1)S(1)} %copy-done.7, bf16[576,2304]{1,0:T(8,128)(2,1)S(1)} %get-tuple-element.341.dpacked.refs_4_, ...), custom_call_target="tpu_custom_call" | custom-call | flops 339738624 | bytes 442368 | tf_op jit(solution)/shard_map/attention_grad/pallas_call | solution.py:523
  267.3 7.0 %input_backward.1 = (f32[576,768]{1,0:T(8,128)S(1)}, f32[8,768]{1,0:T(8,128)S(1)}) custom-call(s32[2]{0:T(128)S(1)} %pad_add_fusion.refs_0_.s_ref, bf16[576,768]{1,0:T(8,128)(2,1)S(1)} %copy-done.5, f32[576,768]{1,0:T(8,128)S(1)} %copy-done.33, f32[8,768]{1,0:T(8,128)S(1)} %fusion.19.refs_4_.refs_1_.refs_3_, ...), custom_call_target="tpu_custom_call" | custom-call | flops 32614907904 | bytes 169869312 | tf_op jit(solution)/shard_map/input_backward/pallas_call | solution.py:135
  279.3 5.8 %add_convert_fusion = bf16[8,384,768]{2,1,0:T(8,128)(2,1)} fusion(bf16[8,384,768]{2,1,0:T(8,128)(2,1)} %collective-permute-done.32, bf16[8,384,768]{2,1,0:T(8,128)(2,1)S(1)} %get-tuple-element.346), kind=kLoop, calls=%fused_computation | loop fusion | flops 9437184 | bytes 14155776 | tf_op jit(solution)/shard_map/convert_element_type | solution.py:933
  285.1 6.4 %collective-permute-done.30 = bf16[384,768]{1,0:T(8,128)(2,1)} collective-permute-done((bf16[384,768]{1,0:T(8,128)(2,1)S(1)}, bf16[384,768]{1,0:T(8,128)(2,1)}, u32[]{:S(2)}, u32[]{:S(2)}) %collective-permute-start.30) | collective-permute-done | bytes 589856 | tf_op jit(solution)/shard_map/ppermute | solution.py:913
  308.7 6.8 %collective-permute-done.33 = bf16[2,96,768]{2,1,0:T(8,128)(2,1)} collective-permute-done((bf16[2,96,768]{2,1,0:T(8,128)(2,1)}, bf16[2,96,768]{2,1,0:T(8,128)(2,1)}, u32[]{:S(2)}, u32[]{:S(2)}) %collective-permute-start.33) | collective-permute-done | bytes 294944 | tf_op jit(solution)/shard_map/ppermute | solution.py:916
  316.0 9.9 %collective-permute-done.34 = bf16[2,96,768]{2,1,0:T(8,128)(2,1)} collective-permute-done((bf16[2,96,768]{2,1,0:T(8,128)(2,1)}, bf16[2,96,768]{2,1,0:T(8,128)(2,1)}, u32[]{:S(2)}, u32[]{:S(2)}) %collective-permute-start.34) | collective-permute-done | bytes 294944 | tf_op jit(solution)/shard_map/ppermute | solution.py:916
  348.9 9.3 %collective-permute-done.39 = bf16[2,96,768]{2,1,0:T(8,128)(2,1)} collective-permute-done((bf16[2,96,768]{2,1,0:T(8,128)(2,1)}, bf16[2,96,768]{2,1,0:T(8,128)(2,1)}, u32[]{:S(2)}, u32[]{:S(2)}) %collective-permute-start.39) | collective-permute-done | bytes 294944 | tf_op jit(solution)/shard_map/ppermute | solution.py:916
  367.6 6.8 %collective-permute-start.46 = (bf16[2,48,768]{2,1,0:T(8,128)(2,1)S(1)}, bf16[2,48,768]{2,1,0:T(8,128)(2,1)S(1)}, u32[]{:S(2)}, u32[]{:S(2)}) collective-permute-start(bf16[2,48,768]{2,1,0:T(8,128)(2,1)S(1)} %get-tuple-element.466), channel_id=1, source_target_pairs={{0,4},{1,5},{2,6},{3,7},{4,8},{5,9},{6,10},{7,11},{8,12},{9,13},{1... | collective-permute-start | bytes 442376 | tf_op jit(solution)/shard_map/ppermute | solution.py:916
  376.2 6.3 %collective-permute-done.49 = f32[10,384]{1,0:T(8,128)S(1)} collective-permute-done((f32[10,384]{1,0:T(8,128)S(1)}, f32[10,384]{1,0:T(8,128)S(1)}, u32[]{:S(2)}, u32[]{:S(2)}) %collective-permute-start.49) | collective-permute-done | bytes 15392 | tf_op jit(solution)/shard_map/ppermute | solution.py:913
  388.1 5.7 %collective-permute-done.47 = bf16[2,48,768]{2,1,0:T(8,128)(2,1)S(1)} collective-permute-done((bf16[2,48,768]{2,1,0:T(8,128)(2,1)S(1)}, bf16[2,48,768]{2,1,0:T(8,128)(2,1)S(1)}, u32[]{:S(2)}, u32[]{:S(2)}) %collective-permute-start.47) | collective-permute-done | bytes 147488 | tf_op jit(solution)/shard_map/ppermute | solution.py:916
  (429 shorter events, 198.6 us)
Async XLA Ops:
  7.2 54.3 %all-gather.3.cloned.1.call-start = ((), (), s32[]{:S(2)}) async-start(), calls=%async_computation.1 | async-start | bytes 7077888 | tf_op jit(solution)/shard_map/all_gather | solution.py:961
  15.2 46.3 %all-gather.5.cloned.1.call-start = ((), (), s32[]{:S(2)}) async-start(), calls=%async_computation.2 | async-start | bytes 7077888 | tf_op jit(solution)/shard_map/all_gather | solution.py:961
  18.0 42.7 %collective-permute-start.5 = (bf16[2,384,768]{2,1,0:T(8,128)(2,1)S(1)}, bf16[2,384,768]{2,1,0:T(8,128)(2,1)}, u32[]{:S(2)}, u32[]{:S(2)}) collective-permute-start(bf16[2,384,768]{2,1,0:T(8,128)(2,1)S(1)} %pad_maximum_fusion.1.refs_3_), channel_id=1, source_target_pairs={{0,1},{1,0},{2,3},{3,2},{4,5},{5,4},{6,7},{7,6},{8,9},{9,8},{10,11... | collective-permute-start | bytes 3538952 | tf_op jit(solution)/shard_map/ppermute | solution.py:913
  20.6 40.1 %collective-permute-start.6 = (bf16[2,384,768]{2,1,0:T(8,128)(2,1)S(1)}, bf16[2,384,768]{2,1,0:T(8,128)(2,1)}, u32[]{:S(2)}, u32[]{:S(2)}) collective-permute-start(bf16[2,384,768]{2,1,0:T(8,128)(2,1)S(1)} %pad_maximum_fusion.1.refs_3_), channel_id=1, source_target_pairs={{0,2},{1,3},{2,0},{3,1},{4,6},{5,7},{6,4},{7,5},{8,10},{9,11},{10,... | collective-permute-start | bytes 3538952 | tf_op jit(solution)/shard_map/ppermute | solution.py:913
  22.1 38.6 %collective-permute-start.7 = (bf16[2,384,768]{2,1,0:T(8,128)(2,1)S(1)}, bf16[2,384,768]{2,1,0:T(8,128)(2,1)}, u32[]{:S(2)}, u32[]{:S(2)}) collective-permute-start(bf16[2,384,768]{2,1,0:T(8,128)(2,1)S(1)} %pad_maximum_fusion.1.refs_3_), channel_id=1, source_target_pairs={{0,16},{16,0},{1,17},{17,1},{2,18},{18,2},{3,19},{19,3},{4,20},{20... | collective-permute-start | bytes 3538952 | tf_op jit(solution)/shard_map/ppermute | solution.py:910
  25.3 30.4 %collective-permute-start.8 = (bf16[304,768]{1,0:T(8,128)(2,1)}, bf16[304,768]{1,0:T(8,128)(2,1)}, u32[]{:S(2)}, u32[]{:S(2)}) collective-permute-start(bf16[304,768]{1,0:T(8,128)(2,1)} %get-tuple-element.228), channel_id=1, source_target_pairs={{0,4},{1,5},{2,6},{3,7},{4,8},{5,9},{6,10},{7,11},{8,12},{9,13},{1... | collective-permute-start | bytes 1400840 | tf_op jit(solution)/shard_map/ppermute | solution.py:916
  26.9 33.8 %collective-permute-start.9 = (bf16[304,768]{1,0:T(8,128)(2,1)}, bf16[304,768]{1,0:T(8,128)(2,1)}, u32[]{:S(2)}, u32[]{:S(2)}) collective-permute-start(bf16[304,768]{1,0:T(8,128)(2,1)} %get-tuple-element.229), channel_id=1, source_target_pairs={{0,8},{1,9},{2,10},{3,11},{4,12},{5,13},{6,14},{7,15},{8,0},{9,1},... | collective-permute-start | bytes 1400840 | tf_op jit(solution)/shard_map/ppermute | solution.py:916
  29.5 408.7 %reduce-scatter.4.cloned.1.call-start = ((), (), s32[]{:S(2)}) async-start(), calls=%async_computation.3 | async-start | bytes 5898240
  55.7 31.7 %collective-permute-start.12 = (bf16[304,768]{1,0:T(8,128)(2,1)}, bf16[304,768]{1,0:T(8,128)(2,1)S(1)}, u32[]{:S(2)}, u32[]{:S(2)}) collective-permute-start(bf16[304,768]{1,0:T(8,128)(2,1)} %get-tuple-element.243), channel_id=1, source_target_pairs={{0,12},{1,13},{2,14},{3,15},{4,0},{5,1},{6,2},{7,3},{8,4},{9,5},{1... | collective-permute-start | bytes 1400840 | tf_op jit(solution)/shard_map/ppermute | solution.py:916
  60.7 27.5 %collective-permute-start.10 = (bf16[2,384,768]{2,1,0:T(8,128)(2,1)}, bf16[2,384,768]{2,1,0:T(8,128)(2,1)}, u32[]{:S(2)}, u32[]{:S(2)}) collective-permute-start(bf16[2,384,768]{2,1,0:T(8,128)(2,1)} %collective-permute-done.5.refs_4_), channel_id=1, source_target_pairs={{0,16},{16,0},{1,17},{17,1},{2,18},{18,2},{3,19},{19,3},{4,20},{20... | collective-permute-start | bytes 3538952 | tf_op jit(solution)/shard_map/ppermute | solution.py:910
  60.8 28.7 %collective-permute-start.13 = (bf16[2,384,768]{2,1,0:T(8,128)(2,1)}, bf16[2,384,768]{2,1,0:T(8,128)(2,1)}, u32[]{:S(2)}, u32[]{:S(2)}) collective-permute-start(bf16[2,384,768]{2,1,0:T(8,128)(2,1)} %collective-permute-done.5.refs_4_), channel_id=1, source_target_pairs={{0,2},{1,3},{2,0},{3,1},{4,6},{5,7},{6,4},{7,5},{8,10},{9,11},{10,... | collective-permute-start | bytes 3538952 | tf_op jit(solution)/shard_map/ppermute | solution.py:913
  61.3 26.8 %collective-permute-start.11 = (bf16[2,384,768]{2,1,0:T(8,128)(2,1)}, bf16[2,384,768]{2,1,0:T(8,128)(2,1)}, u32[]{:S(2)}, u32[]{:S(2)}) collective-permute-start(bf16[2,384,768]{2,1,0:T(8,128)(2,1)} %collective-permute-done.6.refs_5_), channel_id=1, source_target_pairs={{0,16},{16,0},{1,17},{17,1},{2,18},{18,2},{3,19},{19,3},{4,20},{20... | collective-permute-start | bytes 3538952 | tf_op jit(solution)/shard_map/ppermute | solution.py:910
  89.5 26.1 %collective-permute-start.15 = (bf16[320,768]{1,0:T(8,128)(2,1)}, bf16[320,768]{1,0:T(8,128)(2,1)S(1)}, u32[]{:S(2)}, u32[]{:S(2)}) collective-permute-start(bf16[320,768]{1,0:T(8,128)(2,1)} %get-tuple-element.252), channel_id=1, source_target_pairs={{0,12},{1,13},{2,14},{3,15},{4,0},{5,1},{6,2},{7,3},{8,4},{9,5},{1... | collective-permute-start | bytes 1474568 | tf_op jit(solution)/shard_map/ppermute | solution.py:916
  91.1 37.9 %collective-permute-start.17 = (bf16[320,768]{1,0:T(8,128)(2,1)}, bf16[320,768]{1,0:T(8,128)(2,1)}, u32[]{:S(2)}, u32[]{:S(2)}) collective-permute-start(bf16[320,768]{1,0:T(8,128)(2,1)} %get-tuple-element.259), channel_id=1, source_target_pairs={{0,4},{1,5},{2,6},{3,7},{4,8},{5,9},{6,10},{7,11},{8,12},{9,13},{1... | collective-permute-start | bytes 1474568 | tf_op jit(solution)/shard_map/ppermute | solution.py:916
  91.7 54.3 %collective-permute-start.16 = (bf16[320,768]{1,0:T(8,128)(2,1)}, bf16[320,768]{1,0:T(8,128)(2,1)}, u32[]{:S(2)}, u32[]{:S(2)}) collective-permute-start(bf16[320,768]{1,0:T(8,128)(2,1)} %get-tuple-element.258), channel_id=1, source_target_pairs={{0,8},{1,9},{2,10},{3,11},{4,12},{5,13},{6,14},{7,15},{8,0},{9,1},... | collective-permute-start | bytes 1474568 | tf_op jit(solution)/shard_map/ppermute | solution.py:916
  222.7 42.5 %collective-permute-start.26 = (bf16[304,768]{1,0:T(8,128)(2,1)}, bf16[304,768]{1,0:T(8,128)(2,1)}, u32[]{:S(2)}, u32[]{:S(2)}) collective-permute-start(bf16[304,768]{1,0:T(8,128)(2,1)} %get-tuple-element.333), channel_id=1, source_target_pairs={{0,8},{1,9},{2,10},{3,11},{4,12},{5,13},{6,14},{7,15},{8,0},{9,1},... | collective-permute-start | bytes 1400840 | tf_op jit(solution)/shard_map/ppermute | solution.py:916
  222.7 42.5 %collective-permute-start.27 = (bf16[304,768]{1,0:T(8,128)(2,1)}, bf16[304,768]{1,0:T(8,128)(2,1)}, u32[]{:S(2)}, u32[]{:S(2)}) collective-permute-start(bf16[304,768]{1,0:T(8,128)(2,1)} %get-tuple-element.334), channel_id=1, source_target_pairs={{0,4},{1,5},{2,6},{3,7},{4,8},{5,9},{6,10},{7,11},{8,12},{9,13},{1... | collective-permute-start | bytes 1400840 | tf_op jit(solution)/shard_map/ppermute | solution.py:916
  235.2 44.1 %collective-permute-start.32 = (bf16[8,384,768]{2,1,0:T(8,128)(2,1)}, bf16[8,384,768]{2,1,0:T(8,128)(2,1)}, u32[]{:S(2)}, u32[]{:S(2)}) collective-permute-start(bf16[8,384,768]{2,1,0:T(8,128)(2,1)} %get-tuple-element.347), channel_id=1, source_target_pairs={{0,16},{16,0},{1,17},{17,1},{2,18},{18,2},{3,19},{19,3},{4,20},{20... | collective-permute-start | bytes 14155784 | tf_op jit(solution)/shard_map/ppermute | solution.py:910
  238.6 28.4 %collective-permute-start.24 = (bf16[768,768]{1,0:T(8,128)(2,1)S(1)}, bf16[768,768]{1,0:T(8,128)(2,1)S(1)}, u32[]{:S(2)}, u32[]{:S(2)}) collective-permute-start(bf16[768,768]{1,0:T(8,128)(2,1)S(1)} %get-tuple-element.431), channel_id=1, source_target_pairs={{0,2},{1,3},{2,0},{3,1},{4,6},{5,7},{6,4},{7,5},{8,10},{9,11},{10,... | collective-permute-start | bytes 3538952 | tf_op jit(solution)/shard_map/ppermute | solution.py:913
  238.9 28.4 %collective-permute-start.23 = (bf16[768,768]{1,0:T(8,128)(2,1)S(1)}, bf16[768,768]{1,0:T(8,128)(2,1)S(1)}, u32[]{:S(2)}, u32[]{:S(2)}) collective-permute-start(bf16[768,768]{1,0:T(8,128)(2,1)S(1)} %get-tuple-element.433), channel_id=1, source_target_pairs={{0,1},{1,0},{2,3},{3,2},{4,5},{5,4},{6,7},{7,6},{8,9},{9,8},{10,11... | collective-permute-start | bytes 3538952 | tf_op jit(solution)/shard_map/ppermute | solution.py:913
  298.9 27.0 %collective-permute-start.37 = (bf16[384,768]{1,0:T(8,128)(2,1)S(1)}, bf16[384,768]{1,0:T(8,128)(2,1)S(1)}, u32[]{:S(2)}, u32[]{:S(2)}) collective-permute-start(bf16[384,768]{1,0:T(8,128)(2,1)S(1)} %get-tuple-element.443), channel_id=1, source_target_pairs={{0,2},{1,3},{2,0},{3,1},{4,6},{5,7},{6,4},{7,5},{8,10},{9,11},{10,... | collective-permute-start | bytes 1769480 | tf_op jit(solution)/shard_map/ppermute | solution.py:913
  301.6 27.5 %collective-permute-start.36 = (bf16[384,768]{1,0:T(8,128)(2,1)S(1)}, bf16[384,768]{1,0:T(8,128)(2,1)S(1)}, u32[]{:S(2)}, u32[]{:S(2)}) collective-permute-start(bf16[384,768]{1,0:T(8,128)(2,1)S(1)} %get-tuple-element.445), channel_id=1, source_target_pairs={{0,1},{1,0},{2,3},{3,2},{4,5},{5,4},{6,7},{7,6},{8,9},{9,8},{10,11... | collective-permute-start | bytes 1769480 | tf_op jit(solution)/shard_map/ppermute | solution.py:913
  362.5 31.4 %collective-permute-start.44 = (bf16[384,768]{1,0:T(8,128)(2,1)S(1)}, bf16[384,768]{1,0:T(8,128)(2,1)}, u32[]{:S(2)}, u32[]{:S(2)}) collective-permute-start(bf16[384,768]{1,0:T(8,128)(2,1)S(1)} %get-tuple-element.442), channel_id=1, source_target_pairs={{0,2},{1,3},{2,0},{3,1},{4,6},{5,7},{6,4},{7,5},{8,10},{9,11},{10,... | collective-permute-start | bytes 1769480 | tf_op jit(solution)/shard_map/ppermute | solution.py:913
  364.3 29.5 %collective-permute-start.45 = (bf16[384,768]{1,0:T(8,128)(2,1)S(1)}, bf16[384,768]{1,0:T(8,128)(2,1)}, u32[]{:S(2)}, u32[]{:S(2)}) collective-permute-start(bf16[384,768]{1,0:T(8,128)(2,1)S(1)} %get-tuple-element.441), channel_id=1, source_target_pairs={{0,1},{1,0},{2,3},{3,2},{4,5},{5,4},{6,7},{7,6},{8,9},{9,8},{10,11... | collective-permute-start | bytes 1769480 | tf_op jit(solution)/shard_map/ppermute | solution.py:913
  (144 other events, 1299.6 us)
Sparse Core Ops, SparseCore 0:
  15.4 17.0 all-gather.2
  34.0 15.5 all-gather.4
  294.6 80.2 reduce-scatter.3
